TPU v7x, 32 devices: a whole 2x2x4 slice. The times are simulated.
32 devices in a mesh: groups: 2 (over x), leaf: 16 (over z, y, core).
Axes of the slice: x: 2, y: 2, z: 4, core: 2. Of those that a mesh axis runs over, the one named last changes fastest.
Arguments:
- points: float32 [3, 32768], P(None, ('groups', 'leaf')), parts along dimension 1, may hold values from 0 to 1
- leaf_order: int32 [32768], P(('groups', 'leaf')), parts along dimension 0, may hold values from 0 to 1023, as said below
- skeleton: int32 [32, 256], P(('groups', 'leaf')), parts along dimension 0, may hold values from 0 to 1023, as said below
- basis: bfloat16 [32768, 256], P(('groups', 'leaf')), parts along dimension 0, may hold values from -0.1875 to 0.1875
- transfer: bfloat16 [32, 3, 512, 256], P(('groups', 'leaf')), parts along dimension 0, as said below
- coupling: bfloat16 [32, 4, 256, 256], P(('groups', 'leaf')), parts along dimension 0, as said below
- solution: float32 [32768, 256], P(('groups', 'leaf')), parts along dimension 0, may hold values from -6 to 6
- residual: float32 [32768, 256], P(('groups', 'leaf')), parts along dimension 0, may hold values from -6 to 6
- direction: float32 [32768, 256], P(('groups', 'leaf')), parts along dimension 0, may hold values from -6 to 6
Outputs:
- solution_out: float32 [32768, 256], P(('groups', 'leaf')), parts along dimension 0
- residual_out: float32 [32768, 256], P(('groups', 'leaf')), parts along dimension 0
- direction_out: float32 [32768, 256], P(('groups', 'leaf')), parts along dimension 0
There are 2 independent parts, one for each index of `groups`. A program takes and returns all parts, laid end to end along the dimension named above; each array names one. Nothing has to cross between parts.
Inputs may be any that keep to these rules, and one draw needn't show every extreme that they name: `leaf_order`: each aligned block of 1024 entries is an ordering of 0 to 1023. `skeleton`: each row holds 256 different row numbers of its leaf. transfer[d, k] is equal for all leaves d under the same node at level k + 1. coupling[d, k] is equal for all leaves under the same node at level k, and the two sibling nodes hold transposes of each other.
All inputs are finite; a program needn't handle non-finite values.
Results may differ from a plain program's by a relative error of at most 0.0075.
Values may be sent and summed in bfloat16 or wider, within the bound.
No kernel may reach another device: no remote copies, remote signals or barrier semaphores. Data moves between devices by JAX's collectives and lax.ppermute only.
A program may use at most 64 MiB of HBM per device.

v0:
```python
import jax
import jax.numpy as jnp
from jax import lax
from jax.sharding import PartitionSpec as P

ITERS = 2


length_scale = 0.1
nugget = 2.0
smallest = 1e-12


def swapped(value, axis, distance):
    mask = 2**distance
    pairs = [(source, source ^ mask) for source in range(lax.axis_size(axis))]
    return lax.ppermute(value, axis, pairs)


def kernel_block(raw_points, order):
    ordered = jnp.take(raw_points, order, axis=1)
    dist_sq = (ordered[0][:, None] - ordered[0][None, :]) ** 2
    dist_sq = dist_sq + (ordered[1][:, None] - ordered[1][None, :]) ** 2
    dist_sq = dist_sq + (ordered[2][:, None] - ordered[2][None, :]) ** 2
    scaled = jnp.sqrt(3.0 * dist_sq + smallest) / length_scale
    count = ordered.shape[1]
    return ((1.0 + scaled) * jnp.exp(-scaled) + nugget * jnp.eye(count, dtype=jnp.float32)).astype(
        jnp.bfloat16
    )


def local_gram(left, right):
    return lax.dot_general(
        left,
        right,
        (((0,), (0,)), ((), ())),
        precision=lax.Precision.HIGHEST,
        preferred_element_type=jnp.float32,
    )


def product(left, right):
    return jnp.dot(left, right, precision=lax.Precision.HIGHEST, preferred_element_type=jnp.float32)


def solve_spd(matrix, target):
    symmetric = 0.5 * (matrix + matrix.T)
    factor = jnp.linalg.cholesky(symmetric)
    return jax.scipy.linalg.cho_solve((factor, True), target)


def body(points, leaf_order, skeleton, basis, transfer, coupling, solution, residual, direction):
    skel_rows = skeleton[0]
    rank = basis.shape[1]
    levels = lax.axis_size("leaf").bit_length() - 1
    position = lax.axis_index("leaf")
    res_gram = lax.psum(local_gram(residual, residual), "leaf")
    for step_index in range(ITERS):
        block = kernel_block(points, leaf_order)
        vector_low = direction.astype(jnp.bfloat16)
        near = jnp.dot(block, vector_low, preferred_element_type=jnp.float32)
        current = lax.dot_general(
            basis, vector_low, (((0,), (0,)), ((), ())), preferred_element_type=jnp.float32
        )
        current = (current + jnp.take(direction, skel_rows, axis=0)).astype(jnp.bfloat16)
        coupled = []
        for tree_level in range(levels):
            sibling = swapped(current, "leaf", tree_level)
            coupled.append(
                jnp.dot(coupling[0, tree_level], sibling, preferred_element_type=jnp.float32)
            )
            if tree_level < levels - 1:
                on_right = position >> tree_level & 1 == 1
                stacked = jnp.where(
                    on_right,
                    jnp.concatenate([sibling, current], 0),
                    jnp.concatenate([current, sibling], 0),
                )
                current = lax.dot_general(
                    transfer[0, tree_level],
                    stacked,
                    (((0,), (0,)), ((), ())),
                    preferred_element_type=jnp.float32,
                ).astype(jnp.bfloat16)
        downward = coupled[levels - 1]
        for tree_level in reversed(range(levels - 1)):
            on_right = position >> tree_level & 1 == 1
            halves = jnp.where(
                on_right, transfer[0, tree_level, rank:], transfer[0, tree_level, :rank]
            ).astype(jnp.float32)
            downward = coupled[tree_level] + product(halves, downward)
        result = near + jnp.dot(
            basis, downward.astype(jnp.bfloat16), preferred_element_type=jnp.float32
        )
        image = result.at[skel_rows].add(downward)
        curvature = lax.psum(local_gram(direction, image), "leaf")
        alpha = solve_spd(curvature, res_gram)
        solution = solution + product(direction, alpha)
        residual = residual - product(image, alpha)
        fresh = lax.psum(local_gram(residual, residual), "leaf")
        beta = solve_spd(res_gram, fresh)
        direction = residual + product(direction, beta)
        res_gram = fresh
    return (solution, residual, direction)


def solution(mesh):
    placed = (
        P(None, ("groups", "leaf")),
        P(("groups", "leaf")),
        P(("groups", "leaf"), None),
        P(("groups", "leaf"), None),
        P(("groups", "leaf"), None, None, None),
        P(("groups", "leaf"), None, None, None),
        P(("groups", "leaf"), None),
        P(("groups", "leaf"), None),
        P(("groups", "leaf"), None),
    )
    return jax.shard_map(
        body,
        mesh=mesh,
        in_specs=placed,
        out_specs=(
            P(("groups", "leaf"), None),
            P(("groups", "leaf"), None),
            P(("groups", "leaf"), None),
        ),
        check_vma=False,
    )
```

profile of v0, /device:TPU:0, one launch (start us, length us, event | category | flops | bytes accessed | tf_op | source)
XLA Modules:
  0.0 674.3 jit_solution(3719576984923543411)
XLA Ops:
  21.0 5.0 fusion.1
  37.7 5.6 collective-permute-done.3
  56.6 87.6 %all-reduce.13.cloned.1.call-done = (f32[256,256]{1,0:T(8,128)}, f32[256,256]{1,0:T(8,128)}) async-done(((f32[256,256]{1,0:T(8,128)}, f32[256,256]{1,0:T(8,128)}), (f32[256,256]{1,0:T(8,128)}, f32[256,256]{1,0:T(8,128)})) %all-reduce.13.cloned.1.call-update) | async-done | bytes 524304 | tf_op jit(solution)/shard_map/psum | solution.py:57
  146.7 11.7 %cholesky.214 = f32[128,128]{1,0:T(8,128)S(1)} custom-call(f32[128,128]{1,0:T(8,128)S(1)} %cholesky.346), custom_call_target="Cholesky" | custom-call | tf_op jit(solution)/shard_map/jit(cholesky)/cholesky | solution.py:48
  158.5 9.8 %custom-call.19 = f32[1,128,128]{1,2,0:T(8,128)S(1)} custom-call(f32[1,128,128]{2,1,0:T(8,128)S(1)} %get-tuple-element.103), custom_call_target="InvertDiagBlocksLowerTriangular" | custom-call | tf_op jit(solution)/shard_map/jit(cholesky)/cholesky | solution.py:48
  168.8 11.7 %cholesky.231 = f32[128,128]{1,0:T(8,128)S(1)} custom-call(f32[128,128]{1,0:T(8,128)S(1)} %convolution_subtract_fusion.13), custom_call_target="Cholesky" | custom-call | tf_op jit(solution)/shard_map/jit(cholesky)/cholesky | solution.py:48
  183.2 4.2 while.8
  187.4 19.7 %custom-call.20 = f32[2,128,128]{1,2,0:T(8,128)S(1)} custom-call(f32[2,128,128]{2,1,0:T(8,128)S(1)} %get-tuple-element.33), custom_call_target="InvertDiagBlocksLowerTriangular" | custom-call | tf_op jit(solution)/shard_map/jit(_cho_solve)/triangular_solve | solution.py:49
  212.9 11.7 %cholesky.248 = f32[128,128]{1,0:T(8,128)S(1)} custom-call(f32[128,128]{1,0:T(8,128)S(1)} %cholesky.349), custom_call_target="Cholesky" | custom-call | tf_op jit(solution)/shard_map/jit(cholesky)/cholesky | solution.py:48
  224.7 9.8 %custom-call.21 = f32[1,128,128]{1,2,0:T(8,128)S(1)} custom-call(f32[1,128,128]{2,1,0:T(8,128)S(1)} %get-tuple-element.99), custom_call_target="InvertDiagBlocksLowerTriangular" | custom-call | tf_op jit(solution)/shard_map/jit(cholesky)/cholesky | solution.py:48
  235.0 11.7 %cholesky.265 = f32[128,128]{1,0:T(8,128)S(1)} custom-call(f32[128,128]{1,0:T(8,128)S(1)} %convolution_subtract_fusion.12), custom_call_target="Cholesky" | custom-call | tf_op jit(solution)/shard_map/jit(cholesky)/cholesky | solution.py:48
  249.3 4.1 while.9
  253.4 19.7 %custom-call.22 = f32[2,128,128]{1,2,0:T(8,128)S(1)} custom-call(f32[2,128,128]{2,1,0:T(8,128)S(1)} %get-tuple-element.34), custom_call_target="InvertDiagBlocksLowerTriangular" | custom-call | tf_op jit(solution)/shard_map/jit(_cho_solve)/triangular_solve | solution.py:49
  273.1 29.4 %all-reduce.7.cloned.1.call-done = f32[256,256]{1,0:T(8,128)} async-done(((f32[256,256]{1,0:T(8,128)}), f32[256,256]{1,0:T(8,128)}) %all-reduce.7.cloned.1.call-update) | async-done | bytes 262160 | tf_op jit(solution)/shard_map/psum | solution.py:100
  308.2 5.5 fusion
  318.0 11.7 %cholesky.316 = f32[128,128]{1,0:T(8,128)S(1)} custom-call(f32[128,128]{1,0:T(8,128)S(1)} %cholesky.355), custom_call_target="Cholesky" | custom-call | tf_op jit(solution)/shard_map/jit(cholesky)/cholesky | solution.py:48
  331.9 11.3 %custom-call.25 = f32[1,128,128]{1,2,0:T(8,128)} custom-call(f32[1,128,128]{2,1,0:T(8,128)} %get-tuple-element.91), custom_call_target="InvertDiagBlocksLowerTriangular" | custom-call | tf_op jit(solution)/shard_map/jit(cholesky)/cholesky | solution.py:48
  345.2 11.7 %cholesky.333 = f32[128,128]{1,0:T(8,128)S(1)} custom-call(f32[128,128]{1,0:T(8,128)S(1)} %convolution_subtract_fusion.10), custom_call_target="Cholesky" | custom-call | tf_op jit(solution)/shard_map/jit(cholesky)/cholesky | solution.py:48
  359.0 4.8 collective-permute-done.5
  375.5 6.5 collective-permute-done.7
  387.5 4.4 scatter_fusion.1
  391.9 3.7 fusion.192
  395.7 3.9 while.11
  399.6 20.3 %custom-call.26 = f32[2,128,128]{1,2,0:T(8,128)} custom-call(f32[2,128,128]{2,1,0:T(8,128)S(1)} %get-tuple-element.36), custom_call_target="InvertDiagBlocksLowerTriangular" | custom-call | tf_op jit(solution)/shard_map/jit(_cho_solve)/triangular_solve | solution.py:49
  419.9 63.9 %all-reduce.9.cloned.1.call-done = f32[256,256]{1,0:T(8,128)} async-done(((f32[256,256]{1,0:T(8,128)}), f32[256,256]{1,0:T(8,128)}) %all-reduce.9.cloned.1.call-update) | async-done | bytes 262160 | tf_op jit(solution)/shard_map/psum | solution.py:96
  489.1 11.7 %cholesky.282 = f32[128,128]{1,0:T(8,128)S(1)} custom-call(f32[128,128]{1,0:T(8,128)S(1)} %cholesky.352), custom_call_target="Cholesky" | custom-call | tf_op jit(solution)/shard_map/jit(cholesky)/cholesky | solution.py:48
  502.9 11.3 %custom-call.23 = f32[1,128,128]{1,2,0:T(8,128)} custom-call(f32[1,128,128]{2,1,0:T(8,128)} %get-tuple-element.95), custom_call_target="InvertDiagBlocksLowerTriangular" | custom-call | tf_op jit(solution)/shard_map/jit(cholesky)/cholesky | solution.py:48
  517.0 13.2 %cholesky.299 = f32[128,128]{1,0:T(8,128)} custom-call(f32[128,128]{1,0:T(8,128)} %convolution_subtract_fusion.11), custom_call_target="Cholesky" | custom-call | tf_op jit(solution)/shard_map/jit(cholesky)/cholesky | solution.py:48
  535.2 5.0 while.10
  540.2 21.3 %custom-call.24 = f32[2,128,128]{1,2,0:T(8,128)} custom-call(f32[2,128,128]{2,1,0:T(8,128)} %get-tuple-element.35), custom_call_target="InvertDiagBlocksLowerTriangular" | custom-call | tf_op jit(solution)/shard_map/jit(_cho_solve)/triangular_solve | solution.py:49
  572.4 4.4 fusion.5
  579.4 82.5 %all-reduce.11.cloned.1.call-done = f32[256,256]{1,0:T(8,128)} async-done(((f32[256,256]{1,0:T(8,128)}), f32[256,256]{1,0:T(8,128)}) %all-reduce.11.cloned.1.call-update) | async-done | bytes 262160 | tf_op jit(solution)/shard_map/psum | solution.py:100
  (264 shorter events, 131.9 us)
Async XLA Ops:
  7.2 3.8 copy-start
  7.2 137.0 %all-reduce.13.cloned.1.call-start = ((), (), s32[]{:S(2)}) async-start(), calls=%async_computation.3 | async-start | bytes 1048576 | tf_op jit(solution)/shard_map/psum | solution.py:57
  11.4 4.6 collective-permute-start
  15.9 10.0 %copy-start.37 = (f32[1024]{0:T(1024)}, f32[1024]{0:T(1024)S(1)}, u32[]{:S(2)}) copy-start(f32[1024]{0:T(1024)S(1)} %get-tuple-element.45) | copy-start | bytes 12292
  18.2 7.8 %collective-permute-start.1 = (bf16[256,256]{1,0:T(8,128)(2,1)}, bf16[256,256]{1,0:T(8,128)(2,1)S(1)}, u32[]{:S(2)}, u32[]{:S(2)}) collective-permute-start(bf16[256,256]{1,0:T(8,128)(2,1)} %fusion.16), channel_id=1, source_target_pairs={{0,2},{1,3},{2,0},{3,1},{4,6},{5,7},{6,4},{7,5},{8,10},{9,11},{10,... | collective-permute-start | bytes 393224 | tf_op jit(solution)/shard_map/ppermute | solution.py:17
  26.0 3.6 copy-start.10
  28.0 5.7 collective-permute-start.2
  32.1 5.6 copy-start.39
  32.1 11.3 %copy-start.14 = (bf16[1,4,256,256]{3,2,1,0:T(8,128)(2,1)S(1)}, bf16[1,4,256,256]{3,2,1,0:T(8,128)(2,1)}, u32[]{:S(2)}) copy-start(bf16[1,4,256,256]{3,2,1,0:T(8,128)(2,1)} %param.21) | copy-start | bytes 1572868
  35.1 8.3 %collective-permute-start.3 = (bf16[256,256]{0,1:T(8,128)(2,1)S(1)}, bf16[256,256]{0,1:T(8,128)(2,1)S(1)}, u32[]{:S(2)}, u32[]{:S(2)}) collective-permute-start(bf16[256,256]{0,1:T(8,128)(2,1)S(1)} %fusion.18), channel_id=1, source_target_pairs={{0,8},{1,9},{2,10},{3,11},{4,12},{5,13},{6,14},{7,15},{8,0},{9,1},... | collective-permute-start | bytes 393224 | tf_op jit(solution)/shard_map/ppermute | solution.py:17
  53.8 248.7 %all-reduce.7.cloned.1.call-start = ((), (), s32[]{:S(2)}) async-start(), calls=%async_computation | async-start | bytes 524288 | tf_op jit(solution)/shard_map/psum | solution.py:100
  212.5 271.3 %all-reduce.9.cloned.1.call-start = ((), (), s32[]{:S(2)}) async-start(), calls=%async_computation.1 | async-start | bytes 524288 | tf_op jit(solution)/shard_map/psum | solution.py:96
  253.4 52.7 %copy-start.42 = (s32[2,2]{1,0:T(2,128)}, s32[2,2]{1,0:T(2,128)S(1)}, u32[]{:S(2)}) copy-start(s32[2,2]{1,0:T(2,128)S(1)} %get-tuple-element.327) | copy-start | bytes 52
  302.5 3.7 copy-start.3
  308.2 5.5 copy-start.12
  315.5 27.6 %copy-start.41 = (pred[256]{0:T(512)(128)(4,1)S(1)}, pred[256]{0:T(512)(128)(4,1)}, u32[]{:S(2)}) copy-start(pred[256]{0:T(512)(128)(4,1)} %copy-done.40) | copy-start | bytes 772
  344.1 12.7 %collective-permute-start.4 = (bf16[256,256]{1,0:T(8,128)(2,1)}, bf16[256,256]{1,0:T(8,128)(2,1)S(1)}, u32[]{:S(2)}, u32[]{:S(2)}) collective-permute-start(bf16[256,256]{1,0:T(8,128)(2,1)} %fusion.15), channel_id=1, source_target_pairs={{0,1},{1,0},{2,3},{3,2},{4,5},{5,4},{6,7},{7,6},{8,9},{9,8},{10,11... | collective-permute-start | bytes 393224 | tf_op jit(solution)/shard_map/ppermute | solution.py:17
  356.9 8.8 %copy-start.28 = (bf16[256,256]{1,0:T(8,128)(2,1)}, bf16[256,256]{1,0:T(8,128)(2,1)S(1)}, u32[]{:S(2)}) copy-start(bf16[256,256]{1,0:T(8,128)(2,1)S(1)} %collective-permute-done.4) | copy-start | bytes 393220
  358.3 5.5 collective-permute-start.5
  363.8 4.8 copy-start.30
  365.7 6.5 collective-permute-start.6
  371.2 10.8 %copy-start.15 = (bf16[1,4,256,256]{3,2,1,0:T(8,128)(2,1)S(1)}, bf16[1,4,256,256]{3,2,1,0:T(8,128)(2,1)}, u32[]{:S(2)}) copy-start(bf16[1,4,256,256]{3,2,1,0:T(8,128)(2,1)} %param.21) | copy-start | bytes 1572868
  371.2 11.0 %copy-start.24 = (bf16[1,3,512,256]{3,2,1,0:T(8,128)(2,1)S(1)}, bf16[1,3,512,256]{3,2,1,0:T(8,128)(2,1)}, u32[]{:S(2)}) copy-start(bf16[1,3,512,256]{3,2,1,0:T(8,128)(2,1)} %param.20) | copy-start | bytes 2359300
  372.2 3.2 copy-start.32
  373.6 8.3 %collective-permute-start.7 = (bf16[256,256]{0,1:T(8,128)(2,1)S(1)}, bf16[256,256]{0,1:T(8,128)(2,1)S(1)}, u32[]{:S(2)}, u32[]{:S(2)}) collective-permute-start(bf16[256,256]{0,1:T(8,128)(2,1)S(1)} %fusion.21), channel_id=1, source_target_pairs={{0,8},{1,9},{2,10},{3,11},{4,12},{5,13},{6,14},{7,15},{8,0},{9,1},... | collective-permute-start | bytes 393224 | tf_op jit(solution)/shard_map/ppermute | solution.py:17
  375.4 7.3 %copy-start.33 = (bf16[256,256]{1,0:T(8,128)(2,1)S(1)}, bf16[256,256]{1,0:T(8,128)(2,1)}, u32[]{:S(2)}) copy-start(bf16[256,256]{1,0:T(8,128)(2,1)} %copy-done.32) | copy-start | bytes 393220
  391.9 3.8 copy-start.43
  395.6 266.2 %all-reduce.11.cloned.1.call-start = ((), (), s32[]{:S(2)}) async-start(), calls=%async_computation.2 | async-start | bytes 524288 | tf_op jit(solution)/shard_map/psum | solution.py:100
  561.5 5.3 copy-start.4
  561.5 5.3 copy-start.5
  576.8 85.1 %copy-start.25 = (f32[2,128,128]{1,2,0:T(8,128)S(1)}, f32[2,128,128]{1,2,0:T(8,128)}, u32[]{:S(2)}) copy-start(f32[2,128,128]{1,2,0:T(8,128)} %custom-call.26) | copy-start | bytes 393220
  579.4 86.1 %copy-start.9 = (f32[1024,256]{1,0:T(8,128)S(1)}, f32[1024,256]{1,0:T(8,128)}, u32[]{:S(2)}) copy-start(f32[1024,256]{1,0:T(8,128)} %copy-done.8) | copy-start | bytes 3145732
  (24 other events, 37.7 us)
Sparse Core Ops, SparseCore 0:
  53.9 90.2 all-reduce.12
  212.6 89.8 all-reduce.6
  395.8 87.9 all-reduce.8
  572.5 89.2 all-reduce.10
where the time goes:
time: 684 us; the launch traced here: 674 us
  waiting for transfers between devices  283 us (41%)
  other arithmetic  239 us (35%)
  matrix products  75.2 us (11%)
  local copies, waits for them, and re-layouts  41.9 us (6%)
  between operations  20.1 us (3%)
  starting transfers between devices  14 us (2%)
    another operation x28, other arithmetic, solve_spd(): factor = jnp.linalg.cholesky(symmetric)  145 us
    psum x2, waiting for transfers between devices, body(): fresh = lax.psum(local_gram(residual, residual), 'leaf')  112 us
    psum x1, waiting for transfers between devices, body(): res_gram = lax.psum(local_gram(residual, residual), 'leaf')  87.6 us
    another operation x9, other arithmetic, solve_spd(): return jax.scipy.linalg.cho_solve((factor, True), target)  82 us
    psum x1, waiting for transfers between devices, body(): curvature = lax.psum(local_gram(direction, image), 'leaf')  63.9 us
    ppermute x8, waiting for transfers between devices, swapped(): return lax.ppermute(value, axis, pairs)  19.5 us
    another operation x29, local copies, waits for them, and re-layouts, solve_spd(): return jax.scipy.linalg.cho_solve((factor, True), target)  17.2 us
    another operation x24, matrix products, solve_spd(): return jax.scipy.linalg.cho_solve((factor, True), target)  14 us
  transfers between devices with their start and end apart: 12, of which 9 were waited for; matrix products, arithmetic and copies ran while one was open for 17% of the time, Pallas kernels for 0%

commit v1 on v0

v1 whole, which is shorter than its diff:
```python
import functools

import jax
import jax.numpy as jnp
from jax import lax
from jax.experimental import pallas as pl
from jax.experimental.pallas import tpu as pltpu
from jax.sharding import PartitionSpec as P

ITERS = 2
F32 = jnp.float32
BF16 = jnp.bfloat16
VMEM = pl.BlockSpec(memory_space=pltpu.VMEM)
SMEM = pl.BlockSpec(memory_space=pltpu.SMEM)
MAX_STEPS = 60
BOUND = 1e-5


def dot(left, right):
    return jnp.dot(left, right, preferred_element_type=F32)


def dot_t(left, right):
    return lax.dot_general(left, right, (((0,), (0,)), ((), ())), preferred_element_type=F32)


def split(value):
    high = value.astype(BF16)
    return high, (value - high.astype(F32)).astype(BF16)


def dot3(left, right):
    lh, ll = split(left)
    rh, rl = split(right)
    return dot(lh, rh) + (dot(lh, rl) + dot(ll, rh))


def dot_full(left, right):
    return jnp.dot(left, right, precision=lax.Precision.HIGHEST, preferred_element_type=F32)


def iotas(rows, columns):
    return (
        lax.broadcasted_iota(jnp.int32, (rows, columns), 0),
        lax.broadcasted_iota(jnp.int32, (rows, columns), 1),
    )


def eye_mask(size):
    row, column = iotas(size, size)
    return row == column


def skeleton_columns(skel_ref, count):
    row, _ = iotas(count, skel_ref.shape[1])
    return jnp.where(row == skel_ref[...], 1.0, 0.0).astype(BF16)


def skeleton_rows(skel_ref, count):
    rank = skel_ref.shape[1]
    wide = jnp.broadcast_to(skel_ref[...].astype(F32), (128, rank)).T
    column = lax.broadcasted_iota(jnp.int32, (rank, 128), 1).astype(F32)
    tiles = [
        jnp.where(wide == column + float(start), 1.0, 0.0).astype(BF16)
        for start in range(0, count, 128)
    ]
    return jnp.concatenate(tiles, 1)


def leaf_coefficients(vector, basis_ref, skel_ref):
    high, low = split(vector)
    picks = skeleton_rows(skel_ref, vector.shape[0])
    coef = dot_t(basis_ref[...], high) + (dot(picks, high) + dot(picks, low))
    return coef.astype(BF16)


def coef_kernel(direction_ref, basis_ref, skel_ref, coef_ref):
    coef_ref[...] = leaf_coefficients(direction_ref[...], basis_ref, skel_ref)


def block_kernel(points_ref, order_ref, direction_ref, block_ref, near_ref, padded, column_ref):
    count = points_ref.shape[1]
    padded[...] = jnp.zeros_like(padded)
    padded[0:3, :] = points_ref[...]
    raw = padded[...]
    high = raw.astype(BF16).astype(F32)
    middle = (raw - high).astype(BF16).astype(F32)
    low = raw - high - middle
    parts = jnp.concatenate([high, middle, low], 0).astype(BF16)
    row, _ = iotas(count, count)
    picks = jnp.where(row == order_ref[...], 1.0, 0.0).astype(BF16)
    ordered = dot(parts, picks)
    ordered = (ordered[0:8] + ordered[8:16] + ordered[16:24]) * (300.0**0.5)
    column_ref[...] = jnp.concatenate([ordered, jnp.zeros((120, count), F32)], 0).T
    low_direction = direction_ref[...].astype(BF16)
    strip = 128

    def step(index, carry):
        start = pl.multiple_of(index * strip, strip)
        mine = column_ref[pl.ds(start, strip), :]
        square = 1e-10
        for axis in range(3):
            gap = mine[:, axis : axis + 1] - ordered[axis : axis + 1, :]
            square = gap * gap + square
        scaled = square * lax.rsqrt(square)
        values = ((1.0 + scaled) * jnp.exp(-scaled)).astype(BF16)
        block_ref[pl.ds(start, strip), :] = values
        return carry

    lax.fori_loop(0, count // strip, step, 0)
    near_ref[...] = dot(block_ref[...], low_direction) + 2.0 * low_direction.astype(F32)


def near_kernel(block_ref, direction_ref, near_ref):
    low_direction = direction_ref[...].astype(BF16)
    near_ref[...] = dot(block_ref[...], low_direction) + 2.0 * low_direction.astype(F32)


def gram_kernel(value_ref, gram_ref):
    high, low = split(value_ref[...])
    both = dot_t(high, jnp.concatenate([high, low], 1))
    size = high.shape[1]
    cross = both[:, size:]
    gram_ref[...] = both[:, :size] + (cross + cross.T)


def up_kernel(level, position_ref, current_ref, sibling_ref, transfer_ref, coef_ref):
    rank = current_ref.shape[0]
    right = (position_ref[0] >> level) & 1
    mine = transfer_ref[0, level, pl.ds(pl.multiple_of(right * rank, rank), rank), :]
    other = transfer_ref[0, level, pl.ds(pl.multiple_of((1 - right) * rank, rank), rank), :]
    coef_ref[...] = (
        dot_t(mine, current_ref[...]) + dot_t(other, sibling_ref[...])
    ).astype(BF16)


def pack_pair(first, second):
    size = first.shape[0]
    row, column = iotas(size, size)
    diagonal = jnp.sum(jnp.where(row == column, second, 0.0), axis=0, keepdims=True)
    return jnp.where(row >= column, first, second), diagonal


def unpack_pair(packed, diagonal):
    size = packed.shape[0]
    row, column = iotas(size, size)
    turned = packed.T
    first = jnp.where(row >= column, packed, turned)
    second = jnp.where(row < column, packed, turned)
    return first, jnp.where(row == column, diagonal, second)


def payload_rows(size, with_start):
    rows = 2 * size + 8 + (size // 2 if with_start else 0)
    return -(-rows // 32) * 32


def down_kernel(levels, with_start, *refs):
    position_ref, near_ref = refs[0], refs[1]
    siblings = refs[2 : 2 + levels]
    (coupling_ref, transfer_ref, basis_ref, skel_ref, direction_ref, residual_ref) = refs[
        2 + levels : 8 + levels
    ]
    rest = list(refs[8 + levels :])
    start_ref = rest.pop(0) if with_start else None
    image_ref, keep_ref, send_ref, payload = rest
    rank = basis_ref.shape[1]
    count, size = direction_ref.shape
    position = position_ref[0]
    down = dot(coupling_ref[0, levels - 1], siblings[levels - 1][...])
    for level in reversed(range(levels - 1)):
        right = (position >> level) & 1
        half = transfer_ref[0, level, pl.ds(pl.multiple_of(right * rank, rank), rank), :]
        high, low = split(down)
        down = dot(coupling_ref[0, level], siblings[level][...]) + (dot(half, high) + dot(half, low))
    high, low = split(down)
    places = skeleton_columns(skel_ref, count)
    image = near_ref[...] + dot(basis_ref[...], high) + (dot(places, high) + dot(places, low))
    image_ref[...] = image
    image_high, image_low = split(image)
    both = jnp.concatenate([image_high, image_low], 1)
    direction_high, direction_low = split(direction_ref[...])
    residual_high, residual_low = split(residual_ref[...])
    wide = dot_t(direction_high, both)
    curvature = wide[:, :size] + (wide[:, size:] + dot_t(direction_low, image_high))
    wide = dot_t(residual_high, both)
    mixed = wide[:, :size] + (wide[:, size:] + dot_t(residual_low, image_high))
    wide = dot_t(image_high, both)
    cross = wide[:, size:]
    images = wide[:, :size] + (cross + cross.T)
    curvature = 0.5 * (curvature + curvature.T)
    payload[size : 2 * size, :] = mixed
    base = 2 * size
    if with_start:
        pair, diagonal = pack_pair(curvature, start_ref[...])
        half = size // 2
        tri, tail = pack_pair(images[:half, :half], images[half:, half:])
        payload[base : base + half, :] = jnp.concatenate([images[half:, :half], tri], 1)
        base += half
        tail = jnp.concatenate([tail, tail], 1)
    else:
        pair, diagonal = pack_pair(curvature, images)
        tail = diagonal
    payload[0:size, :] = pair
    payload[base:, :] = jnp.zeros((payload.shape[0] - base, size), F32)
    payload[base : base + 1, :] = diagonal
    payload[base + 1 : base + 2, :] = tail
    quarter = payload.shape[0] // 4
    core, side = position & 1, (position >> 1) & 1

    def part(core_at, side_at):
        start = pl.multiple_of((core_at * 2 + side_at) * quarter, 8)
        return payload[pl.ds(start, quarter), :]

    keep_ref[0:quarter, :] = part(core, side)
    keep_ref[quarter:, :] = part(core, 1 - side)
    send_ref[0:quarter, :] = part(1 - core, side)
    send_ref[quarter:, :] = part(1 - core, 1 - side)


def scaled_problem(matrix):
    size = matrix.shape[0]
    eye = eye_mask(size)
    picked = jnp.where(eye, matrix, 0.0)
    row_scale = lax.rsqrt(jnp.sum(picked, axis=0, keepdims=True))
    column_scale = lax.rsqrt(jnp.sum(picked, axis=1, keepdims=True))
    scaled = matrix * column_scale * row_scale
    widest = jnp.max(jnp.sum(jnp.abs(scaled), axis=0, keepdims=True), axis=1, keepdims=True)
    return scaled, column_scale, 1.8 / widest


def inverses(matrices, store, errors):
    count = len(matrices)
    size = matrices[0].shape[0]
    eye = jnp.where(eye_mask(size), 1.0, 0.0)
    problems = [scaled_problem(matrix) for matrix in matrices]
    starts = [eye * gain for _, _, gain in problems]
    slopes = [eye - scaled * gain for scaled, _, gain in problems]
    guesses = [start + slope * gain for start, slope, (_, _, gain) in zip(starts, slopes, problems)]
    gaps = list(slopes)
    for _ in range(3):
        for at in range(count):
            rough = gaps[at].astype(BF16)
            gaps[at] = dot(rough, rough)
        for at in range(count):
            guesses[at] = guesses[at] + dot(guesses[at].astype(BF16), gaps[at].astype(BF16))
    total = 0.0
    for at in range(count):
        scaled = problems[at][0]
        gap = eye - dot_full(scaled, guesses[at])
        near = jnp.sum(jnp.sum(gap * gap, axis=0, keepdims=True), axis=1, keepdims=True) < 0.5
        guess = jnp.where(near, guesses[at], starts[at])
        gap = jnp.where(near, gap, slopes[at])
        guess = guess + dot3(guess, gap)
        gap = eye - dot_full(scaled, guess)
        store[at], errors[at] = guess, gap
        total = total + jnp.sum(gap * gap)

    def unfinished(carry):
        step, total = carry
        return (step < MAX_STEPS) & (total > BOUND)

    def refine(carry):
        step, _ = carry
        total = 0.0
        for at in range(count):
            guess = store[at] + dot3(store[at], errors[at])
            gap = eye - dot_full(problems[at][0], guess)
            store[at], errors[at] = guess, gap
            total = total + jnp.sum(gap * gap)
        return step + 1, total

    lax.while_loop(unfinished, refine, (0, total))
    results = []
    for at in range(count):
        guess = store[at]
        results.append(guess + dot(guess.astype(BF16), errors[at].astype(BF16)))
    return [(result, problem[1]) for result, problem in zip(results, problems)]


def solve_kernel(with_start, last, *refs):
    position_ref, own_ref, side_ref, core_ref, far_ref = refs[:5]
    rest = list(refs[5:])
    start_ref = None if with_start else rest.pop(0)
    image_ref, residual_ref, direction_ref = rest[:3]
    rest = rest[3:]
    if last:
        solution_ref = rest.pop(0)
        solution_out, residual_out, direction_out = rest[:3]
        rest = rest[3:]
    else:
        basis_ref, skel_ref = rest[:2]
        direction_out, coef_out, alpha_out, fresh_out = rest[2:6]
        rest = rest[6:]
    payload, store, errors = rest
    size = direction_ref.shape[1]
    quarter = payload.shape[0] // 4
    position = position_ref[0]
    core, side = position & 1, (position >> 1) & 1
    for ref, core_at, side_at in (
        (own_ref, core, side),
        (side_ref, core, 1 - side),
        (core_ref, 1 - core, side),
        (far_ref, 1 - core, 1 - side),
    ):
        start = pl.multiple_of((core_at * 2 + side_at) * quarter, 8)
        payload[pl.ds(start, quarter), :] = ref[...]
    mixed = payload[size : 2 * size, :]
    base = 2 * size
    if with_start:
        half = size // 2
        low_rows = payload[base : base + half, :]
        base += half
        curvature, res_gram = unpack_pair(payload[0:size, :], payload[base : base + 1, :])
        upper, lower = unpack_pair(low_rows[:, half:], payload[base + 1 : base + 2, :half])
        corner = low_rows[:, :half]
        images = jnp.concatenate(
            [jnp.concatenate([upper, corner.T], 1), jnp.concatenate([corner, lower], 1)], 0
        )
    else:
        curvature, images = unpack_pair(payload[0:size, :], payload[base : base + 1, :])
        res_gram = start_ref[...]
    (first, first_scale), (second, second_scale) = inverses([curvature, res_gram], store, errors)
    alpha = dot3(first, res_gram * first_scale) * first_scale
    slope = dot3(mixed, alpha)
    bend = dot3(alpha.T, dot3(images, alpha))
    change = 0.5 * bend - slope
    fresh = res_gram + (change + change.T)
    beta = dot3(second, fresh * second_scale) * second_scale
    direction = direction_ref[...]
    residual = residual_ref[...] - dot3(image_ref[...], alpha)
    moved = residual + dot3(direction, beta)
    direction_out[...] = moved
    if last:
        residual_out[...] = residual
        solution_out[...] = solution_ref[...] + dot3(direction, alpha)
    else:
        coef_out[...] = leaf_coefficients(moved, basis_ref, skel_ref)
        alpha_out[...] = alpha
        fresh_out[...] = fresh


def update_kernel(
    image_ref, residual_ref, direction_ref, solution_ref, alpha_ref, residual_out, solution_out
):
    alpha = alpha_ref[...]
    residual_out[...] = residual_ref[...] - dot3(image_ref[...], alpha)
    solution_out[...] = solution_ref[...] + dot3(direction_ref[...], alpha)


def call(kernel, name, inputs, outputs, scratch=(), flops=0, limit=32):
    specs = [SMEM if value.dtype == jnp.int32 and value.shape == (1,) else VMEM for value in inputs]
    size = sum(value.size * value.dtype.itemsize for value in inputs)
    return pl.pallas_call(
        kernel,
        name=name,
        in_specs=specs,
        out_specs=[VMEM] * len(outputs),
        out_shape=[jax.ShapeDtypeStruct(shape, dtype) for shape, dtype in outputs],
        scratch_shapes=list(scratch),
        cost_estimate=pl.CostEstimate(flops=flops, bytes_accessed=size, transcendentals=0),
        compiler_params=pltpu.CompilerParams(vmem_limit_bytes=limit * 2**20),
    )(*inputs)


def swapped(value, distance):
    mask = 2**distance
    pairs = [(source, source ^ mask) for source in range(lax.axis_size("leaf"))]
    return lax.ppermute(value, "leaf", pairs)


def body(points, leaf_order, skeleton, basis, transfer, coupling, solution, residual, direction):
    levels = lax.axis_size("leaf").bit_length() - 1
    count, size = direction.shape
    rank = basis.shape[1]
    position = lax.axis_index("leaf").astype(jnp.int32).reshape(1)
    order = leaf_order.reshape(1, count)
    tall = ((count, size), F32)
    square = ((size, size), F32)
    coef = ((rank, size), BF16)
    product = 2 * count * size * size

    (current,) = call(coef_kernel, "coef", [direction, basis, skeleton], [coef], flops=product)
    block, near = call(
        block_kernel,
        "block",
        [points, order, direction],
        [((count, count), BF16), tall],
        [pltpu.VMEM((8, count), F32), pltpu.VMEM((count, 128), F32)],
        flops=20 * product,
    )
    (res_gram,) = call(gram_kernel, "gram", [residual], [square], flops=4 * product)
    for step in range(ITERS):
        first, last = step == 0, step == ITERS - 1
        if not first:
            (near,) = call(near_kernel, "near", [block, direction], [tall], flops=8 * product)
        siblings = []
        for level in range(levels):
            sibling = swapped(current, level)
            siblings.append(sibling)
            if level < levels - 1:
                (current,) = call(
                    functools.partial(up_kernel, level),
                    "up",
                    [position, current, sibling, transfer],
                    [coef],
                    flops=product,
                )
        rows = payload_rows(size, first)
        image, keep, send = call(
            functools.partial(down_kernel, levels, first),
            "down",
            [position, near, *siblings, coupling, transfer, basis, skeleton, direction, residual]
            + ([res_gram] if first else []),
            [tall, ((rows // 2, size), F32), ((rows // 2, size), F32)],
            [pltpu.VMEM((rows, size), F32)],
            flops=10 * product,
        )
        quarter = rows // 4
        half = keep + swapped(send, 0)
        own = half[:quarter] + swapped(half[quarter:], 1)
        for level in range(2, levels):
            own = own + swapped(own, level)
        side = swapped(own, 1)
        core = swapped(own, 0)
        far = swapped(side, 0)
        pieces = [position, own, side, core, far] + ([] if first else [res_gram])
        scratch = [
            pltpu.VMEM((rows, size), F32),
            pltpu.VMEM((2, size, size), F32),
            pltpu.VMEM((2, size, size), F32),
        ]
        if last:
            solution, residual, direction = call(
                functools.partial(solve_kernel, first, True),
                "solve",
                pieces + [image, residual, direction, solution],
                [tall, tall, tall],
                scratch,
                flops=10 * product,
            )
        else:
            moved, current, alpha, res_gram = call(
                functools.partial(solve_kernel, first, False),
                "solve",
                pieces + [image, residual, direction, basis, skeleton],
                [tall, coef, square, square],
                scratch,
                flops=10 * product,
            )
            residual, solution = call(
                update_kernel,
                "update",
                [image, residual, direction, solution, alpha],
                [tall, tall],
                flops=6 * product,
            )
            direction = moved
    return (solution, residual, direction)


def solution(mesh):
    placed = (
        P(None, ("groups", "leaf")),
        P(("groups", "leaf")),
        P(("groups", "leaf"), None),
        P(("groups", "leaf"), None),
        P(("groups", "leaf"), None, None, None),
        P(("groups", "leaf"), None, None, None),
        P(("groups", "leaf"), None),
        P(("groups", "leaf"), None),
        P(("groups", "leaf"), None),
    )
    return jax.shard_map(
        body,
        mesh=mesh,
        in_specs=placed,
        out_specs=(
            P(("groups", "leaf"), None),
            P(("groups", "leaf"), None),
            P(("groups", "leaf"), None),
        ),
        check_vma=False,
    )
```

time: 684 us -> 149 us (0.22); the launches traced: 674 us -> 149 us
  other arithmetic: 239 us -> 0.21 us
  waiting for transfers between devices: 283 us -> 67.3 us
  matrix products: 75.2 us -> 0 us
  Pallas kernels: 0 us -> 53.7 us
  local copies, waits for them, and re-layouts: 41.9 us -> 3.49 us
  between operations: 20.1 us -> 0.89 us
  starting transfers between devices: 14 us -> 23.4 us
    psum x4 -> x0, waiting for transfers between devices: 263 us -> none  [the longest x2 112 us: body(): fresh = lax.psum(local_gram(residual, residual), 'leaf')]
    another operation x37 -> x0, other arithmetic: 227 us -> none  [the longest x28 145 us: solve_spd(): factor = jnp.linalg.cholesky(symmetric)]
    dot_general x37 -> x0, matrix products: 57 us -> none  [the longest x5 13.9 us: local_gram(): lax.dot_general(left, right, (((0,), (0,)), ((), ())), precision=lax.Prec...]
    pallas_call x0 -> x15, Pallas kernels: none -> 53.7 us  [call(): pl.pallas_call(kernel, name=name, in_specs=specs, out_specs=[VMEM] * len(...]
    ppermute x8 -> x22, waiting for transfers between devices: 19.5 us -> 67.3 us  [swapped(): return lax.ppermute(value, 'leaf', pairs)]
    another operation x37 -> x0, local copies, waits for them, and re-layouts: 18.9 us -> none  [the longest x29 17.2 us: solve_spd(): return jax.scipy.linalg.cho_solve((factor, True), target)]
    another operation x32 -> x0, matrix products: 18.2 us -> none  [the longest x24 14 us: solve_spd(): return jax.scipy.linalg.cho_solve((factor, True), target)]
    ppermute x8 -> x22, starting transfers between devices: 13.4 us -> 23.4 us  [swapped(): return lax.ppermute(value, 'leaf', pairs)]
  transfers between devices with their start and end apart: 12 -> 22, of which waited for: 9 -> 20; matrix products, arithmetic and copies ran while one was open for 17% -> 0% of each run, Pallas kernels for 0% -> 4%
where the time goes in v1:
time: 149 us
  waiting for transfers between devices  67.3 us (45%)
  Pallas kernels  53.7 us (36%)
  starting transfers between devices  23.4 us (16%)
  local copies, waits for them, and re-layouts  3.49 us (2%)
    ppermute x22, waiting for transfers between devices, swapped(): return lax.ppermute(value, 'leaf', pairs)  67.3 us
    pallas_call x15, Pallas kernels, call(): pl.pallas_call(kernel, name=name, in_specs=specs, out_specs=[VMEM] * len(...  53.7 us
    ppermute x22, starting transfers between devices, swapped(): return lax.ppermute(value, 'leaf', pairs)  23.4 us
    unnamed x24, local copies, waits for them, and re-layouts  3.47 us
  transfers between devices with their start and end apart: 22, of which 20 were waited for; matrix products, arithmetic and copies ran while one was open for 0% of the time, Pallas kernels for 4%

profile of v1, /device:TPU:0, one launch (start us, length us, event | category | flops | bytes accessed | tf_op | source)
XLA Modules:
  0.0 149.1 jit_solution(9891755461085198738)
XLA Ops:
  6.2 2.9 %collective-permute-start.1 = (bf16[256,256]{1,0:T(8,128)(2,1)S(1)}, bf16[256,256]{1,0:T(8,128)(2,1)S(1)}, u32[]{:S(2)}, u32[]{:S(2)}) collective-permute-start(bf16[256,256]{1,0:T(8,128)(2,1)S(1)} %up.6.current_ref), channel_id=1, source_target_pairs={{0,2},{1,3},{2,0},{3,1},{4,6},{5,7},{6,4},{7,5},{8,10},{9,11},{10,... | collective-permute-start | bytes 393224 | tf_op jit(solution)/shard_map/ppermute | solution.py:369
  9.1 3.8 %collective-permute-done.1.sibling_ref.refs_3_ = bf16[256,256]{1,0:T(8,128)(2,1)S(1)} collective-permute-done((bf16[256,256]{1,0:T(8,128)(2,1)S(1)}, bf16[256,256]{1,0:T(8,128)(2,1)S(1)}, u32[]{:S(2)}, u32[]{:S(2)}) %collective-permute-start.1) | collective-permute-done | bytes 131104 | tf_op jit(solution)/shard_map/ppermute | solution.py:369
  13.2 1.9 %collective-permute-start.2 = (bf16[256,256]{1,0:T(8,128)(2,1)S(1)}, bf16[256,256]{1,0:T(8,128)(2,1)S(1)}, u32[]{:S(2)}, u32[]{:S(2)}) collective-permute-start(bf16[256,256]{1,0:T(8,128)(2,1)S(1)} %up.7.current_ref), channel_id=1, source_target_pairs={{0,4},{1,5},{2,6},{3,7},{4,0},{5,1},{6,2},{7,3},{8,12},{9,13},{10,... | collective-permute-start | bytes 393224 | tf_op jit(solution)/shard_map/ppermute | solution.py:369
  15.1 3.2 %collective-permute-done.2.sibling_ref.refs_4_ = bf16[256,256]{1,0:T(8,128)(2,1)S(1)} collective-permute-done((bf16[256,256]{1,0:T(8,128)(2,1)S(1)}, bf16[256,256]{1,0:T(8,128)(2,1)S(1)}, u32[]{:S(2)}, u32[]{:S(2)}) %collective-permute-start.2) | collective-permute-done | bytes 131104 | tf_op jit(solution)/shard_map/ppermute | solution.py:369
  18.6 2.8 %collective-permute-start.3 = (bf16[256,256]{1,0:T(8,128)(2,1)S(1)}, bf16[256,256]{1,0:T(8,128)(2,1)S(1)}, u32[]{:S(2)}, u32[]{:S(2)}) collective-permute-start(bf16[256,256]{1,0:T(8,128)(2,1)S(1)} %up.8), channel_id=1, source_target_pairs={{0,8},{1,9},{2,10},{3,11},{4,12},{5,13},{6,14},{7,15},{8,0},{9,1},... | collective-permute-start | bytes 393224 | tf_op jit(solution)/shard_map/ppermute | solution.py:369
  21.4 4.3 %block.1 = (bf16[1024,1024]{1,0:T(8,128)(2,1)S(1)}, f32[1024,256]{1,0:T(8,128)S(1)}) custom-call(f32[3,1024]{1,0:T(4,128)S(1)} %copy-done.10, s32[1,1024]{1,0:T(1,128)S(1)} %bitcast.2, f32[1024,256]{1,0:T(8,128)S(1)} %copy-done.2), custom_call_target="tpu_custom_call" | custom-call | flops 2684354560 | bytes 1064960 | tf_op jit(solution)/shard_map/block/pallas_call | solution.py:354
  26.9 3.7 %down.2 = (f32[1024,256]{1,0:T(8,128)S(1)}, f32[336,256]{1,0:T(8,128)S(1)}, f32[336,256]{1,0:T(8,128)S(1)}) custom-call(s32[1]{0:T(128)} %bitcast.position_ref.refs_0_, f32[1024,256]{1,0:T(8,128)S(1)} %get-tuple-element.18.refs_1_, bf16[256,256]{1,0:T(8,128)(2,1)S(1)} %collective-permute-done.sibling_ref.refs_2_, ...), custom_call_target="tpu_custom_call" | custom-call | flops 1342177280 | bytes 5768196 | tf_op jit(solution)/shard_map/down/pallas_call | solution.py:354
  30.7 1.6 %collective-permute-done.4 = f32[336,256]{1,0:T(8,128)S(1)} collective-permute-done((f32[336,256]{1,0:T(8,128)S(1)}, f32[336,256]{1,0:T(8,128)S(1)}, u32[]{:S(2)}, u32[]{:S(2)}) %collective-permute-start.4) | collective-permute-done | bytes 344096 | tf_op jit(solution)/shard_map/ppermute | solution.py:369
  32.4 1.6 %collective-permute-start.5 = (f32[168,256]{1,0:T(8,128)S(1)}, f32[168,256]{1,0:T(8,128)S(1)}, u32[]{:S(2)}, u32[]{:S(2)}) collective-permute-start(f32[168,256]{1,0:T(8,128)S(1)} %slice.17), channel_id=1, source_target_pairs={{0,2},{1,3},{2,0},{3,1},{4,6},{5,7},{6,4},{7,5},{8,10},{9,11},{10,... | collective-permute-start | bytes 516104 | tf_op jit(solution)/shard_map/ppermute | solution.py:369
  33.9 4.9 %collective-permute-done.5 = f32[168,256]{1,0:T(8,128)S(1)} collective-permute-done((f32[168,256]{1,0:T(8,128)S(1)}, f32[168,256]{1,0:T(8,128)S(1)}, u32[]{:S(2)}, u32[]{:S(2)}) %collective-permute-start.5) | collective-permute-done | bytes 172064 | tf_op jit(solution)/shard_map/ppermute | solution.py:369
  38.9 1.6 %collective-permute-start.6 = (f32[168,256]{1,0:T(8,128)S(1)}, f32[168,256]{1,0:T(8,128)S(1)}, u32[]{:S(2)}, u32[]{:S(2)}) collective-permute-start(f32[168,256]{1,0:T(8,128)S(1)} %slice_add_fusion), channel_id=1, source_target_pairs={{0,4},{1,5},{2,6},{3,7},{4,0},{5,1},{6,2},{7,3},{8,12},{9,13},{10,... | collective-permute-start | bytes 516104 | tf_op jit(solution)/shard_map/ppermute | solution.py:369
  40.5 4.0 %collective-permute-done.6 = f32[168,256]{1,0:T(8,128)S(1)} collective-permute-done((f32[168,256]{1,0:T(8,128)S(1)}, f32[168,256]{1,0:T(8,128)S(1)}, u32[]{:S(2)}, u32[]{:S(2)}) %collective-permute-start.6) | collective-permute-done | bytes 172064 | tf_op jit(solution)/shard_map/ppermute | solution.py:369
  44.5 1.6 %collective-permute-start.7 = (f32[168,256]{1,0:T(8,128)S(1)}, f32[168,256]{1,0:T(8,128)S(1)}, u32[]{:S(2)}, u32[]{:S(2)}) collective-permute-start(f32[168,256]{1,0:T(8,128)S(1)} %add.26), channel_id=1, source_target_pairs={{0,8},{1,9},{2,10},{3,11},{4,12},{5,13},{6,14},{7,15},{8,0},{9,1},... | collective-permute-start | bytes 516104 | tf_op jit(solution)/shard_map/ppermute | solution.py:369
  46.1 7.8 %collective-permute-done.7 = f32[168,256]{1,0:T(8,128)S(1)} collective-permute-done((f32[168,256]{1,0:T(8,128)S(1)}, f32[168,256]{1,0:T(8,128)S(1)}, u32[]{:S(2)}, u32[]{:S(2)}) %collective-permute-start.7) | collective-permute-done | bytes 172064 | tf_op jit(solution)/shard_map/ppermute | solution.py:369
  53.9 1.6 %collective-permute-start.8 = (f32[168,256]{1,0:T(8,128)S(1)}, f32[168,256]{1,0:T(8,128)S(1)}, u32[]{:S(2)}, u32[]{:S(2)}) collective-permute-start(f32[168,256]{1,0:T(8,128)S(1)} %add.27.refs_1_), channel_id=1, source_target_pairs={{0,2},{1,3},{2,0},{3,1},{4,6},{5,7},{6,4},{7,5},{8,10},{9,11},{10,... | collective-permute-start | bytes 516104 | tf_op jit(solution)/shard_map/ppermute | solution.py:369
  55.5 3.9 %collective-permute-done.8.refs_2_ = f32[168,256]{1,0:T(8,128)S(1)} collective-permute-done((f32[168,256]{1,0:T(8,128)S(1)}, f32[168,256]{1,0:T(8,128)S(1)}, u32[]{:S(2)}, u32[]{:S(2)}) %collective-permute-start.8) | collective-permute-done | bytes 172064 | tf_op jit(solution)/shard_map/ppermute | solution.py:369
  60.8 16.3 %solve.2 = (f32[1024,256]{1,0:T(8,128)S(1)}, bf16[256,256]{1,0:T(8,128)(2,1)S(1)}, f32[256,256]{1,0:T(8,128)S(1)}, f32[256,256]{1,0:T(8,128)S(1)}) custom-call(s32[1]{0:T(128)} %bitcast.position_ref.refs_0_, f32[168,256]{1,0:T(8,128)S(1)} %add.27.refs_1_, f32[168,256]{1,0:T(8,128)S(1)} %collective-permute-done.8.refs_2_, ...), custom_call_target="tpu_custom_call" | custom-call | flops 1342177280 | bytes 4359172 | tf_op jit(solution)/shard_map/solve/pallas_call | solution.py:354
  78.8 1.6 %collective-permute-start.12 = (bf16[256,256]{1,0:T(8,128)(2,1)S(1)}, bf16[256,256]{1,0:T(8,128)(2,1)S(1)}, u32[]{:S(2)}, u32[]{:S(2)}) collective-permute-start(bf16[256,256]{1,0:T(8,128)(2,1)S(1)} %up.9.current_ref), channel_id=1, source_target_pairs={{0,2},{1,3},{2,0},{3,1},{4,6},{5,7},{6,4},{7,5},{8,10},{9,11},{10,... | collective-permute-start | bytes 393224 | tf_op jit(solution)/shard_map/ppermute | solution.py:369
  80.4 4.0 %collective-permute-done.12.sibling_ref.refs_3_ = bf16[256,256]{1,0:T(8,128)(2,1)S(1)} collective-permute-done((bf16[256,256]{1,0:T(8,128)(2,1)S(1)}, bf16[256,256]{1,0:T(8,128)(2,1)S(1)}, u32[]{:S(2)}, u32[]{:S(2)}) %collective-permute-start.12) | collective-permute-done | bytes 131104 | tf_op jit(solution)/shard_map/ppermute | solution.py:369
  85.1 4.7 %collective-permute-done.13.sibling_ref.refs_4_ = bf16[256,256]{1,0:T(8,128)(2,1)S(1)} collective-permute-done((bf16[256,256]{1,0:T(8,128)(2,1)S(1)}, bf16[256,256]{1,0:T(8,128)(2,1)S(1)}, u32[]{:S(2)}, u32[]{:S(2)}) %collective-permute-start.13) | collective-permute-done | bytes 131104 | tf_op jit(solution)/shard_map/ppermute | solution.py:369
  90.0 1.8 %collective-permute-start.14 = (bf16[256,256]{1,0:T(8,128)(2,1)S(1)}, bf16[256,256]{1,0:T(8,128)(2,1)S(1)}, u32[]{:S(2)}, u32[]{:S(2)}) collective-permute-start(bf16[256,256]{1,0:T(8,128)(2,1)S(1)} %up.11), channel_id=1, source_target_pairs={{0,8},{1,9},{2,10},{3,11},{4,12},{5,13},{6,14},{7,15},{8,0},{9,1},... | collective-permute-start | bytes 393224 | tf_op jit(solution)/shard_map/ppermute | solution.py:369
  93.5 3.8 %collective-permute-done.14.refs_5_ = bf16[256,256]{1,0:T(8,128)(2,1)S(1)} collective-permute-done((bf16[256,256]{1,0:T(8,128)(2,1)S(1)}, bf16[256,256]{1,0:T(8,128)(2,1)S(1)}, u32[]{:S(2)}, u32[]{:S(2)}) %collective-permute-start.14) | collective-permute-done | bytes 131104 | tf_op jit(solution)/shard_map/ppermute | solution.py:369
  97.3 3.6 %down.3 = (f32[1024,256]{1,0:T(8,128)S(1)}, f32[272,256]{1,0:T(8,128)S(1)}, f32[272,256]{1,0:T(8,128)S(1)}) custom-call(s32[1]{0:T(128)} %bitcast.position_ref.refs_0_, f32[1024,256]{1,0:T(8,128)S(1)} %near.1.refs_1_, bf16[256,256]{1,0:T(8,128)(2,1)S(1)} %collective-permute-done.11.sibling_ref.refs_2_, ...), custom_call_target="tpu_custom_call" | custom-call | flops 1342177280 | bytes 5506052 | tf_op jit(solution)/shard_map/down/pallas_call | solution.py:354
  101.1 1.5 %collective-permute-done.15 = f32[272,256]{1,0:T(8,128)S(1)} collective-permute-done((f32[272,256]{1,0:T(8,128)S(1)}, f32[272,256]{1,0:T(8,128)S(1)}, u32[]{:S(2)}, u32[]{:S(2)}) %collective-permute-start.15) | collective-permute-done | bytes 278560 | tf_op jit(solution)/shard_map/ppermute | solution.py:369
  102.7 1.6 %collective-permute-start.16 = (f32[136,256]{1,0:T(8,128)S(1)}, f32[136,256]{1,0:T(8,128)S(1)}, u32[]{:S(2)}, u32[]{:S(2)}) collective-permute-start(f32[136,256]{1,0:T(8,128)S(1)} %slice.19), channel_id=1, source_target_pairs={{0,2},{1,3},{2,0},{3,1},{4,6},{5,7},{6,4},{7,5},{8,10},{9,11},{10,... | collective-permute-start | bytes 417800 | tf_op jit(solution)/shard_map/ppermute | solution.py:369
  104.3 4.2 %collective-permute-done.16 = f32[136,256]{1,0:T(8,128)S(1)} collective-permute-done((f32[136,256]{1,0:T(8,128)S(1)}, f32[136,256]{1,0:T(8,128)S(1)}, u32[]{:S(2)}, u32[]{:S(2)}) %collective-permute-start.16) | collective-permute-done | bytes 139296 | tf_op jit(solution)/shard_map/ppermute | solution.py:369
  108.6 5.0 %collective-permute-done.17 = f32[136,256]{1,0:T(8,128)S(1)} collective-permute-done((f32[136,256]{1,0:T(8,128)S(1)}, f32[136,256]{1,0:T(8,128)S(1)}, u32[]{:S(2)}, u32[]{:S(2)}) %collective-permute-start.17) | collective-permute-done | bytes 139296 | tf_op jit(solution)/shard_map/ppermute | solution.py:369
  113.6 1.6 %collective-permute-start.18 = (f32[136,256]{1,0:T(8,128)S(1)}, f32[136,256]{1,0:T(8,128)S(1)}, u32[]{:S(2)}, u32[]{:S(2)}) collective-permute-start(f32[136,256]{1,0:T(8,128)S(1)} %add.30), channel_id=1, source_target_pairs={{0,8},{1,9},{2,10},{3,11},{4,12},{5,13},{6,14},{7,15},{8,0},{9,1},... | collective-permute-start | bytes 417800 | tf_op jit(solution)/shard_map/ppermute | solution.py:369
  115.2 6.1 %collective-permute-done.18 = f32[136,256]{1,0:T(8,128)S(1)} collective-permute-done((f32[136,256]{1,0:T(8,128)S(1)}, f32[136,256]{1,0:T(8,128)S(1)}, u32[]{:S(2)}, u32[]{:S(2)}) %collective-permute-start.18) | collective-permute-done | bytes 139296 | tf_op jit(solution)/shard_map/ppermute | solution.py:369
  121.3 1.6 %collective-permute-start.19 = (f32[136,256]{1,0:T(8,128)S(1)}, f32[136,256]{1,0:T(8,128)S(1)}, u32[]{:S(2)}, u32[]{:S(2)}) collective-permute-start(f32[136,256]{1,0:T(8,128)S(1)} %add.31.refs_1_), channel_id=1, source_target_pairs={{0,2},{1,3},{2,0},{3,1},{4,6},{5,7},{6,4},{7,5},{8,10},{9,11},{10,... | collective-permute-start | bytes 417800 | tf_op jit(solution)/shard_map/ppermute | solution.py:369
  122.9 3.5 %collective-permute-done.19.refs_2_ = f32[136,256]{1,0:T(8,128)S(1)} collective-permute-done((f32[136,256]{1,0:T(8,128)S(1)}, f32[136,256]{1,0:T(8,128)S(1)}, u32[]{:S(2)}, u32[]{:S(2)}) %collective-permute-start.19) | collective-permute-done | bytes 139296 | tf_op jit(solution)/shard_map/ppermute | solution.py:369
  127.8 21.2 %solve.3 = (f32[1024,256]{1,0:T(8,128)}, f32[1024,256]{1,0:T(8,128)}, f32[1024,256]{1,0:T(8,128)}) custom-call(s32[1]{0:T(128)} %bitcast.position_ref.refs_0_, f32[136,256]{1,0:T(8,128)S(1)} %add.31.refs_1_, f32[136,256]{1,0:T(8,128)S(1)} %collective-permute-done.19.refs_2_, f32[136,256]{1,0:T(8,128)S(1)} %collective-permute-done.20.refs_3_, ...), custom_call_target="tpu_custom_call" | custom-call | flops 1342177280 | bytes 5013508 | tf_op jit(solution)/shard_map/solve/pallas_call | solution.py:354
  (61 shorter events, 14.8 us)
Async XLA Ops:
  0.6 5.3 %copy-start = (bf16[1,3,512,256]{3,2,1,0:T(8,128)(2,1)S(1)}, bf16[1,3,512,256]{3,2,1,0:T(8,128)(2,1)}, u32[]{:S(2)}) copy-start(bf16[1,3,512,256]{3,2,1,0:T(8,128)(2,1)} %refs_7_.5) | copy-start | bytes 2359300
  0.6 1.3 copy-start.1
  4.3 17.0 %copy-start.2 = (f32[1024,256]{1,0:T(8,128)S(1)}, f32[1024,256]{1,0:T(8,128)}, u32[]{:S(2)}) copy-start(f32[1024,256]{1,0:T(8,128)} %direction_ref.5) | copy-start | bytes 3145732
  4.4 17.0 %copy-start.10 = (f32[3,1024]{1,0:T(4,128)S(1)}, f32[3,1024]{1,0:T(4,128)}, u32[]{:S(2)}) copy-start(f32[3,1024]{1,0:T(4,128)} %points_ref.1) | copy-start | bytes 36868
  4.4 17.0 %copy-start.11 = (s32[1024]{0:T(1024)S(1)}, s32[1024]{0:T(1024)}, u32[]{:S(2)}) copy-start(s32[1024]{0:T(1024)} %param.10) | copy-start | bytes 12292
  4.4 1.5 %collective-permute-start = (bf16[256,256]{1,0:T(8,128)(2,1)S(1)}, bf16[256,256]{1,0:T(8,128)(2,1)S(1)}, u32[]{:S(2)}, u32[]{:S(2)}) collective-permute-start(bf16[256,256]{1,0:T(8,128)(2,1)S(1)} %coef.1.current_ref), channel_id=1, source_target_pairs={{0,1},{1,0},{2,3},{3,2},{4,5},{5,4},{6,7},{7,6},{8,9},{9,8},{10,11... | collective-permute-start | bytes 393224 | tf_op jit(solution)/shard_map/ppermute | solution.py:369
  6.2 6.7 %collective-permute-start.1 = (bf16[256,256]{1,0:T(8,128)(2,1)S(1)}, bf16[256,256]{1,0:T(8,128)(2,1)S(1)}, u32[]{:S(2)}, u32[]{:S(2)}) collective-permute-start(bf16[256,256]{1,0:T(8,128)(2,1)S(1)} %up.6.current_ref), channel_id=1, source_target_pairs={{0,2},{1,3},{2,0},{3,1},{4,6},{5,7},{6,4},{7,5},{8,10},{9,11},{10,... | collective-permute-start | bytes 393224 | tf_op jit(solution)/shard_map/ppermute | solution.py:369
  13.2 5.1 %collective-permute-start.2 = (bf16[256,256]{1,0:T(8,128)(2,1)S(1)}, bf16[256,256]{1,0:T(8,128)(2,1)S(1)}, u32[]{:S(2)}, u32[]{:S(2)}) collective-permute-start(bf16[256,256]{1,0:T(8,128)(2,1)S(1)} %up.7.current_ref), channel_id=1, source_target_pairs={{0,4},{1,5},{2,6},{3,7},{4,0},{5,1},{6,2},{7,3},{8,12},{9,13},{10,... | collective-permute-start | bytes 393224 | tf_op jit(solution)/shard_map/ppermute | solution.py:369
  18.6 7.9 %collective-permute-start.3 = (bf16[256,256]{1,0:T(8,128)(2,1)S(1)}, bf16[256,256]{1,0:T(8,128)(2,1)S(1)}, u32[]{:S(2)}, u32[]{:S(2)}) collective-permute-start(bf16[256,256]{1,0:T(8,128)(2,1)S(1)} %up.8), channel_id=1, source_target_pairs={{0,8},{1,9},{2,10},{3,11},{4,12},{5,13},{6,14},{7,15},{8,0},{9,1},... | collective-permute-start | bytes 393224 | tf_op jit(solution)/shard_map/ppermute | solution.py:369
  21.4 4.3 %copy-start.5 = (f32[1024,256]{1,0:T(8,128)S(1)}, f32[1024,256]{1,0:T(8,128)}, u32[]{:S(2)}) copy-start(f32[1024,256]{1,0:T(8,128)} %residual_ref.1) | copy-start | bytes 3145732
  21.4 5.1 %copy-start.9 = (s32[1,256]{1,0:T(1,128)S(1)}, s32[1,256]{1,0:T(1,128)}, u32[]{:S(2)}) copy-start(s32[1,256]{1,0:T(1,128)} %refs_9_.5) | copy-start | bytes 3076
  25.7 1.0 copy-start.4
  25.7 1.2 copy-start.6
  30.6 1.7 %collective-permute-start.4 = (f32[336,256]{1,0:T(8,128)S(1)}, f32[336,256]{1,0:T(8,128)S(1)}, u32[]{:S(2)}, u32[]{:S(2)}) collective-permute-start(f32[336,256]{1,0:T(8,128)S(1)} %get-tuple-element.20), channel_id=1, source_target_pairs={{0,1},{1,0},{2,3},{3,2},{4,5},{5,4},{6,7},{7,6},{8,9},{9,8},{10,11... | collective-permute-start | bytes 1032200 | tf_op jit(solution)/shard_map/ppermute | solution.py:369
  32.4 6.5 %collective-permute-start.5 = (f32[168,256]{1,0:T(8,128)S(1)}, f32[168,256]{1,0:T(8,128)S(1)}, u32[]{:S(2)}, u32[]{:S(2)}) collective-permute-start(f32[168,256]{1,0:T(8,128)S(1)} %slice.17), channel_id=1, source_target_pairs={{0,2},{1,3},{2,0},{3,1},{4,6},{5,7},{6,4},{7,5},{8,10},{9,11},{10,... | collective-permute-start | bytes 516104 | tf_op jit(solution)/shard_map/ppermute | solution.py:369
  38.9 5.7 %collective-permute-start.6 = (f32[168,256]{1,0:T(8,128)S(1)}, f32[168,256]{1,0:T(8,128)S(1)}, u32[]{:S(2)}, u32[]{:S(2)}) collective-permute-start(f32[168,256]{1,0:T(8,128)S(1)} %slice_add_fusion), channel_id=1, source_target_pairs={{0,4},{1,5},{2,6},{3,7},{4,0},{5,1},{6,2},{7,3},{8,12},{9,13},{10,... | collective-permute-start | bytes 516104 | tf_op jit(solution)/shard_map/ppermute | solution.py:369
  44.5 9.3 %collective-permute-start.7 = (f32[168,256]{1,0:T(8,128)S(1)}, f32[168,256]{1,0:T(8,128)S(1)}, u32[]{:S(2)}, u32[]{:S(2)}) collective-permute-start(f32[168,256]{1,0:T(8,128)S(1)} %add.26), channel_id=1, source_target_pairs={{0,8},{1,9},{2,10},{3,11},{4,12},{5,13},{6,14},{7,15},{8,0},{9,1},... | collective-permute-start | bytes 516104 | tf_op jit(solution)/shard_map/ppermute | solution.py:369
  53.9 5.5 %collective-permute-start.8 = (f32[168,256]{1,0:T(8,128)S(1)}, f32[168,256]{1,0:T(8,128)S(1)}, u32[]{:S(2)}, u32[]{:S(2)}) collective-permute-start(f32[168,256]{1,0:T(8,128)S(1)} %add.27.refs_1_), channel_id=1, source_target_pairs={{0,2},{1,3},{2,0},{3,1},{4,6},{5,7},{6,4},{7,5},{8,10},{9,11},{10,... | collective-permute-start | bytes 516104 | tf_op jit(solution)/shard_map/ppermute | solution.py:369
  55.5 3.9 %collective-permute-start.9 = (f32[168,256]{1,0:T(8,128)S(1)}, f32[168,256]{1,0:T(8,128)S(1)}, u32[]{:S(2)}, u32[]{:S(2)}) collective-permute-start(f32[168,256]{1,0:T(8,128)S(1)} %add.27.refs_1_), channel_id=1, source_target_pairs={{0,1},{1,0},{2,3},{3,2},{4,5},{5,4},{6,7},{7,6},{8,9},{9,8},{10,11... | collective-permute-start | bytes 516104 | tf_op jit(solution)/shard_map/ppermute | solution.py:369
  59.4 1.4 collective-permute-start.10
  77.1 14.7 %copy-start.7 = (f32[1024,256]{1,0:T(8,128)S(1)}, f32[1024,256]{1,0:T(8,128)}, u32[]{:S(2)}) copy-start(f32[1024,256]{1,0:T(8,128)} %solution_ref.1) | copy-start | bytes 3145732
  77.1 1.4 collective-permute-start.11
  78.8 5.6 %collective-permute-start.12 = (bf16[256,256]{1,0:T(8,128)(2,1)S(1)}, bf16[256,256]{1,0:T(8,128)(2,1)S(1)}, u32[]{:S(2)}, u32[]{:S(2)}) collective-permute-start(bf16[256,256]{1,0:T(8,128)(2,1)S(1)} %up.9.current_ref), channel_id=1, source_target_pairs={{0,2},{1,3},{2,0},{3,1},{4,6},{5,7},{6,4},{7,5},{8,10},{9,11},{10,... | collective-permute-start | bytes 393224 | tf_op jit(solution)/shard_map/ppermute | solution.py:369
  84.7 5.0 %collective-permute-start.13 = (bf16[256,256]{1,0:T(8,128)(2,1)S(1)}, bf16[256,256]{1,0:T(8,128)(2,1)S(1)}, u32[]{:S(2)}, u32[]{:S(2)}) collective-permute-start(bf16[256,256]{1,0:T(8,128)(2,1)S(1)} %up.10.current_ref), channel_id=1, source_target_pairs={{0,4},{1,5},{2,6},{3,7},{4,0},{5,1},{6,2},{7,3},{8,12},{9,13},{10,... | collective-permute-start | bytes 393224 | tf_op jit(solution)/shard_map/ppermute | solution.py:369
  90.0 7.3 %collective-permute-start.14 = (bf16[256,256]{1,0:T(8,128)(2,1)S(1)}, bf16[256,256]{1,0:T(8,128)(2,1)S(1)}, u32[]{:S(2)}, u32[]{:S(2)}) collective-permute-start(bf16[256,256]{1,0:T(8,128)(2,1)S(1)} %up.11), channel_id=1, source_target_pairs={{0,8},{1,9},{2,10},{3,11},{4,12},{5,13},{6,14},{7,15},{8,0},{9,1},... | collective-permute-start | bytes 393224 | tf_op jit(solution)/shard_map/ppermute | solution.py:369
  101.0 1.6 %collective-permute-start.15 = (f32[272,256]{1,0:T(8,128)S(1)}, f32[272,256]{1,0:T(8,128)S(1)}, u32[]{:S(2)}, u32[]{:S(2)}) collective-permute-start(f32[272,256]{1,0:T(8,128)S(1)} %get-tuple-element.27), channel_id=1, source_target_pairs={{0,1},{1,0},{2,3},{3,2},{4,5},{5,4},{6,7},{7,6},{8,9},{9,8},{10,11... | collective-permute-start | bytes 835592 | tf_op jit(solution)/shard_map/ppermute | solution.py:369
  102.7 5.8 %collective-permute-start.16 = (f32[136,256]{1,0:T(8,128)S(1)}, f32[136,256]{1,0:T(8,128)S(1)}, u32[]{:S(2)}, u32[]{:S(2)}) collective-permute-start(f32[136,256]{1,0:T(8,128)S(1)} %slice.19), channel_id=1, source_target_pairs={{0,2},{1,3},{2,0},{3,1},{4,6},{5,7},{6,4},{7,5},{8,10},{9,11},{10,... | collective-permute-start | bytes 417800 | tf_op jit(solution)/shard_map/ppermute | solution.py:369
  108.5 5.1 %collective-permute-start.17 = (f32[136,256]{1,0:T(8,128)S(1)}, f32[136,256]{1,0:T(8,128)S(1)}, u32[]{:S(2)}, u32[]{:S(2)}) collective-permute-start(f32[136,256]{1,0:T(8,128)S(1)} %slice_add_fusion.1), channel_id=1, source_target_pairs={{0,4},{1,5},{2,6},{3,7},{4,0},{5,1},{6,2},{7,3},{8,12},{9,13},{10,... | collective-permute-start | bytes 417800 | tf_op jit(solution)/shard_map/ppermute | solution.py:369
  113.6 7.7 %collective-permute-start.18 = (f32[136,256]{1,0:T(8,128)S(1)}, f32[136,256]{1,0:T(8,128)S(1)}, u32[]{:S(2)}, u32[]{:S(2)}) collective-permute-start(f32[136,256]{1,0:T(8,128)S(1)} %add.30), channel_id=1, source_target_pairs={{0,8},{1,9},{2,10},{3,11},{4,12},{5,13},{6,14},{7,15},{8,0},{9,1},... | collective-permute-start | bytes 417800 | tf_op jit(solution)/shard_map/ppermute | solution.py:369
  121.3 5.1 %collective-permute-start.19 = (f32[136,256]{1,0:T(8,128)S(1)}, f32[136,256]{1,0:T(8,128)S(1)}, u32[]{:S(2)}, u32[]{:S(2)}) collective-permute-start(f32[136,256]{1,0:T(8,128)S(1)} %add.31.refs_1_), channel_id=1, source_target_pairs={{0,2},{1,3},{2,0},{3,1},{4,6},{5,7},{6,4},{7,5},{8,10},{9,11},{10,... | collective-permute-start | bytes 417800 | tf_op jit(solution)/shard_map/ppermute | solution.py:369
  122.9 3.5 %collective-permute-start.20 = (f32[136,256]{1,0:T(8,128)S(1)}, f32[136,256]{1,0:T(8,128)S(1)}, u32[]{:S(2)}, u32[]{:S(2)}) collective-permute-start(f32[136,256]{1,0:T(8,128)S(1)} %add.31.refs_1_), channel_id=1, source_target_pairs={{0,1},{1,0},{2,3},{3,2},{4,5},{5,4},{6,7},{7,6},{8,9},{9,8},{10,11... | collective-permute-start | bytes 417800 | tf_op jit(solution)/shard_map/ppermute | solution.py:369
  126.5 1.4 collective-permute-start.21
  (2 other events, 1.7 us)

commit v2 on v1

v2 whole, which is shorter than its diff:
```python
import functools

import jax
import jax.numpy as jnp
from jax import lax
from jax.experimental import pallas as pl
from jax.experimental.pallas import tpu as pltpu
from jax.sharding import PartitionSpec as P

ITERS = 2
F32 = jnp.float32
BF16 = jnp.bfloat16
VMEM = pl.BlockSpec(memory_space=pltpu.VMEM)
SMEM = pl.BlockSpec(memory_space=pltpu.SMEM)
ANY = pl.BlockSpec(memory_space=pl.ANY)
MAX_STEPS = 60
BOUND = 1e-5


def dot(left, right):
    return jnp.dot(left, right, preferred_element_type=F32)


def dot_t(left, right):
    return lax.dot_general(left, right, (((0,), (0,)), ((), ())), preferred_element_type=F32)


def split(value):
    high = value.astype(BF16)
    return high, (value - high.astype(F32)).astype(BF16)


def dot3(left, right):
    lh, ll = split(left)
    rh, rl = split(right)
    return dot(lh, rh) + (dot(lh, rl) + dot(ll, rh))


def dot_full(left, right):
    return jnp.dot(left, right, precision=lax.Precision.HIGHEST, preferred_element_type=F32)


def iotas(rows, columns):
    return (
        lax.broadcasted_iota(jnp.int32, (rows, columns), 0),
        lax.broadcasted_iota(jnp.int32, (rows, columns), 1),
    )


def eye_mask(size):
    row, column = iotas(size, size)
    return row == column


def skeleton_columns(skel_ref, count):
    row, _ = iotas(count, skel_ref.shape[1])
    return jnp.where(row == skel_ref[...], 1.0, 0.0).astype(BF16)


def skeleton_rows(skel_ref, count):
    rank = skel_ref.shape[1]
    wide = jnp.broadcast_to(skel_ref[...].astype(F32), (128, rank)).T
    column = lax.broadcasted_iota(jnp.int32, (rank, 128), 1).astype(F32)
    tiles = [
        jnp.where(wide == column + float(start), 1.0, 0.0).astype(BF16)
        for start in range(0, count, 128)
    ]
    return jnp.concatenate(tiles, 1)


def leaf_coefficients(vector, basis_ref, skel_ref):
    high, low = split(vector)
    picks = skeleton_rows(skel_ref, vector.shape[0])
    coef = dot_t(basis_ref[...], high) + (dot(picks, high) + dot(picks, low))
    return coef.astype(BF16)


def coef_kernel(direction_ref, basis_ref, skel_ref, coef_ref):
    coef_ref[...] = leaf_coefficients(direction_ref[...], basis_ref, skel_ref)


def block_kernel(points_ref, order_ref, after_ref, block_ref, padded, column_ref):
    count = points_ref.shape[1]
    padded[...] = jnp.zeros_like(padded)
    padded[0:3, :] = points_ref[...]
    raw = padded[...]
    high = raw.astype(BF16).astype(F32)
    middle = (raw - high).astype(BF16).astype(F32)
    low = raw - high - middle
    parts = jnp.concatenate([high, middle, low], 0).astype(BF16)
    row, _ = iotas(count, count)
    picks = jnp.where(row == order_ref[...], 1.0, 0.0).astype(BF16)
    ordered = dot(parts, picks)
    ordered = (ordered[0:8] + ordered[8:16] + ordered[16:24]) * (300.0**0.5)
    column_ref[...] = jnp.concatenate([ordered, jnp.zeros((120, count), F32)], 0).T
    strip = 128

    def step(index, carry):
        start = pl.multiple_of(index * strip, strip)
        mine = column_ref[pl.ds(start, strip), :]
        square = 1e-10
        for axis in range(3):
            gap = mine[:, axis : axis + 1] - ordered[axis : axis + 1, :]
            square = gap * gap + square
        scaled = square * lax.rsqrt(square)
        values = ((1.0 + scaled) * jnp.exp(-scaled)).astype(BF16)
        block_ref[pl.ds(start, strip), :] = values
        return carry

    lax.fori_loop(0, count // strip, step, 0)

def near_kernel(block_ref, direction_ref, near_ref):
    low_direction = direction_ref[...].astype(BF16)
    near_ref[...] = dot(block_ref[...], low_direction) + 2.0 * low_direction.astype(F32)


def turned_splits(value, high_ref, low_ref, start):
    size = value.shape[1]
    high, low = split(value)
    high_ref[start : start + size, :] = high.T
    low_ref[start : start + size, :] = low.T
    return high, low


def prepare_kernel(direction_ref, residual_ref, high_ref, low_ref, gram_ref):
    size = direction_ref.shape[1]
    turned_splits(direction_ref[...], high_ref, low_ref, 0)
    high, low = turned_splits(residual_ref[...], high_ref, low_ref, size)
    both = dot(high_ref[size:, :], jnp.concatenate([high, low], 1))
    cross = both[:, size:]
    gram_ref[...] = both[:, :size] + (cross + cross.T)


def up_kernel(level, position_ref, current_ref, sibling_ref, transfer_ref, *rest):
    coef_ref = rest[-1]
    rank = current_ref.shape[0]
    right = (position_ref[0] >> level) & 1
    mine = transfer_ref[0, level, pl.ds(pl.multiple_of(right * rank, rank), rank), :]
    other = transfer_ref[0, level, pl.ds(pl.multiple_of((1 - right) * rank, rank), rank), :]
    coef_ref[...] = (
        dot_t(mine, current_ref[...]) + dot_t(other, sibling_ref[...])
    ).astype(BF16)


def pack_pair(first, second):
    size = first.shape[0]
    row, column = iotas(size, size)
    diagonal = jnp.sum(jnp.where(row == column, second, 0.0), axis=0, keepdims=True)
    return jnp.where(row >= column, first, second), diagonal


def unpack_pair(packed, diagonal):
    size = packed.shape[0]
    row, column = iotas(size, size)
    turned = packed.T
    first = jnp.where(row >= column, packed, turned)
    second = jnp.where(row < column, packed, turned)
    return first, jnp.where(row == column, diagonal, second)


def pack_half(matrix):
    half = matrix.shape[0] // 2
    corner, tail = pack_pair(matrix[:half, :half], matrix[half:, half:])
    return jnp.concatenate([matrix[half:, :half], corner], 1), jnp.concatenate([tail, tail], 1)


def unpack_half(packed, tail):
    half = packed.shape[0]
    upper, lower = unpack_pair(packed[:, half:], tail[:, :half])
    corner = packed[:, :half]
    return jnp.concatenate(
        [jnp.concatenate([upper, corner.T], 1), jnp.concatenate([corner, lower], 1)], 0
    )


def payload_rows(size, with_start):
    rows = size + size // 2 + 8 + (size if with_start else 0)
    return -(-rows // 32) * 32


def sides(position):
    core = position & 1
    return core, (position >> (1 + core)) & 1, (position >> (2 - core)) & 1


def down_kernel(levels, with_start, *refs):
    position_ref, near_ref = refs[0], refs[1]
    siblings = refs[2 : 2 + levels]
    coupling_ref, transfer_ref, basis_ref, skel_ref, high_ref, low_ref = refs[
        2 + levels : 8 + levels
    ]
    rest = list(refs[8 + levels :])
    start_ref = rest.pop(0)
    image_ref, keep_ref, send_ref, payload = rest
    rank = basis_ref.shape[1]
    count, size = near_ref.shape
    position = position_ref[0]
    down = dot(coupling_ref[0, levels - 1], siblings[levels - 1][...])
    for level in reversed(range(levels - 1)):
        right = (position >> level) & 1
        half = transfer_ref[0, level, pl.ds(pl.multiple_of(right * rank, rank), rank), :]
        high, low = split(down)
        down = dot(coupling_ref[0, level], siblings[level][...]) + (dot(half, high) + dot(half, low))
    high, low = split(down)
    places = skeleton_columns(skel_ref, count)
    image = near_ref[...] + dot(basis_ref[...], high) + (dot(places, high) + dot(places, low))
    image_ref[...] = image
    image_high, image_low = split(image)
    both = jnp.concatenate([image_high, image_low], 1)
    wide = dot(high_ref[...], both)
    grams = wide[:, :size] + (wide[:, size:] + dot(low_ref[...], image_high))
    wide = dot_t(image_high, both)
    cross = wide[:, size:]
    images = wide[:, :size] + (cross + cross.T)
    packed, tail = pack_half(images)
    base = 0
    if with_start:
        curvature = grams[:size]
        pair, diagonal = pack_pair(0.5 * (curvature + curvature.T), start_ref[...])
        payload[0:size, :] = pair
        base = size
    else:
        diagonal = tail
    payload[base : base + size, :] = grams[base:]
    base += size
    payload[base : base + size // 2, :] = packed
    base += size // 2
    payload[base:, :] = jnp.zeros((payload.shape[0] - base, size), F32)
    payload[base : base + 1, :] = tail
    payload[base + 1 : base + 2, :] = diagonal
    quarter = payload.shape[0] // 4
    core, side, _ = sides(position)

    def part(core_at, side_at):
        start = pl.multiple_of((core_at * 2 + side_at) * quarter, 8)
        return payload[pl.ds(start, quarter), :]

    keep_ref[0:quarter, :] = part(core, side)
    keep_ref[quarter:, :] = part(core, 1 - side)
    send_ref[0:quarter, :] = part(1 - core, sides(position ^ 1)[1])
    send_ref[quarter:, :] = part(1 - core, 1 - sides(position ^ 1)[1])


def scaled_problem(matrix):
    size = matrix.shape[0]
    eye = eye_mask(size)
    picked = jnp.where(eye, matrix, 0.0)
    row_scale = lax.rsqrt(jnp.sum(picked, axis=0, keepdims=True))
    column_scale = lax.rsqrt(jnp.sum(picked, axis=1, keepdims=True))
    scaled = matrix * column_scale * row_scale
    widest = jnp.max(jnp.sum(jnp.abs(scaled), axis=0, keepdims=True), axis=1, keepdims=True)
    return scaled, column_scale, 1.8 / widest


def inverses(matrices, store, errors):
    count = len(matrices)
    size = matrices[0].shape[0]
    eye = jnp.where(eye_mask(size), 1.0, 0.0)
    problems = [scaled_problem(matrix) for matrix in matrices]
    starts = [eye * gain for _, _, gain in problems]
    slopes = [eye - scaled * gain for scaled, _, gain in problems]
    guesses = [start + slope * gain for start, slope, (_, _, gain) in zip(starts, slopes, problems)]
    gaps = list(slopes)
    for _ in range(4):
        for at in range(count):
            rough = gaps[at].astype(BF16)
            gaps[at] = dot(rough, rough)
        for at in range(count):
            guesses[at] = guesses[at] + dot(guesses[at].astype(BF16), gaps[at].astype(BF16))
    total = 0.0
    for at in range(count):
        scaled = problems[at][0]
        gap = eye - dot3(scaled, guesses[at])
        near = jnp.sum(jnp.sum(gap * gap, axis=0, keepdims=True), axis=1, keepdims=True) < 0.5
        guess = jnp.where(near, guesses[at], starts[at])
        gap = jnp.where(near, gap, slopes[at])
        guess = guess + dot3(guess, gap)
        gap = eye - dot_full(scaled, guess)
        store[at], errors[at] = guess, gap
        total = total + jnp.sum(gap * gap)

    def unfinished(carry):
        step, total = carry
        return (step < MAX_STEPS) & (total > BOUND)

    def refine(carry):
        step, _ = carry
        total = 0.0
        for at in range(count):
            guess = store[at] + dot3(store[at], errors[at])
            gap = eye - dot_full(problems[at][0], guess)
            store[at], errors[at] = guess, gap
            total = total + jnp.sum(gap * gap)
        return step + 1, total

    lax.while_loop(unfinished, refine, (0, total))
    results = []
    for at in range(count):
        guess = store[at]
        results.append(guess + dot(guess.astype(BF16), errors[at].astype(BF16)))
    return [(result, problem[1]) for result, problem in zip(results, problems)]


def collect(position, own_ref, side_ref, core_ref, far_ref, payload):
    quarter = payload.shape[0] // 4
    core, side, _ = sides(position)
    other = sides(position ^ 1)[1]
    for ref, core_at, side_at in (
        (own_ref, core, side),
        (side_ref, core, 1 - side),
        (core_ref, 1 - core, other),
        (far_ref, 1 - core, 1 - other),
    ):
        start = pl.multiple_of((core_at * 2 + side_at) * quarter, 8)
        payload[pl.ds(start, quarter), :] = ref[...]


def fresh_gram(res_gram, mixed, images, alpha):
    bend = dot3(alpha.T, dot3(images, alpha))
    change = 0.5 * bend - dot3(mixed, alpha)
    return res_gram + (change + change.T)


def first_kernel(
    position_ref,
    own_ref,
    side_ref,
    core_ref,
    far_ref,
    image_ref,
    residual_ref,
    direction_ref,
    basis_ref,
    skel_ref,
    direction_out,
    coef_out,
    alpha_out,
    beta_out,
    fresh_out,
    mixed_out,
    images_out,
    curvature_out,
    payload,
    store,
    errors,
):
    size = direction_ref.shape[1]
    collect(position_ref[0], own_ref, side_ref, core_ref, far_ref, payload)
    mixed = payload[size : 2 * size, :]
    base = 2 * size + size // 2
    images = unpack_half(payload[2 * size : base, :], payload[base : base + 1, :])
    curvature, res_gram = unpack_pair(payload[0:size, :], payload[base + 1 : base + 2, :])
    (first, first_scale), (second, second_scale) = inverses([curvature, res_gram], store, errors)
    alpha = dot3(first, res_gram * first_scale) * first_scale
    fresh = fresh_gram(res_gram, mixed, images, alpha)
    beta = dot3(second, fresh * second_scale) * second_scale
    moved = residual_ref[...] - dot3(image_ref[...], alpha) + dot3(direction_ref[...], beta)
    direction_out[...] = moved
    coef_out[...] = leaf_coefficients(moved, basis_ref, skel_ref)
    alpha_out[...] = alpha
    beta_out[...] = beta
    fresh_out[...] = fresh
    mixed_out[...] = mixed
    images_out[...] = images
    curvature_out[...] = curvature


def carry_kernel(
    alpha_ref,
    beta_ref,
    fresh_ref,
    mixed_ref,
    images_ref,
    curvature_ref,
    inverse_out,
    turn_out,
    store,
    errors,
):
    beta = beta_ref[...]
    ((inverse, scale),) = inverses([fresh_ref[...]], store, errors)
    inverse_out[...] = inverse * scale
    across = mixed_ref[...].T - dot3(images_ref[...], alpha_ref[...])
    across = across + dot3(curvature_ref[...], beta)
    turn = dot3(beta.T, across)
    turn_out[...] = 0.5 * (turn + turn.T)


def update_kernel(
    image_ref,
    residual_ref,
    direction_ref,
    solution_ref,
    alpha_ref,
    residual_out,
    solution_out,
    high_out,
    low_out,
):
    alpha = alpha_ref[...]
    residual = residual_ref[...] - dot3(image_ref[...], alpha)
    residual_out[...] = residual
    turned_splits(residual, high_out, low_out, 0)
    solution_out[...] = solution_ref[...] + dot3(direction_ref[...], alpha)


def last_kernel(
    position_ref,
    own_ref,
    side_ref,
    core_ref,
    far_ref,
    image_ref,
    residual_ref,
    direction_ref,
    solution_ref,
    fresh_ref,
    inverse_ref,
    turn_ref,
    solution_out,
    residual_out,
    direction_out,
    payload,
    store,
    errors,
    solution_held,
    residual_held,
    direction_held,
    sems,
):
    count, size = direction_ref.shape
    collect(position_ref[0], own_ref, side_ref, core_ref, far_ref, payload)
    mixed = payload[0:size, :]
    base = size + size // 2
    images = unpack_half(payload[size:base, :], payload[base : base + 1, :])
    res_gram = fresh_ref[...]
    curvature = 0.5 * (mixed + mixed.T) + turn_ref[...]
    ((first, scale),) = inverses([curvature], store, errors)
    alpha = dot3(first, res_gram * scale) * scale
    residual = residual_ref[...] - dot3(image_ref[...], alpha)
    residual_held[...] = residual
    copies = [pltpu.make_async_copy(residual_held, residual_out, sems.at[0])]
    copies[0].start()
    solution_held[...] = solution_ref[...] + dot3(direction_ref[...], alpha)
    copies.append(pltpu.make_async_copy(solution_held, solution_out, sems.at[1]))
    copies[1].start()
    fresh = fresh_gram(res_gram, mixed, images, alpha)
    picked = jnp.where(eye_mask(size), res_gram, 0.0)
    column_scale = lax.rsqrt(jnp.sum(picked, axis=1, keepdims=True))
    beta = dot3(inverse_ref[...], fresh * column_scale)
    strip = count // 4
    for at in range(4):
        rows = pl.ds(at * strip, strip)
        direction_held[rows, :] = residual_held[rows, :] + dot3(direction_ref[rows, :], beta)
        copy = pltpu.make_async_copy(
            direction_held.at[rows, :], direction_out.at[rows, :], sems.at[2 + at]
        )
        copy.start()
        copies.append(copy)
    for copy in copies:
        copy.wait()


def call(kernel, name, inputs, outputs, scratch=(), flops=0, limit=32, unused=0, apart=False):
    specs = [SMEM if value.dtype == jnp.int32 and value.shape == (1,) else VMEM for value in inputs]
    specs[len(specs) - unused :] = [ANY] * unused
    size = sum(value.size * value.dtype.itemsize for value in inputs)
    return pl.pallas_call(
        kernel,
        name=name,
        in_specs=specs,
        out_specs=[ANY if apart else VMEM] * len(outputs),
        out_shape=[jax.ShapeDtypeStruct(shape, dtype) for shape, dtype in outputs],
        scratch_shapes=list(scratch),
        cost_estimate=pl.CostEstimate(flops=flops, bytes_accessed=size, transcendentals=0),
        compiler_params=pltpu.CompilerParams(vmem_limit_bytes=limit * 2**20),
    )(*inputs)


def swapped(value, distance, other=None):
    masks = (2**distance, 2 ** (distance if other is None else other))
    pairs = [(source, source ^ masks[source & 1]) for source in range(lax.axis_size("leaf"))]
    return lax.ppermute(value, "leaf", pairs)


def summed(keep, send, levels):
    quarter = keep.shape[0] // 2
    half = keep + swapped(send, 0)
    own = half[:quarter] + swapped(half[quarter:], 1, 2)
    own = own + swapped(own, 2, 1)
    for level in range(3, levels):
        own = own + swapped(own, level)
    side = swapped(own, 1, 2)
    return [own, side, swapped(own, 0), swapped(side, 0)]


def body(points, leaf_order, skeleton, basis, transfer, coupling, solution, residual, direction):
    levels = lax.axis_size("leaf").bit_length() - 1
    count, size = direction.shape
    rank = basis.shape[1]
    position = lax.axis_index("leaf").astype(jnp.int32).reshape(1)
    order = leaf_order.reshape(1, count)
    tall = ((count, size), F32)
    square = ((size, size), F32)
    coef = ((rank, size), BF16)
    product = 2 * count * size * size
    work = pltpu.VMEM((2, size, size), F32)

    (current,) = call(
        coef_kernel, "coef", [direction, basis, skeleton], [coef], flops=product, limit=60
    )
    for step in range(ITERS):
        first = step == 0
        siblings = []
        for level in range(levels):
            sibling = swapped(current, level)
            siblings.append(sibling)
            if level == levels - 1:
                break
            extra = []
            if first and level == 1:
                (block,) = call(
                    block_kernel,
                    "block",
                    [points, order, current],
                    [((count, count), BF16)],
                    [pltpu.VMEM((8, count), F32), pltpu.VMEM((count, 128), F32)],
                    flops=20 * product,
                    unused=1,
                )
                extra = [block]
            (current,) = call(
                functools.partial(up_kernel, level),
                "up",
                [position, current, sibling, transfer] + extra,
                [coef],
                flops=product,
                unused=len(extra),
            )
        (near,) = call(near_kernel, "near", [block, direction], [tall], flops=8 * product)
        if first:
            high, low, gram = call(
                prepare_kernel,
                "prepare",
                [direction, residual],
                [((2 * size, count), BF16), ((2 * size, count), BF16), square],
                flops=8 * product,
            )
        rows = payload_rows(size, first)
        image, keep, send = call(
            functools.partial(down_kernel, levels, first),
            "down",
            [position, near, *siblings, coupling, transfer, basis, skeleton, high, low]
            + ([gram] if first else [inverse]),
            [tall, ((rows // 2, size), F32), ((rows // 2, size), F32)],
            [pltpu.VMEM((rows, size), F32)],
            flops=10 * product,
            unused=0 if first else 1,
        )
        pieces = [position] + summed(keep, send, levels)
        scratch = [pltpu.VMEM((rows, size), F32), work, work]
        if first:
            moved, current, alpha, beta, fresh, mixed, images, curvature = call(
                first_kernel,
                "first",
                pieces + [image, residual, direction, basis, skeleton],
                [tall, coef] + [square] * 6,
                scratch,
                flops=10 * product,
            )
            inverse, turn = call(
                carry_kernel,
                "carry",
                [alpha, beta, fresh, mixed, images, curvature],
                [square, square],
                [work, work],
                flops=8 * product,
            )
            residual, solution, high, low = call(
                update_kernel,
                "update",
                [image, residual, direction, solution, alpha],
                [tall, tall, ((size, count), BF16), ((size, count), BF16)],
                flops=6 * product,
            )
            direction = moved
    tall_work = pltpu.VMEM((count, size), F32)
    return tuple(
        call(
            last_kernel,
            "last",
            pieces + [image, residual, direction, solution, fresh, inverse, turn],
            [tall, tall, tall],
            scratch + [tall_work] * 3 + [pltpu.SemaphoreType.DMA((6,))],
            flops=10 * product,
            apart=True,
        )
    )


def solution(mesh):
    placed = (
        P(None, ("groups", "leaf")),
        P(("groups", "leaf")),
        P(("groups", "leaf"), None),
        P(("groups", "leaf"), None),
        P(("groups", "leaf"), None, None, None),
        P(("groups", "leaf"), None, None, None),
        P(("groups", "leaf"), None),
        P(("groups", "leaf"), None),
        P(("groups", "leaf"), None),
    )
    return jax.shard_map(
        body,
        mesh=mesh,
        in_specs=placed,
        out_specs=(
            P(("groups", "leaf"), None),
            P(("groups", "leaf"), None),
            P(("groups", "leaf"), None),
        ),
        check_vma=False,
    )
```

time: 149 us -> 152 us (1.020)
  Pallas kernels: 53.7 us -> 69 us
  waiting for transfers between devices: 67.3 us -> 58.6 us
  local copies, waits for them, and re-layouts: 3.49 us -> 0.98 us
    pallas_call x15 -> x17, Pallas kernels: 53.7 us -> 69 us  [call(): pl.pallas_call(kernel, name=name, in_specs=specs, out_specs=[ANY if apart...]
    ppermute x22, waiting for transfers between devices: 67.3 us -> 58.6 us  [swapped(): return lax.ppermute(value, 'leaf', pairs)]
    unnamed x24 -> x20, local copies, waits for them, and re-layouts: 3.47 us -> 0.95 us
  transfers between devices with their start and end apart: 22 -> 22, of which waited for: 20 -> 19; matrix products, arithmetic and copies ran while one was open for 0% -> 0% of each run, Pallas kernels for 4% -> 15%
where the time goes in v2:
time: 152 us
  Pallas kernels  69 us (45%)
  waiting for transfers between devices  58.6 us (39%)
  starting transfers between devices  22 us (14%)
    pallas_call x17, Pallas kernels, call(): pl.pallas_call(kernel, name=name, in_specs=specs, out_specs=[ANY if apart...  69 us
    ppermute x22, waiting for transfers between devices, swapped(): return lax.ppermute(value, 'leaf', pairs)  58.6 us
    ppermute x22, starting transfers between devices, swapped(): return lax.ppermute(value, 'leaf', pairs)  22 us
  transfers between devices with their start and end apart: 22, of which 19 were waited for; matrix products, arithmetic and copies ran while one was open for 0% of the time, Pallas kernels for 15%

profile of v2, /device:TPU:0, one launch (start us, length us, event | category | flops | bytes accessed | tf_op | source)
XLA Modules:
  0.0 151.8 jit_solution(4463776955894097575)
XLA Ops:
  0.7 2.8 %coef.1.current_ref = bf16[256,256]{1,0:T(8,128)(2,1)} custom-call(f32[1024,256]{1,0:T(8,128)} %direction_ref.9, bf16[1024,256]{1,0:T(8,128)(2,1)} %refs_8_.3, s32[1,256]{1,0:T(1,128)} %refs_9_.3), custom_call_target="tpu_custom_call" | custom-call | flops 134217728 | bytes 1573888 | tf_op jit(solution)/shard_map/coef/pallas_call | solution.py:468
  6.3 2.9 %collective-permute-start.1 = (bf16[256,256]{1,0:T(8,128)(2,1)S(1)}, bf16[256,256]{1,0:T(8,128)(2,1)S(1)}, u32[]{:S(2)}, u32[]{:S(2)}) collective-permute-start(bf16[256,256]{1,0:T(8,128)(2,1)S(1)} %up.6.after_ref.current_ref), channel_id=1, source_target_pairs={{0,2},{1,3},{2,0},{3,1},{4,6},{5,7},{6,4},{7,5},{8,10},{9,11},{10,... | collective-permute-start | bytes 393224 | tf_op jit(solution)/shard_map/ppermute | solution.py:483
  9.2 3.6 %block.1.block_ref.rest_0_ = bf16[1024,1024]{1,0:T(8,128)(2,1)S(1)} custom-call(f32[3,1024]{1,0:T(4,128)S(1)} %copy-done.8, s32[1,1024]{1,0:T(1,128)S(1)} %bitcast.2, bf16[256,256]{1,0:T(8,128)(2,1)S(1)} %up.6.after_ref.current_ref), custom_call_target="tpu_custom_call" | custom-call | flops 2684354560 | bytes 147456 | tf_op jit(solution)/shard_map/block/pallas_call | solution.py:468
  13.3 1.9 %collective-permute-start.2 = (bf16[256,256]{1,0:T(8,128)(2,1)S(1)}, bf16[256,256]{1,0:T(8,128)(2,1)S(1)}, u32[]{:S(2)}, u32[]{:S(2)}) collective-permute-start(bf16[256,256]{1,0:T(8,128)(2,1)S(1)} %up.7.current_ref), channel_id=1, source_target_pairs={{0,4},{1,5},{2,6},{3,7},{4,0},{5,1},{6,2},{7,3},{8,12},{9,13},{10,... | collective-permute-start | bytes 393224 | tf_op jit(solution)/shard_map/ppermute | solution.py:483
  15.2 3.3 %collective-permute-done.2.sibling_ref.refs_4_ = bf16[256,256]{1,0:T(8,128)(2,1)S(1)} collective-permute-done((bf16[256,256]{1,0:T(8,128)(2,1)S(1)}, bf16[256,256]{1,0:T(8,128)(2,1)S(1)}, u32[]{:S(2)}, u32[]{:S(2)}) %collective-permute-start.2) | collective-permute-done | bytes 131104 | tf_op jit(solution)/shard_map/ppermute | solution.py:483
  18.7 2.8 %collective-permute-start.3 = (bf16[256,256]{1,0:T(8,128)(2,1)S(1)}, bf16[256,256]{1,0:T(8,128)(2,1)S(1)}, u32[]{:S(2)}, u32[]{:S(2)}) collective-permute-start(bf16[256,256]{1,0:T(8,128)(2,1)S(1)} %up.8), channel_id=1, source_target_pairs={{0,8},{1,9},{2,10},{3,11},{4,12},{5,13},{6,14},{7,15},{8,0},{9,1},... | collective-permute-start | bytes 393224 | tf_op jit(solution)/shard_map/ppermute | solution.py:483
  23.0 3.7 %collective-permute-done.3.refs_5_ = bf16[256,256]{1,0:T(8,128)(2,1)S(1)} collective-permute-done((bf16[256,256]{1,0:T(8,128)(2,1)S(1)}, bf16[256,256]{1,0:T(8,128)(2,1)S(1)}, u32[]{:S(2)}, u32[]{:S(2)}) %collective-permute-start.3) | collective-permute-done | bytes 131104 | tf_op jit(solution)/shard_map/ppermute | solution.py:483
  26.7 3.6 %down.2 = (f32[1024,256]{1,0:T(8,128)S(1)}, f32[336,256]{1,0:T(8,128)S(1)}, f32[336,256]{1,0:T(8,128)S(1)}) custom-call(s32[1]{0:T(128)} %bitcast.position_ref.refs_0_, f32[1024,256]{1,0:T(8,128)S(1)} %near.2.refs_1_, bf16[256,256]{1,0:T(8,128)(2,1)S(1)} %collective-permute-done.sibling_ref.refs_2_, ...), custom_call_target="tpu_custom_call" | custom-call | flops 1342177280 | bytes 5768196 | tf_op jit(solution)/shard_map/down/pallas_call | solution.py:468
  30.4 1.6 %collective-permute-done.4 = f32[336,256]{1,0:T(8,128)S(1)} collective-permute-done((f32[336,256]{1,0:T(8,128)S(1)}, f32[336,256]{1,0:T(8,128)S(1)}, u32[]{:S(2)}, u32[]{:S(2)}) %collective-permute-start.4) | collective-permute-done | bytes 344096 | tf_op jit(solution)/shard_map/ppermute | solution.py:483
  33.2 4.4 %collective-permute-done.5 = f32[168,256]{1,0:T(8,128)S(1)} collective-permute-done((f32[168,256]{1,0:T(8,128)S(1)}, f32[168,256]{1,0:T(8,128)S(1)}, u32[]{:S(2)}, u32[]{:S(2)}) %collective-permute-start.5) | collective-permute-done | bytes 172064 | tf_op jit(solution)/shard_map/ppermute | solution.py:483
  38.0 5.1 %collective-permute-done.6 = f32[168,256]{1,0:T(8,128)S(1)} collective-permute-done((f32[168,256]{1,0:T(8,128)S(1)}, f32[168,256]{1,0:T(8,128)S(1)}, u32[]{:S(2)}, u32[]{:S(2)}) %collective-permute-start.6) | collective-permute-done | bytes 172064 | tf_op jit(solution)/shard_map/ppermute | solution.py:483
  43.1 1.7 %collective-permute-start.7 = (f32[168,256]{1,0:T(8,128)S(1)}, f32[168,256]{1,0:T(8,128)S(1)}, u32[]{:S(2)}, u32[]{:S(2)}) collective-permute-start(f32[168,256]{1,0:T(8,128)S(1)} %add.26), channel_id=1, source_target_pairs={{0,8},{1,9},{2,10},{3,11},{4,12},{5,13},{6,14},{7,15},{8,0},{9,1},... | collective-permute-start | bytes 516104 | tf_op jit(solution)/shard_map/ppermute | solution.py:483
  44.9 7.6 %collective-permute-done.7 = f32[168,256]{1,0:T(8,128)S(1)} collective-permute-done((f32[168,256]{1,0:T(8,128)S(1)}, f32[168,256]{1,0:T(8,128)S(1)}, u32[]{:S(2)}, u32[]{:S(2)}) %collective-permute-start.7) | collective-permute-done | bytes 172064 | tf_op jit(solution)/shard_map/ppermute | solution.py:483
  53.6 4.4 %collective-permute-done.8.side_ref = f32[168,256]{1,0:T(8,128)S(1)} collective-permute-done((f32[168,256]{1,0:T(8,128)S(1)}, f32[168,256]{1,0:T(8,128)S(1)}, u32[]{:S(2)}, u32[]{:S(2)}) %collective-permute-start.8) | collective-permute-done | bytes 172064 | tf_op jit(solution)/shard_map/ppermute | solution.py:483
  58.0 1.4 collective-permute-done.10.far_ref
  59.4 16.2 %first.1 = (f32[1024,256]{1,0:T(8,128)S(1)}, bf16[256,256]{1,0:T(8,128)(2,1)S(1)}, f32[256,256]{1,0:T(8,128)S(1)}, f32[256,256]{1,0:T(8,128)S(1)}, f32[256,256]{...) custom-call(s32[1]{0:T(128)} %bitcast.position_ref.refs_0_, ...), custom_call_target="tpu_custom_call" | custom-call | flops 1342177280 | bytes 4359172 | tf_op jit(solution)/shard_map/first/pallas_call | solution.py:468
  75.8 1.2 collective-permute-done.11.sibling_ref.refs_2_
  78.4 4.5 %collective-permute-done.12.sibling_ref.refs_3_ = bf16[256,256]{1,0:T(8,128)(2,1)S(1)} collective-permute-done((bf16[256,256]{1,0:T(8,128)(2,1)S(1)}, bf16[256,256]{1,0:T(8,128)(2,1)S(1)}, u32[]{:S(2)}, u32[]{:S(2)}) %collective-permute-start.12) | collective-permute-done | bytes 131104 | tf_op jit(solution)/shard_map/ppermute | solution.py:483
  84.0 4.2 %collective-permute-done.13.sibling_ref.refs_4_ = bf16[256,256]{1,0:T(8,128)(2,1)S(1)} collective-permute-done((bf16[256,256]{1,0:T(8,128)(2,1)S(1)}, bf16[256,256]{1,0:T(8,128)(2,1)S(1)}, u32[]{:S(2)}, u32[]{:S(2)}) %collective-permute-start.13) | collective-permute-done | bytes 131104 | tf_op jit(solution)/shard_map/ppermute | solution.py:483
  90.8 15.7 %carry.1 = (f32[256,256]{1,0:T(8,128)S(1)}, f32[256,256]{1,0:T(8,128)S(1)}) custom-call(f32[256,256]{1,0:T(8,128)S(1)} %get-tuple-element.34.alpha_ref, f32[256,256]{1,0:T(8,128)S(1)} %get-tuple-element.37.beta_ref, f32[256,256]{1,0:T(8,128)S(1)} %get-tuple-element.38.fresh_ref, f32[256,256]{1,0:T(8,128)S(1)} %get-tuple-element.39.mixed_ref, ...), custom_call_target="tpu_custom_call" | custom-call | flops 1073741824 | bytes 1572864 | tf_op jit(solution)/shard_map/carry/pallas_call | solution.py:468
  106.6 3.2 %down.3 = (f32[1024,256]{1,0:T(8,128)S(1)}, f32[208,256]{1,0:T(8,128)S(1)}, f32[208,256]{1,0:T(8,128)S(1)}) custom-call(s32[1]{0:T(128)} %bitcast.position_ref.refs_0_, f32[1024,256]{1,0:T(8,128)S(1)} %near.3.refs_1_, bf16[256,256]{1,0:T(8,128)(2,1)S(1)} %collective-permute-done.11.sibling_ref.refs_2_, ...), custom_call_target="tpu_custom_call" | custom-call | flops 1342177280 | bytes 4719620 | tf_op jit(solution)/shard_map/down/pallas_call | solution.py:468
  109.8 1.5 collective-permute-done.15
  111.3 1.5 %collective-permute-start.16 = (f32[104,256]{1,0:T(8,128)S(1)}, f32[104,256]{1,0:T(8,128)S(1)}, u32[]{:S(2)}, u32[]{:S(2)}) collective-permute-start(f32[104,256]{1,0:T(8,128)S(1)} %slice.19), channel_id=1, source_target_pairs={{0,2},{1,5},{2,0},{3,7},{4,6},{5,1},{6,4},{7,3},{8,10},{9,13},{10,... | collective-permute-start | bytes 319496 | tf_op jit(solution)/shard_map/ppermute | solution.py:483
  112.9 3.2 %collective-permute-done.16 = f32[104,256]{1,0:T(8,128)S(1)} collective-permute-done((f32[104,256]{1,0:T(8,128)S(1)}, f32[104,256]{1,0:T(8,128)S(1)}, u32[]{:S(2)}, u32[]{:S(2)}) %collective-permute-start.16) | collective-permute-done | bytes 106528 | tf_op jit(solution)/shard_map/ppermute | solution.py:483
  116.1 2.0 %collective-permute-start.17 = (f32[104,256]{1,0:T(8,128)S(1)}, f32[104,256]{1,0:T(8,128)S(1)}, u32[]{:S(2)}, u32[]{:S(2)}) collective-permute-start(f32[104,256]{1,0:T(8,128)S(1)} %slice_add_fusion.1), channel_id=1, source_target_pairs={{0,4},{1,3},{2,6},{3,1},{4,0},{5,7},{6,2},{7,5},{8,12},{9,11},{10,... | collective-permute-start | bytes 319496 | tf_op jit(solution)/shard_map/ppermute | solution.py:483
  118.2 2.7 %collective-permute-done.17 = f32[104,256]{1,0:T(8,128)S(1)} collective-permute-done((f32[104,256]{1,0:T(8,128)S(1)}, f32[104,256]{1,0:T(8,128)S(1)}, u32[]{:S(2)}, u32[]{:S(2)}) %collective-permute-start.17) | collective-permute-done | bytes 106528 | tf_op jit(solution)/shard_map/ppermute | solution.py:483
  120.9 1.8 %collective-permute-start.18 = (f32[104,256]{1,0:T(8,128)S(1)}, f32[104,256]{1,0:T(8,128)S(1)}, u32[]{:S(2)}, u32[]{:S(2)}) collective-permute-start(f32[104,256]{1,0:T(8,128)S(1)} %add.30), channel_id=1, source_target_pairs={{0,8},{1,9},{2,10},{3,11},{4,12},{5,13},{6,14},{7,15},{8,0},{9,1},... | collective-permute-start | bytes 319496 | tf_op jit(solution)/shard_map/ppermute | solution.py:483
  122.8 3.8 %collective-permute-done.18 = f32[104,256]{1,0:T(8,128)S(1)} collective-permute-done((f32[104,256]{1,0:T(8,128)S(1)}, f32[104,256]{1,0:T(8,128)S(1)}, u32[]{:S(2)}, u32[]{:S(2)}) %collective-permute-start.18) | collective-permute-done | bytes 106528 | tf_op jit(solution)/shard_map/ppermute | solution.py:483
  126.6 1.5 %collective-permute-start.19 = (f32[104,256]{1,0:T(8,128)S(1)}, f32[104,256]{1,0:T(8,128)S(1)}, u32[]{:S(2)}, u32[]{:S(2)}) collective-permute-start(f32[104,256]{1,0:T(8,128)S(1)} %add.31.own_ref), channel_id=1, source_target_pairs={{0,2},{1,5},{2,0},{3,7},{4,6},{5,1},{6,4},{7,3},{8,10},{9,13},{10,... | collective-permute-start | bytes 319496 | tf_op jit(solution)/shard_map/ppermute | solution.py:483
  128.2 3.2 %collective-permute-done.19.side_ref = f32[104,256]{1,0:T(8,128)S(1)} collective-permute-done((f32[104,256]{1,0:T(8,128)S(1)}, f32[104,256]{1,0:T(8,128)S(1)}, u32[]{:S(2)}, u32[]{:S(2)}) %collective-permute-start.19) | collective-permute-done | bytes 106528 | tf_op jit(solution)/shard_map/ppermute | solution.py:483
  131.4 1.3 collective-permute-done.21.far_ref
  132.7 18.9 %last.1 = (f32[1024,256]{1,0:T(8,128)}, f32[1024,256]{1,0:T(8,128)}, f32[1024,256]{1,0:T(8,128)}) custom-call(s32[1]{0:T(128)} %bitcast.position_ref.refs_0_, f32[104,256]{1,0:T(8,128)S(1)} %add.31.own_ref, f32[104,256]{1,0:T(8,128)S(1)} %collective-permute-done.19.side_ref, f32[104,256]{1,0:T(8,128)S(1)} %collective-permute-done.20.core_ref, ...), custom_call_target="tpu_custom_call" | custom-call | flops 1342177280 | bytes 5406724 | tf_op jit(solution)/shard_map/last/pallas_call | solution.py:468
  (59 shorter events, 13.2 us)
Async XLA Ops:
  0.6 4.5 %copy-start = (bf16[1,3,512,256]{3,2,1,0:T(8,128)(2,1)S(1)}, bf16[1,3,512,256]{3,2,1,0:T(8,128)(2,1)}, u32[]{:S(2)}) copy-start(bf16[1,3,512,256]{3,2,1,0:T(8,128)(2,1)} %refs_7_.3) | copy-start | bytes 2359300
  0.6 8.6 %copy-start.9 = (s32[1024]{0:T(1024)S(1)}, s32[1024]{0:T(1024)}, u32[]{:S(2)}) copy-start(s32[1024]{0:T(1024)} %param.10) | copy-start | bytes 12292
  0.7 8.6 %copy-start.8 = (f32[3,1024]{1,0:T(4,128)S(1)}, f32[3,1024]{1,0:T(4,128)}, u32[]{:S(2)}) copy-start(f32[3,1024]{1,0:T(4,128)} %points_ref.1) | copy-start | bytes 36868
  3.5 1.7 %collective-permute-start = (bf16[256,256]{1,0:T(8,128)(2,1)}, bf16[256,256]{1,0:T(8,128)(2,1)S(1)}, u32[]{:S(2)}, u32[]{:S(2)}) collective-permute-start(bf16[256,256]{1,0:T(8,128)(2,1)} %coef.1.current_ref), channel_id=1, source_target_pairs={{0,1},{1,0},{2,3},{3,2},{4,5},{5,4},{6,7},{7,6},{8,9},{9,8},{10,11... | collective-permute-start | bytes 393224 | tf_op jit(solution)/shard_map/ppermute | solution.py:483
  5.1 0.9 copy-start.6
  6.3 6.7 %collective-permute-start.1 = (bf16[256,256]{1,0:T(8,128)(2,1)S(1)}, bf16[256,256]{1,0:T(8,128)(2,1)S(1)}, u32[]{:S(2)}, u32[]{:S(2)}) collective-permute-start(bf16[256,256]{1,0:T(8,128)(2,1)S(1)} %up.6.after_ref.current_ref), channel_id=1, source_target_pairs={{0,2},{1,3},{2,0},{3,1},{4,6},{5,7},{6,4},{7,5},{8,10},{9,11},{10,... | collective-permute-start | bytes 393224 | tf_op jit(solution)/shard_map/ppermute | solution.py:483
  12.8 8.7 %copy-start.1 = (f32[1024,256]{1,0:T(8,128)S(1)}, f32[1024,256]{1,0:T(8,128)}, u32[]{:S(2)}) copy-start(f32[1024,256]{1,0:T(8,128)} %direction_ref.9) | copy-start | bytes 3145732
  12.8 8.7 %copy-start.3 = (f32[1024,256]{1,0:T(8,128)S(1)}, f32[1024,256]{1,0:T(8,128)}, u32[]{:S(2)}) copy-start(f32[1024,256]{1,0:T(8,128)} %residual_ref.5) | copy-start | bytes 3145732
  13.3 5.1 %collective-permute-start.2 = (bf16[256,256]{1,0:T(8,128)(2,1)S(1)}, bf16[256,256]{1,0:T(8,128)(2,1)S(1)}, u32[]{:S(2)}, u32[]{:S(2)}) collective-permute-start(bf16[256,256]{1,0:T(8,128)(2,1)S(1)} %up.7.current_ref), channel_id=1, source_target_pairs={{0,4},{1,5},{2,6},{3,7},{4,0},{5,1},{6,2},{7,3},{8,12},{9,13},{10,... | collective-permute-start | bytes 393224 | tf_op jit(solution)/shard_map/ppermute | solution.py:483
  18.7 8.0 %collective-permute-start.3 = (bf16[256,256]{1,0:T(8,128)(2,1)S(1)}, bf16[256,256]{1,0:T(8,128)(2,1)S(1)}, u32[]{:S(2)}, u32[]{:S(2)}) collective-permute-start(bf16[256,256]{1,0:T(8,128)(2,1)S(1)} %up.8), channel_id=1, source_target_pairs={{0,8},{1,9},{2,10},{3,11},{4,12},{5,13},{6,14},{7,15},{8,0},{9,1},... | collective-permute-start | bytes 393224 | tf_op jit(solution)/shard_map/ppermute | solution.py:483
  22.3 4.4 %copy-start.2 = (bf16[1024,256]{1,0:T(8,128)(2,1)S(1)}, bf16[1024,256]{1,0:T(8,128)(2,1)}, u32[]{:S(2)}) copy-start(bf16[1024,256]{1,0:T(8,128)(2,1)} %refs_8_.3) | copy-start | bytes 1572868
  22.3 4.4 %copy-start.5 = (bf16[1,4,256,256]{3,2,1,0:T(8,128)(2,1)S(1)}, bf16[1,4,256,256]{3,2,1,0:T(8,128)(2,1)}, u32[]{:S(2)}) copy-start(bf16[1,4,256,256]{3,2,1,0:T(8,128)(2,1)} %refs_6_.3) | copy-start | bytes 1572868
  22.3 4.4 %copy-start.7 = (s32[1,256]{1,0:T(1,128)S(1)}, s32[1,256]{1,0:T(1,128)}, u32[]{:S(2)}) copy-start(s32[1,256]{1,0:T(1,128)} %refs_9_.3) | copy-start | bytes 3076
  30.3 1.7 %collective-permute-start.4 = (f32[336,256]{1,0:T(8,128)S(1)}, f32[336,256]{1,0:T(8,128)S(1)}, u32[]{:S(2)}, u32[]{:S(2)}) collective-permute-start(f32[336,256]{1,0:T(8,128)S(1)} %get-tuple-element.30), channel_id=1, source_target_pairs={{0,1},{1,0},{2,3},{3,2},{4,5},{5,4},{6,7},{7,6},{8,9},{9,8},{10,11... | collective-permute-start | bytes 1032200 | tf_op jit(solution)/shard_map/ppermute | solution.py:483
  32.1 5.5 %collective-permute-start.5 = (f32[168,256]{1,0:T(8,128)S(1)}, f32[168,256]{1,0:T(8,128)S(1)}, u32[]{:S(2)}, u32[]{:S(2)}) collective-permute-start(f32[168,256]{1,0:T(8,128)S(1)} %slice.17), channel_id=1, source_target_pairs={{0,2},{1,5},{2,0},{3,7},{4,6},{5,1},{6,4},{7,3},{8,10},{9,13},{10,... | collective-permute-start | bytes 516104 | tf_op jit(solution)/shard_map/ppermute | solution.py:483
  37.6 5.5 %collective-permute-start.6 = (f32[168,256]{1,0:T(8,128)S(1)}, f32[168,256]{1,0:T(8,128)S(1)}, u32[]{:S(2)}, u32[]{:S(2)}) collective-permute-start(f32[168,256]{1,0:T(8,128)S(1)} %slice_add_fusion), channel_id=1, source_target_pairs={{0,4},{1,3},{2,6},{3,1},{4,0},{5,7},{6,2},{7,5},{8,12},{9,11},{10,... | collective-permute-start | bytes 516104 | tf_op jit(solution)/shard_map/ppermute | solution.py:483
  43.1 9.4 %collective-permute-start.7 = (f32[168,256]{1,0:T(8,128)S(1)}, f32[168,256]{1,0:T(8,128)S(1)}, u32[]{:S(2)}, u32[]{:S(2)}) collective-permute-start(f32[168,256]{1,0:T(8,128)S(1)} %add.26), channel_id=1, source_target_pairs={{0,8},{1,9},{2,10},{3,11},{4,12},{5,13},{6,14},{7,15},{8,0},{9,1},... | collective-permute-start | bytes 516104 | tf_op jit(solution)/shard_map/ppermute | solution.py:483
  52.5 5.5 %collective-permute-start.8 = (f32[168,256]{1,0:T(8,128)S(1)}, f32[168,256]{1,0:T(8,128)S(1)}, u32[]{:S(2)}, u32[]{:S(2)}) collective-permute-start(f32[168,256]{1,0:T(8,128)S(1)} %add.27.own_ref), channel_id=1, source_target_pairs={{0,2},{1,5},{2,0},{3,7},{4,6},{5,1},{6,4},{7,3},{8,10},{9,13},{10,... | collective-permute-start | bytes 516104 | tf_op jit(solution)/shard_map/ppermute | solution.py:483
  53.6 4.4 %collective-permute-start.9 = (f32[168,256]{1,0:T(8,128)S(1)}, f32[168,256]{1,0:T(8,128)S(1)}, u32[]{:S(2)}, u32[]{:S(2)}) collective-permute-start(f32[168,256]{1,0:T(8,128)S(1)} %add.27.own_ref), channel_id=1, source_target_pairs={{0,1},{1,0},{2,3},{3,2},{4,5},{5,4},{6,7},{7,6},{8,9},{9,8},{10,11... | collective-permute-start | bytes 516104 | tf_op jit(solution)/shard_map/ppermute | solution.py:483
  58.0 1.4 collective-permute-start.10
  75.6 1.4 collective-permute-start.11
  77.3 5.6 %collective-permute-start.12 = (bf16[256,256]{1,0:T(8,128)(2,1)S(1)}, bf16[256,256]{1,0:T(8,128)(2,1)S(1)}, u32[]{:S(2)}, u32[]{:S(2)}) collective-permute-start(bf16[256,256]{1,0:T(8,128)(2,1)S(1)} %up.9.current_ref), channel_id=1, source_target_pairs={{0,2},{1,3},{2,0},{3,1},{4,6},{5,7},{6,4},{7,5},{8,10},{9,11},{10,... | collective-permute-start | bytes 393224 | tf_op jit(solution)/shard_map/ppermute | solution.py:483
  83.2 5.0 %collective-permute-start.13 = (bf16[256,256]{1,0:T(8,128)(2,1)S(1)}, bf16[256,256]{1,0:T(8,128)(2,1)S(1)}, u32[]{:S(2)}, u32[]{:S(2)}) collective-permute-start(bf16[256,256]{1,0:T(8,128)(2,1)S(1)} %up.10.current_ref), channel_id=1, source_target_pairs={{0,4},{1,5},{2,6},{3,7},{4,0},{5,1},{6,2},{7,3},{8,12},{9,13},{10,... | collective-permute-start | bytes 393224 | tf_op jit(solution)/shard_map/ppermute | solution.py:483
  83.3 6.4 %copy-start.4 = (f32[1024,256]{1,0:T(8,128)S(1)}, f32[1024,256]{1,0:T(8,128)}, u32[]{:S(2)}) copy-start(f32[1024,256]{1,0:T(8,128)} %solution_ref.1) | copy-start | bytes 3145732
  88.5 18.0 %collective-permute-start.14 = (bf16[256,256]{1,0:T(8,128)(2,1)S(1)}, bf16[256,256]{1,0:T(8,128)(2,1)S(1)}, u32[]{:S(2)}, u32[]{:S(2)}) collective-permute-start(bf16[256,256]{1,0:T(8,128)(2,1)S(1)} %up.11), channel_id=1, source_target_pairs={{0,8},{1,9},{2,10},{3,11},{4,12},{5,13},{6,14},{7,15},{8,0},{9,1},... | collective-permute-start | bytes 393224 | tf_op jit(solution)/shard_map/ppermute | solution.py:483
  109.8 1.5 %collective-permute-start.15 = (f32[208,256]{1,0:T(8,128)S(1)}, f32[208,256]{1,0:T(8,128)S(1)}, u32[]{:S(2)}, u32[]{:S(2)}) collective-permute-start(f32[208,256]{1,0:T(8,128)S(1)} %get-tuple-element.44), channel_id=1, source_target_pairs={{0,1},{1,0},{2,3},{3,2},{4,5},{5,4},{6,7},{7,6},{8,9},{9,8},{10,11... | collective-permute-start | bytes 638984 | tf_op jit(solution)/shard_map/ppermute | solution.py:483
  111.3 4.8 %collective-permute-start.16 = (f32[104,256]{1,0:T(8,128)S(1)}, f32[104,256]{1,0:T(8,128)S(1)}, u32[]{:S(2)}, u32[]{:S(2)}) collective-permute-start(f32[104,256]{1,0:T(8,128)S(1)} %slice.19), channel_id=1, source_target_pairs={{0,2},{1,5},{2,0},{3,7},{4,6},{5,1},{6,4},{7,3},{8,10},{9,13},{10,... | collective-permute-start | bytes 319496 | tf_op jit(solution)/shard_map/ppermute | solution.py:483
  116.1 4.8 %collective-permute-start.17 = (f32[104,256]{1,0:T(8,128)S(1)}, f32[104,256]{1,0:T(8,128)S(1)}, u32[]{:S(2)}, u32[]{:S(2)}) collective-permute-start(f32[104,256]{1,0:T(8,128)S(1)} %slice_add_fusion.1), channel_id=1, source_target_pairs={{0,4},{1,3},{2,6},{3,1},{4,0},{5,7},{6,2},{7,5},{8,12},{9,11},{10,... | collective-permute-start | bytes 319496 | tf_op jit(solution)/shard_map/ppermute | solution.py:483
  120.9 5.7 %collective-permute-start.18 = (f32[104,256]{1,0:T(8,128)S(1)}, f32[104,256]{1,0:T(8,128)S(1)}, u32[]{:S(2)}, u32[]{:S(2)}) collective-permute-start(f32[104,256]{1,0:T(8,128)S(1)} %add.30), channel_id=1, source_target_pairs={{0,8},{1,9},{2,10},{3,11},{4,12},{5,13},{6,14},{7,15},{8,0},{9,1},... | collective-permute-start | bytes 319496 | tf_op jit(solution)/shard_map/ppermute | solution.py:483
  126.6 4.8 %collective-permute-start.19 = (f32[104,256]{1,0:T(8,128)S(1)}, f32[104,256]{1,0:T(8,128)S(1)}, u32[]{:S(2)}, u32[]{:S(2)}) collective-permute-start(f32[104,256]{1,0:T(8,128)S(1)} %add.31.own_ref), channel_id=1, source_target_pairs={{0,2},{1,5},{2,0},{3,7},{4,6},{5,1},{6,4},{7,3},{8,10},{9,13},{10,... | collective-permute-start | bytes 319496 | tf_op jit(solution)/shard_map/ppermute | solution.py:483
  128.2 3.2 %collective-permute-start.20 = (f32[104,256]{1,0:T(8,128)S(1)}, f32[104,256]{1,0:T(8,128)S(1)}, u32[]{:S(2)}, u32[]{:S(2)}) collective-permute-start(f32[104,256]{1,0:T(8,128)S(1)} %add.31.own_ref), channel_id=1, source_target_pairs={{0,1},{1,0},{2,3},{3,2},{4,5},{5,4},{6,7},{7,6},{8,9},{9,8},{10,11... | collective-permute-start | bytes 319496 | tf_op jit(solution)/shard_map/ppermute | solution.py:483
  131.4 1.3 collective-permute-start.21

commit v3 on v2

--- a/solution.py
+++ b/solution.py
@@ -7,7 +7,6 @@
 from jax.experimental.pallas import tpu as pltpu
 from jax.sharding import PartitionSpec as P
 
-ITERS = 2
 F32 = jnp.float32
 BF16 = jnp.bfloat16
 VMEM = pl.BlockSpec(memory_space=pltpu.VMEM)
@@ -183,25 +182,49 @@
     return core, (position >> (1 + core)) & 1, (position >> (2 - core)) & 1
 
 
-def down_kernel(levels, with_start, *refs):
-    position_ref, near_ref = refs[0], refs[1]
-    siblings = refs[2 : 2 + levels]
-    coupling_ref, transfer_ref, basis_ref, skel_ref, high_ref, low_ref = refs[
-        2 + levels : 8 + levels
-    ]
-    rest = list(refs[8 + levels :])
-    start_ref = rest.pop(0)
-    image_ref, keep_ref, send_ref, payload = rest
-    rank = basis_ref.shape[1]
-    count, size = near_ref.shape
-    position = position_ref[0]
-    down = dot(coupling_ref[0, levels - 1], siblings[levels - 1][...])
+def write_parts(position, blocks, rows, payload, keep_ref, send_ref):
+    base = 0
+    for block in blocks:
+        payload[base : base + block.shape[0], :] = block
+        base += block.shape[0]
+    payload[base:, :] = jnp.zeros((payload.shape[0] - base, payload.shape[1]), F32)
+    for at, row in enumerate(rows):
+        payload[base + at : base + at + 1, :] = row
+    quarter = payload.shape[0] // 4
+    core, side, _ = sides(position)
+    other = sides(position ^ 1)[1]
+
+    def part(core_at, side_at):
+        start = pl.multiple_of((core_at * 2 + side_at) * quarter, 8)
+        return payload[pl.ds(start, quarter), :]
+
+    keep_ref[0:quarter, :] = part(core, side)
+    keep_ref[quarter:, :] = part(core, 1 - side)
+    send_ref[0:quarter, :] = part(1 - core, other)
+    send_ref[quarter:, :] = part(1 - core, 1 - other)
+
+
+def down_chain(position, levels, coupling_ref, transfer_ref, siblings):
+    rank = coupling_ref.shape[2]
+    down = dot(coupling_ref[0, levels - 1], siblings[levels - 1])
     for level in reversed(range(levels - 1)):
         right = (position >> level) & 1
         half = transfer_ref[0, level, pl.ds(pl.multiple_of(right * rank, rank), rank), :]
         high, low = split(down)
-        down = dot(coupling_ref[0, level], siblings[level][...]) + (dot(half, high) + dot(half, low))
-    high, low = split(down)
+        down = dot(coupling_ref[0, level], siblings[level]) + (dot(half, high) + dot(half, low))
+    return split(down)
+
+
+def down_kernel(levels, *refs):
+    position_ref, near_ref = refs[0], refs[1]
+    siblings = [ref[...] for ref in refs[2 : 2 + levels]]
+    coupling_ref, transfer_ref, basis_ref, skel_ref, high_ref, low_ref, gram_ref = refs[
+        2 + levels : 9 + levels
+    ]
+    image_ref, keep_ref, send_ref, payload = refs[9 + levels :]
+    count, size = near_ref.shape
+    position = position_ref[0]
+    high, low = down_chain(position, levels, coupling_ref, transfer_ref, siblings)
     places = skeleton_columns(skel_ref, count)
     image = near_ref[...] + dot(basis_ref[...], high) + (dot(places, high) + dot(places, low))
     image_ref[...] = image
@@ -211,34 +234,53 @@
     grams = wide[:, :size] + (wide[:, size:] + dot(low_ref[...], image_high))
     wide = dot_t(image_high, both)
     cross = wide[:, size:]
-    images = wide[:, :size] + (cross + cross.T)
-    packed, tail = pack_half(images)
-    base = 0
-    if with_start:
-        curvature = grams[:size]
-        pair, diagonal = pack_pair(0.5 * (curvature + curvature.T), start_ref[...])
-        payload[0:size, :] = pair
-        base = size
-    else:
-        diagonal = tail
-    payload[base : base + size, :] = grams[base:]
-    base += size
-    payload[base : base + size // 2, :] = packed
-    base += size // 2
-    payload[base:, :] = jnp.zeros((payload.shape[0] - base, size), F32)
-    payload[base : base + 1, :] = tail
-    payload[base + 1 : base + 2, :] = diagonal
-    quarter = payload.shape[0] // 4
-    core, side, _ = sides(position)
-
-    def part(core_at, side_at):
-        start = pl.multiple_of((core_at * 2 + side_at) * quarter, 8)
-        return payload[pl.ds(start, quarter), :]
-
-    keep_ref[0:quarter, :] = part(core, side)
-    keep_ref[quarter:, :] = part(core, 1 - side)
-    send_ref[0:quarter, :] = part(1 - core, sides(position ^ 1)[1])
-    send_ref[quarter:, :] = part(1 - core, 1 - sides(position ^ 1)[1])
+    packed, tail = pack_half(wide[:, :size] + (cross + cross.T))
+    curvature = grams[:size]
+    pair, diagonal = pack_pair(0.5 * (curvature + curvature.T), gram_ref[...])
+    write_parts(
+        position, [pair, grams[size:], packed], [tail, diagonal], payload, keep_ref, send_ref
+    )
+
+
+def pair_coef_kernel(image_ref, residual_ref, basis_ref, skel_ref, pair_ref):
+    count, size = image_ref.shape
+    picks = skeleton_rows(skel_ref, count)
+    parts = jnp.concatenate([*split(image_ref[...]), *split(residual_ref[...])], 1)
+    coef = dot_t(basis_ref[...], parts) + dot(picks, parts)
+    pair_ref[0] = (coef[:, :size] + coef[:, size : 2 * size]).astype(BF16)
+    pair_ref[1] = (coef[:, 2 * size : 3 * size] + coef[:, 3 * size :]).astype(BF16)
+
+
+def pair_up_kernel(position_ref, pair_ref, sibling_ref, transfer_ref, coef_ref):
+    core = position_ref[0] & 1
+    up_kernel(0, position_ref, pair_ref.at[core], sibling_ref.at[core], transfer_ref, coef_ref)
+
+
+def pair_near_kernel(block_ref, image_ref, residual_ref, near_ref):
+    block = block_ref[...]
+    for at, ref in enumerate((image_ref, residual_ref)):
+        value = ref[...]
+        high, low = split(value)
+        near_ref[at] = 2.0 * value + (dot(block, high) + dot(block, low))
+
+
+def pair_down_kernel(levels, *refs):
+    position_ref, near_ref, pair_ref = refs[:3]
+    own_refs, other_refs = refs[3 : 2 + levels], refs[2 + levels : 1 + 2 * levels]
+    coupling_ref, transfer_ref, basis_ref, skel_ref, applied_ref = refs[1 + 2 * levels :]
+    _, count, size = near_ref.shape
+    position = position_ref[0]
+    core = position & 1
+    siblings = [jnp.concatenate([pair_ref[core], pair_ref[1 - core]], 1)]
+    for own_ref, other_ref in zip(own_refs, other_refs):
+        siblings.append(jnp.concatenate([own_ref[...], other_ref[...]], 1))
+    high, low = down_chain(position, levels, coupling_ref, transfer_ref, siblings)
+    places = skeleton_columns(skel_ref, count)
+    spread = (dot(basis_ref[...], high) + dot(basis_ref[...], low)) + (
+        dot(places, high) + dot(places, low)
+    )
+    applied_ref[core] = near_ref[core] + spread[:, :size]
+    applied_ref[1 - core] = near_ref[1 - core] + spread[:, size:]
 
 
 def scaled_problem(matrix):
@@ -329,11 +371,11 @@
     far_ref,
     image_ref,
     residual_ref,
-    direction_ref,
-    basis_ref,
-    skel_ref,
-    direction_out,
-    coef_out,
+    applied_ref,
+    image_out,
+    residual_out,
+    keep_out,
+    send_out,
     alpha_out,
     beta_out,
     fresh_out,
@@ -341,11 +383,13 @@
     images_out,
     curvature_out,
     payload,
+    later,
     store,
     errors,
 ):
-    size = direction_ref.shape[1]
-    collect(position_ref[0], own_ref, side_ref, core_ref, far_ref, payload)
+    size = image_ref.shape[1]
+    position = position_ref[0]
+    collect(position, own_ref, side_ref, core_ref, far_ref, payload)
     mixed = payload[size : 2 * size, :]
     base = 2 * size + size // 2
     images = unpack_half(payload[2 * size : base, :], payload[base : base + 1, :])
@@ -354,9 +398,20 @@
     alpha = dot3(first, res_gram * first_scale) * first_scale
     fresh = fresh_gram(res_gram, mixed, images, alpha)
     beta = dot3(second, fresh * second_scale) * second_scale
-    moved = residual_ref[...] - dot3(image_ref[...], alpha) + dot3(direction_ref[...], beta)
-    direction_out[...] = moved
-    coef_out[...] = leaf_coefficients(moved, basis_ref, skel_ref)
+    old_image = image_ref[...]
+    residual = residual_ref[...] - dot3(old_image, alpha)
+    image = (applied_ref[1] - dot3(applied_ref[0], alpha)) + dot3(old_image, beta)
+    residual_out[...] = residual
+    image_out[...] = image
+    high, low = split(image)
+    both = jnp.concatenate([high, low], 1)
+    residual_high, residual_low = split(residual)
+    wide = dot_t(residual_high, both)
+    cross_gram = wide[:, :size] + (wide[:, size:] + dot_t(residual_low, high))
+    wide = dot_t(high, both)
+    cross = wide[:, size:]
+    packed, tail = pack_half(wide[:, :size] + (cross + cross.T))
+    write_parts(position, [cross_gram, packed], [tail], later, keep_out, send_out)
     alpha_out[...] = alpha
     beta_out[...] = beta
     fresh_out[...] = fresh
@@ -387,21 +442,11 @@
 
 
 def update_kernel(
-    image_ref,
-    residual_ref,
-    direction_ref,
-    solution_ref,
-    alpha_ref,
-    residual_out,
-    solution_out,
-    high_out,
-    low_out,
+    residual_ref, direction_ref, solution_ref, alpha_ref, beta_ref, direction_out, solution_out
 ):
-    alpha = alpha_ref[...]
-    residual = residual_ref[...] - dot3(image_ref[...], alpha)
-    residual_out[...] = residual
-    turned_splits(residual, high_out, low_out, 0)
-    solution_out[...] = solution_ref[...] + dot3(direction_ref[...], alpha)
+    direction = direction_ref[...]
+    direction_out[...] = residual_ref[...] + dot3(direction, beta_ref[...])
+    solution_out[...] = solution_ref[...] + dot3(direction, alpha_ref[...])
 
 
 def last_kernel(
@@ -461,10 +506,9 @@
         copy.wait()
 
 
-def call(kernel, name, inputs, outputs, scratch=(), flops=0, limit=32, unused=0, apart=False):
+def call(kernel, name, inputs, outputs, scratch=(), micros=1.0, limit=32, unused=0, apart=False):
     specs = [SMEM if value.dtype == jnp.int32 and value.shape == (1,) else VMEM for value in inputs]
     specs[len(specs) - unused :] = [ANY] * unused
-    size = sum(value.size * value.dtype.itemsize for value in inputs)
     return pl.pallas_call(
         kernel,
         name=name,
@@ -472,7 +516,9 @@
         out_specs=[ANY if apart else VMEM] * len(outputs),
         out_shape=[jax.ShapeDtypeStruct(shape, dtype) for shape, dtype in outputs],
         scratch_shapes=list(scratch),
-        cost_estimate=pl.CostEstimate(flops=flops, bytes_accessed=size, transcendentals=0),
+        cost_estimate=pl.CostEstimate(
+            flops=int(micros * 1.1e9), bytes_accessed=0, transcendentals=0
+        ),
         compiler_params=pltpu.CompilerParams(vmem_limit_bytes=limit * 2**20),
     )(*inputs)
 
@@ -483,13 +529,24 @@
     return lax.ppermute(value, "leaf", pairs)
 
 
-def summed(keep, send, levels):
+def add_kernel(left_ref, right_ref, *rest):
+    rest[-1][...] = left_ref[...] + right_ref[...]
+
+
+def plus(left, right, after):
+    if not after:
+        return left + right
+    result = (left.shape, F32)
+    return call(add_kernel, "add", [left, right, *after], [result], micros=0.2, unused=len(after))[0]
+
+
+def summed(keep, send, levels, afters=((), ())):
     quarter = keep.shape[0] // 2
     half = keep + swapped(send, 0)
     own = half[:quarter] + swapped(half[quarter:], 1, 2)
-    own = own + swapped(own, 2, 1)
+    own = plus(own, swapped(own, 2, 1), afters[0])
     for level in range(3, levels):
-        own = own + swapped(own, level)
+        own = plus(own, swapped(own, level), afters[1])
     side = swapped(own, 1, 2)
     return [own, side, swapped(own, 0), swapped(side, 0)]
 
@@ -503,96 +560,124 @@
     tall = ((count, size), F32)
     square = ((size, size), F32)
     coef = ((rank, size), BF16)
-    product = 2 * count * size * size
+    tall_pair = ((2, count, size), F32)
     work = pltpu.VMEM((2, size, size), F32)
+    rows, later_rows = payload_rows(size, True), payload_rows(size, False)
+
+    def up(level, current, sibling, extra=()):
+        (result,) = call(
+            functools.partial(up_kernel, level),
+            "up",
+            [position, current, sibling, transfer, *extra],
+            [coef],
+            micros=0.3,
+            unused=len(extra),
+        )
+        return result
 
     (current,) = call(
-        coef_kernel, "coef", [direction, basis, skeleton], [coef], flops=product, limit=60
-    )
-    for step in range(ITERS):
-        first = step == 0
-        siblings = []
-        for level in range(levels):
-            sibling = swapped(current, level)
-            siblings.append(sibling)
-            if level == levels - 1:
-                break
-            extra = []
-            if first and level == 1:
-                (block,) = call(
-                    block_kernel,
-                    "block",
-                    [points, order, current],
-                    [((count, count), BF16)],
-                    [pltpu.VMEM((8, count), F32), pltpu.VMEM((count, 128), F32)],
-                    flops=20 * product,
-                    unused=1,
-                )
-                extra = [block]
-            (current,) = call(
-                functools.partial(up_kernel, level),
-                "up",
-                [position, current, sibling, transfer] + extra,
-                [coef],
-                flops=product,
-                unused=len(extra),
-            )
-        (near,) = call(near_kernel, "near", [block, direction], [tall], flops=8 * product)
-        if first:
-            high, low, gram = call(
-                prepare_kernel,
-                "prepare",
-                [direction, residual],
-                [((2 * size, count), BF16), ((2 * size, count), BF16), square],
-                flops=8 * product,
-            )
-        rows = payload_rows(size, first)
-        image, keep, send = call(
-            functools.partial(down_kernel, levels, first),
-            "down",
-            [position, near, *siblings, coupling, transfer, basis, skeleton, high, low]
-            + ([gram] if first else [inverse]),
-            [tall, ((rows // 2, size), F32), ((rows // 2, size), F32)],
-            [pltpu.VMEM((rows, size), F32)],
-            flops=10 * product,
-            unused=0 if first else 1,
-        )
-        pieces = [position] + summed(keep, send, levels)
-        scratch = [pltpu.VMEM((rows, size), F32), work, work]
-        if first:
-            moved, current, alpha, beta, fresh, mixed, images, curvature = call(
-                first_kernel,
-                "first",
-                pieces + [image, residual, direction, basis, skeleton],
-                [tall, coef] + [square] * 6,
-                scratch,
-                flops=10 * product,
-            )
-            inverse, turn = call(
-                carry_kernel,
-                "carry",
-                [alpha, beta, fresh, mixed, images, curvature],
-                [square, square],
-                [work, work],
-                flops=8 * product,
-            )
-            residual, solution, high, low = call(
-                update_kernel,
-                "update",
-                [image, residual, direction, solution, alpha],
-                [tall, tall, ((size, count), BF16), ((size, count), BF16)],
-                flops=6 * product,
-            )
-            direction = moved
-    tall_work = pltpu.VMEM((count, size), F32)
+        coef_kernel, "coef", [direction, basis, skeleton], [coef], micros=2.7, limit=60
+    )
+    siblings = [swapped(current, 0)]
+    current = up(0, current, siblings[0])
+    siblings.append(swapped(current, 1))
+    (block,) = call(
+        block_kernel,
+        "block",
+        [points, order, current],
+        [((count, count), BF16)],
+        [pltpu.VMEM((8, count), F32), pltpu.VMEM((count, 128), F32)],
+        micros=3.6,
+        unused=1,
+    )
+    for level in range(1, levels - 1):
+        current = up(level, current, siblings[level], [block] if level == 1 else ())
+        siblings.append(swapped(current, level + 1))
+    (near,) = call(near_kernel, "near", [block, direction], [tall], micros=0.7)
+    high, low, gram = call(
+        prepare_kernel,
+        "prepare",
+        [direction, residual],
+        [((2 * size, count), BF16), ((2 * size, count), BF16), square],
+        micros=0.8,
+    )
+    image, keep, send = call(
+        functools.partial(down_kernel, levels),
+        "down",
+        [position, near, *siblings, coupling, transfer, basis, skeleton, high, low, gram],
+        [tall, ((rows // 2, size), F32), ((rows // 2, size), F32)],
+        [pltpu.VMEM((rows, size), F32)],
+        micros=3.5,
+    )
+
+    pieces = [position] + summed(keep, send, levels)
+    (pair,) = call(
+        pair_coef_kernel,
+        "pair_coef",
+        [image, residual, basis, skeleton],
+        [((2, rank, size), BF16)],
+        micros=1.0,
+    )
+    pair_sibling = swapped(pair, 0)
+    (current,) = call(
+        pair_up_kernel,
+        "pair_up",
+        [position, pair, pair_sibling, transfer],
+        [coef],
+        micros=0.3,
+    )
+    (near,) = call(
+        pair_near_kernel, "pair_near", [block, image, residual], [tall_pair], micros=2.0
+    )
+    own = []
+    for level in range(1, levels):
+        own.append(swapped(current, level))
+        if level < levels - 1:
+            current = up(level, current, own[-1], [near] if level == 1 else ())
+    other = [swapped(value, 0) for value in own]
+    (applied,) = call(
+        functools.partial(pair_down_kernel, levels),
+        "pair_down",
+        [position, near, pair_sibling, *own, *other, coupling, transfer, basis, skeleton],
+        [tall_pair],
+        micros=2.5,
+    )
+
+    image, residual, keep, send, alpha, beta, fresh, mixed, images, curvature = call(
+        first_kernel,
+        "first",
+        pieces + [image, residual, applied],
+        [tall, tall, ((later_rows // 2, size), F32), ((later_rows // 2, size), F32)] + [square] * 6,
+        [pltpu.VMEM((rows, size), F32), pltpu.VMEM((later_rows, size), F32), work, work],
+        micros=9.0,
+    )
+    inverse, turn = call(
+        carry_kernel,
+        "carry",
+        [alpha, beta, fresh, mixed, images, curvature],
+        [square, square],
+        [work, work],
+        micros=3.7,
+    )
+    direction, solution = call(
+        update_kernel,
+        "update",
+        [residual, direction, solution, alpha, beta],
+        [tall, tall],
+        micros=1.0,
+    )
+    pieces = [position] + summed(keep, send, levels, ((inverse,), (direction,)))
+    held = pltpu.VMEM((count, size), F32)
     return tuple(
         call(
             last_kernel,
             "last",
             pieces + [image, residual, direction, solution, fresh, inverse, turn],
             [tall, tall, tall],
-            scratch + [tall_work] * 3 + [pltpu.SemaphoreType.DMA((6,))],
-            flops=10 * product,
+            [pltpu.VMEM((later_rows, size), F32), work, work]
+            + [held] * 3
+            + [pltpu.SemaphoreType.DMA((6,))],
+            micros=7.0,
             apart=True,
         )
     )

time: 152 us -> 136 us (0.89)
  waiting for transfers between devices: 58.6 us -> 40 us
  starting transfers between devices: 22 us -> 24.4 us
    ppermute x22 -> x25, waiting for transfers between devices: 58.6 us -> 40 us  [swapped(): return lax.ppermute(value, 'leaf', pairs)]
    ppermute x22 -> x25, starting transfers between devices: 22 us -> 24.4 us  [swapped(): return lax.ppermute(value, 'leaf', pairs)]
    pallas_call x17 -> x20, Pallas kernels: 69 us -> 68.6 us  [call(): pl.pallas_call(kernel, name=name, in_specs=specs, out_specs=[ANY if apart...]
  transfers between devices with their start and end apart: 22 -> 25, of which waited for: 19 -> 14; matrix products, arithmetic and copies ran while one was open for 0% -> 0% of each run, Pallas kernels for 15% -> 21%
where the time goes in v3:
time: 136 us; the launch traced here: 135 us
  Pallas kernels  68.6 us (50%)
  waiting for transfers between devices  40 us (29%)
  starting transfers between devices  24.4 us (18%)
    pallas_call x20, Pallas kernels, call(): pl.pallas_call(kernel, name=name, in_specs=specs, out_specs=[ANY if apart...  68.6 us
    ppermute x25, waiting for transfers between devices, swapped(): return lax.ppermute(value, 'leaf', pairs)  40 us
    ppermute x25, starting transfers between devices, swapped(): return lax.ppermute(value, 'leaf', pairs)  24.4 us
  transfers between devices with their start and end apart: 25, of which 14 were waited for; matrix products, arithmetic and copies ran while one was open for 0% of the time, Pallas kernels for 21%

profile of v3, /device:TPU:0, one launch (start us, length us, event | category | flops | bytes accessed | tf_op | source)
XLA Modules:
  0.0 135.3 jit_solution(11420653135419473447)
XLA Ops:
  0.7 2.8 %coef.1.current_ref = bf16[256,256]{1,0:T(8,128)(2,1)} custom-call(f32[1024,256]{1,0:T(8,128)} %direction_ref.7, bf16[1024,256]{1,0:T(8,128)(2,1)} %refs_11_.1, s32[1,256]{1,0:T(1,128)} %refs_12_.1), custom_call_target="tpu_custom_call" | custom-call | flops 2969999872 | tf_op jit(solution)/shard_map/coef/pallas_call | solution.py:512
  3.9 1.2 collective-permute-done.sibling_ref.refs_2_
  6.3 2.9 %collective-permute-start.1 = (bf16[256,256]{1,0:T(8,128)(2,1)S(1)}, bf16[256,256]{1,0:T(8,128)(2,1)S(1)}, u32[]{:S(2)}, u32[]{:S(2)}) collective-permute-start(bf16[256,256]{1,0:T(8,128)(2,1)S(1)} %up.5.after_ref.current_ref), channel_id=1, source_target_pairs={{0,2},{1,3},{2,0},{3,1},{4,6},{5,7},{6,4},{7,5},{8,10},{9,11},{10,... | collective-permute-start | bytes 393224 | tf_op jit(solution)/shard_map/ppermute | solution.py:529
  9.2 3.6 %block.1.block_ref.rest_0_ = bf16[1024,1024]{1,0:T(8,128)(2,1)S(1)} custom-call(f32[3,1024]{1,0:T(4,128)S(1)} %copy-done.7, s32[1,1024]{1,0:T(1,128)S(1)} %bitcast.2, bf16[256,256]{1,0:T(8,128)(2,1)S(1)} %up.5.after_ref.current_ref), custom_call_target="tpu_custom_call" | custom-call | flops 3960000000 | tf_op jit(solution)/shard_map/block/pallas_call | solution.py:512
  13.3 1.9 %collective-permute-start.2 = (bf16[256,256]{1,0:T(8,128)(2,1)S(1)}, bf16[256,256]{1,0:T(8,128)(2,1)S(1)}, u32[]{:S(2)}, u32[]{:S(2)}) collective-permute-start(bf16[256,256]{1,0:T(8,128)(2,1)S(1)} %up.6.current_ref), channel_id=1, source_target_pairs={{0,4},{1,5},{2,6},{3,7},{4,0},{5,1},{6,2},{7,3},{8,12},{9,13},{10,... | collective-permute-start | bytes 393224 | tf_op jit(solution)/shard_map/ppermute | solution.py:529
  15.2 3.3 %collective-permute-done.2.sibling_ref.refs_4_ = bf16[256,256]{1,0:T(8,128)(2,1)S(1)} collective-permute-done((bf16[256,256]{1,0:T(8,128)(2,1)S(1)}, bf16[256,256]{1,0:T(8,128)(2,1)S(1)}, u32[]{:S(2)}, u32[]{:S(2)}) %collective-permute-start.2) | collective-permute-done | bytes 131104 | tf_op jit(solution)/shard_map/ppermute | solution.py:529
  18.7 2.8 %collective-permute-start.3 = (bf16[256,256]{1,0:T(8,128)(2,1)S(1)}, bf16[256,256]{1,0:T(8,128)(2,1)S(1)}, u32[]{:S(2)}, u32[]{:S(2)}) collective-permute-start(bf16[256,256]{1,0:T(8,128)(2,1)S(1)} %up.7), channel_id=1, source_target_pairs={{0,8},{1,9},{2,10},{3,11},{4,12},{5,13},{6,14},{7,15},{8,0},{9,1},... | collective-permute-start | bytes 393224 | tf_op jit(solution)/shard_map/ppermute | solution.py:529
  23.0 3.7 %collective-permute-done.3.refs_5_ = bf16[256,256]{1,0:T(8,128)(2,1)S(1)} collective-permute-done((bf16[256,256]{1,0:T(8,128)(2,1)S(1)}, bf16[256,256]{1,0:T(8,128)(2,1)S(1)}, u32[]{:S(2)}, u32[]{:S(2)}) %collective-permute-start.3) | collective-permute-done | bytes 131104 | tf_op jit(solution)/shard_map/ppermute | solution.py:529
  26.7 3.6 %down.1 = (f32[1024,256]{1,0:T(8,128)S(1)}, f32[336,256]{1,0:T(8,128)S(1)}, f32[336,256]{1,0:T(8,128)S(1)}) custom-call(s32[1]{0:T(128)} %bitcast.position_ref.refs_0_, f32[1024,256]{1,0:T(8,128)S(1)} %near.1.refs_1_, bf16[256,256]{1,0:T(8,128)(2,1)S(1)} %collective-permute-done.sibling_ref.refs_2_, ...), custom_call_target="tpu_custom_call" | custom-call | flops 3849999872 | tf_op jit(solution)/shard_map/down/pallas_call | solution.py:512
  30.4 1.4 %pair_coef.1.pair_ref = bf16[2,256,256]{2,1,0:T(8,128)(2,1)S(1)} custom-call(f32[1024,256]{1,0:T(8,128)S(1)} %get-tuple-element.28.image_ref, f32[1024,256]{1,0:T(8,128)S(1)} %copy-done.2, bf16[1024,256]{1,0:T(8,128)(2,1)S(1)} %copy-done.4, s32[1,256]{1,0:T(1,128)S(1)} %copy-done.9), custom_call_target="tpu_custom_call" | custom-call | flops 1100000000 | tf_op jit(solution)/shard_map/pair_coef/pallas_call | solution.py:512
  32.5 1.1 collective-permute-start.5
  33.8 1.1 collective-permute-start.12
  34.9 4.1 %collective-permute-done.5 = f32[168,256]{1,0:T(8,128)S(1)} collective-permute-done((f32[168,256]{1,0:T(8,128)S(1)}, f32[168,256]{1,0:T(8,128)S(1)}, u32[]{:S(2)}, u32[]{:S(2)}) %collective-permute-start.5) | collective-permute-done | bytes 172064 | tf_op jit(solution)/shard_map/ppermute | solution.py:529
  39.3 2.4 %pair_near.1.rest_0_.refs_1_ = f32[2,1024,256]{2,1,0:T(8,128)S(1)} custom-call(bf16[1024,1024]{1,0:T(8,128)(2,1)S(1)} %block.1.block_ref.rest_0_, f32[1024,256]{1,0:T(8,128)S(1)} %get-tuple-element.28.image_ref, f32[1024,256]{1,0:T(8,128)S(1)} %copy-done.2), custom_call_target="tpu_custom_call" | custom-call | flops 2200000000 | tf_op jit(solution)/shard_map/pair_near/pallas_call | solution.py:512
  42.0 1.9 %collective-permute-start.13 = (bf16[256,256]{1,0:T(8,128)(2,1)S(1)}, bf16[256,256]{1,0:T(8,128)(2,1)S(1)}, u32[]{:S(2)}, u32[]{:S(2)}) collective-permute-start(bf16[256,256]{1,0:T(8,128)(2,1)S(1)} %up.8.current_ref), channel_id=1, source_target_pairs={{0,4},{1,5},{2,6},{3,7},{4,0},{5,1},{6,2},{7,3},{8,12},{9,13},{10,... | collective-permute-start | bytes 393224 | tf_op jit(solution)/shard_map/ppermute | solution.py:529
  43.9 2.0 %collective-permute-done.6 = f32[168,256]{1,0:T(8,128)S(1)} collective-permute-done((f32[168,256]{1,0:T(8,128)S(1)}, f32[168,256]{1,0:T(8,128)S(1)}, u32[]{:S(2)}, u32[]{:S(2)}) %collective-permute-start.6) | collective-permute-done | bytes 172064 | tf_op jit(solution)/shard_map/ppermute | solution.py:529
  45.9 1.0 collective-permute-start.7
  46.9 1.6 %collective-permute-done.13.sibling_ref.refs_4_ = bf16[256,256]{1,0:T(8,128)(2,1)S(1)} collective-permute-done((bf16[256,256]{1,0:T(8,128)(2,1)S(1)}, bf16[256,256]{1,0:T(8,128)(2,1)S(1)}, u32[]{:S(2)}, u32[]{:S(2)}) %collective-permute-start.13) | collective-permute-done | bytes 131104 | tf_op jit(solution)/shard_map/ppermute | solution.py:529
  48.7 2.5 %collective-permute-start.14 = (bf16[256,256]{1,0:T(8,128)(2,1)S(1)}, bf16[256,256]{1,0:T(8,128)(2,1)S(1)}, u32[]{:S(2)}, u32[]{:S(2)}) collective-permute-start(bf16[256,256]{1,0:T(8,128)(2,1)S(1)} %up.9), channel_id=1, source_target_pairs={{0,8},{1,9},{2,10},{3,11},{4,12},{5,13},{6,14},{7,15},{8,0},{9,1},... | collective-permute-start | bytes 393224 | tf_op jit(solution)/shard_map/ppermute | solution.py:529
  51.3 6.7 %collective-permute-done.7 = f32[168,256]{1,0:T(8,128)S(1)} collective-permute-done((f32[168,256]{1,0:T(8,128)S(1)}, f32[168,256]{1,0:T(8,128)S(1)}, u32[]{:S(2)}, u32[]{:S(2)}) %collective-permute-start.7) | collective-permute-done | bytes 172064 | tf_op jit(solution)/shard_map/ppermute | solution.py:529
  59.9 3.6 %collective-permute-done.8.side_ref = f32[168,256]{1,0:T(8,128)S(1)} collective-permute-done((f32[168,256]{1,0:T(8,128)S(1)}, f32[168,256]{1,0:T(8,128)S(1)}, u32[]{:S(2)}, u32[]{:S(2)}) %collective-permute-start.8) | collective-permute-done | bytes 172064 | tf_op jit(solution)/shard_map/ppermute | solution.py:529
  63.5 2.5 %pair_down.1.applied_ref = f32[2,1024,256]{2,1,0:T(8,128)S(1)} custom-call(s32[1]{0:T(128)} %bitcast.position_ref.refs_0_, f32[2,1024,256]{2,1,0:T(8,128)S(1)} %pair_near.1.rest_0_.refs_1_, bf16[2,256,256]{2,1,0:T(8,128)(2,1)S(1)} %collective-permute-done.11.sibling_ref.refs_2_, bf16[256,256]{1,0:T(8,128)(2,1)S(1)} %collective-permute-done.12.sibling_ref.refs_3_, ...), custom_call_target="tpu_custom_call" | custom-call | flops 2750000128 | tf_op jit(solution)/shard_map/pair_down/pallas_call | solution.py:512
  66.0 15.7 %first.1 = (f32[1024,256]{1,0:T(8,128)S(1)}, f32[1024,256]{1,0:T(8,128)S(1)}, f32[208,256]{1,0:T(8,128)S(1)}, f32[208,256]{1,0:T(8,128)S(1)}, f32[256,256]{1,0:T...) custom-call(s32[1]{0:T(128)} %bitcast.position_ref.refs_0_, ...), custom_call_target="tpu_custom_call" | custom-call | flops 9900000256 | tf_op jit(solution)/shard_map/first/pallas_call | solution.py:512
  82.3 1.1 collective-permute-done.18
  84.2 3.9 %collective-permute-done.19 = f32[104,256]{1,0:T(8,128)S(1)} collective-permute-done((f32[104,256]{1,0:T(8,128)S(1)}, f32[104,256]{1,0:T(8,128)S(1)}, u32[]{:S(2)}, u32[]{:S(2)}) %collective-permute-start.19) | collective-permute-done | bytes 106528 | tf_op jit(solution)/shard_map/ppermute | solution.py:529
  88.3 14.8 %carry.1 = (f32[256,256]{1,0:T(8,128)S(1)}, f32[256,256]{1,0:T(8,128)S(1)}) custom-call(f32[256,256]{1,0:T(8,128)S(1)} %get-tuple-element.31.alpha_ref, f32[256,256]{1,0:T(8,128)S(1)} %get-tuple-element.32.beta_ref, f32[256,256]{1,0:T(8,128)S(1)} %get-tuple-element.33.fresh_ref, f32[256,256]{1,0:T(8,128)S(1)} %get-tuple-element.34.mixed_ref, ...), custom_call_target="tpu_custom_call" | custom-call | flops 4070000128 | tf_op jit(solution)/shard_map/carry/pallas_call | solution.py:512
  103.1 3.3 %collective-permute-start.21 = (f32[104,256]{1,0:T(8,128)S(1)}, f32[104,256]{1,0:T(8,128)S(1)}, u32[]{:S(2)}, u32[]{:S(2)}) collective-permute-start(f32[104,256]{1,0:T(8,128)S(1)} %add.28.left_ref), channel_id=1, source_target_pairs={{0,8},{1,9},{2,10},{3,11},{4,12},{5,13},{6,14},{7,15},{8,0},{9,1},... | collective-permute-start | bytes 319496 | tf_op jit(solution)/shard_map/ppermute | solution.py:529
  107.3 3.9 %collective-permute-done.21.right_ref = f32[104,256]{1,0:T(8,128)S(1)} collective-permute-done((f32[104,256]{1,0:T(8,128)S(1)}, f32[104,256]{1,0:T(8,128)S(1)}, u32[]{:S(2)}, u32[]{:S(2)}) %collective-permute-start.21) | collective-permute-done | bytes 106528 | tf_op jit(solution)/shard_map/ppermute | solution.py:529
  111.2 1.3 collective-permute-start.22
  112.5 3.5 %collective-permute-done.22.side_ref = f32[104,256]{1,0:T(8,128)S(1)} collective-permute-done((f32[104,256]{1,0:T(8,128)S(1)}, f32[104,256]{1,0:T(8,128)S(1)}, u32[]{:S(2)}, u32[]{:S(2)}) %collective-permute-start.22) | collective-permute-done | bytes 106528 | tf_op jit(solution)/shard_map/ppermute | solution.py:529
  116.0 1.3 collective-permute-done.24.far_ref
  117.3 17.8 %last.1 = (f32[1024,256]{1,0:T(8,128)}, f32[1024,256]{1,0:T(8,128)}, f32[1024,256]{1,0:T(8,128)}) custom-call(s32[1]{0:T(128)} %bitcast.position_ref.refs_0_, f32[104,256]{1,0:T(8,128)S(1)} %add.29.own_ref, f32[104,256]{1,0:T(8,128)S(1)} %collective-permute-done.22.side_ref, f32[104,256]{1,0:T(8,128)S(1)} %collective-permute-done.23.core_ref, ...), custom_call_target="tpu_custom_call" | custom-call | flops 7699999744 | tf_op jit(solution)/shard_map/last/pallas_call | solution.py:512
  (66 shorter events, 10.2 us)
Async XLA Ops:
  0.6 4.5 %copy-start = (bf16[1,3,512,256]{3,2,1,0:T(8,128)(2,1)S(1)}, bf16[1,3,512,256]{3,2,1,0:T(8,128)(2,1)}, u32[]{:S(2)}) copy-start(bf16[1,3,512,256]{3,2,1,0:T(8,128)(2,1)} %refs_10_.1) | copy-start | bytes 2359300
  0.6 8.6 %copy-start.8 = (s32[1024]{0:T(1024)S(1)}, s32[1024]{0:T(1024)}, u32[]{:S(2)}) copy-start(s32[1024]{0:T(1024)} %param.10) | copy-start | bytes 12292
  0.7 8.6 %copy-start.7 = (f32[3,1024]{1,0:T(4,128)S(1)}, f32[3,1024]{1,0:T(4,128)}, u32[]{:S(2)}) copy-start(f32[3,1024]{1,0:T(4,128)} %points_ref.1) | copy-start | bytes 36868
  3.5 1.7 %collective-permute-start = (bf16[256,256]{1,0:T(8,128)(2,1)}, bf16[256,256]{1,0:T(8,128)(2,1)S(1)}, u32[]{:S(2)}, u32[]{:S(2)}) collective-permute-start(bf16[256,256]{1,0:T(8,128)(2,1)} %coef.1.current_ref), channel_id=1, source_target_pairs={{0,1},{1,0},{2,3},{3,2},{4,5},{5,4},{6,7},{7,6},{8,9},{9,8},{10,11... | collective-permute-start | bytes 393224 | tf_op jit(solution)/shard_map/ppermute | solution.py:529
  6.3 6.7 %collective-permute-start.1 = (bf16[256,256]{1,0:T(8,128)(2,1)S(1)}, bf16[256,256]{1,0:T(8,128)(2,1)S(1)}, u32[]{:S(2)}, u32[]{:S(2)}) collective-permute-start(bf16[256,256]{1,0:T(8,128)(2,1)S(1)} %up.5.after_ref.current_ref), channel_id=1, source_target_pairs={{0,2},{1,3},{2,0},{3,1},{4,6},{5,7},{6,4},{7,5},{8,10},{9,11},{10,... | collective-permute-start | bytes 393224 | tf_op jit(solution)/shard_map/ppermute | solution.py:529
  12.8 8.7 %copy-start.1 = (f32[1024,256]{1,0:T(8,128)S(1)}, f32[1024,256]{1,0:T(8,128)}, u32[]{:S(2)}) copy-start(f32[1024,256]{1,0:T(8,128)} %direction_ref.7) | copy-start | bytes 3145732
  12.8 8.7 %copy-start.2 = (f32[1024,256]{1,0:T(8,128)S(1)}, f32[1024,256]{1,0:T(8,128)}, u32[]{:S(2)}) copy-start(f32[1024,256]{1,0:T(8,128)} %residual_ref.7) | copy-start | bytes 3145732
  13.3 5.1 %collective-permute-start.2 = (bf16[256,256]{1,0:T(8,128)(2,1)S(1)}, bf16[256,256]{1,0:T(8,128)(2,1)S(1)}, u32[]{:S(2)}, u32[]{:S(2)}) collective-permute-start(bf16[256,256]{1,0:T(8,128)(2,1)S(1)} %up.6.current_ref), channel_id=1, source_target_pairs={{0,4},{1,5},{2,6},{3,7},{4,0},{5,1},{6,2},{7,3},{8,12},{9,13},{10,... | collective-permute-start | bytes 393224 | tf_op jit(solution)/shard_map/ppermute | solution.py:529
  18.7 8.0 %collective-permute-start.3 = (bf16[256,256]{1,0:T(8,128)(2,1)S(1)}, bf16[256,256]{1,0:T(8,128)(2,1)S(1)}, u32[]{:S(2)}, u32[]{:S(2)}) collective-permute-start(bf16[256,256]{1,0:T(8,128)(2,1)S(1)} %up.7), channel_id=1, source_target_pairs={{0,8},{1,9},{2,10},{3,11},{4,12},{5,13},{6,14},{7,15},{8,0},{9,1},... | collective-permute-start | bytes 393224 | tf_op jit(solution)/shard_map/ppermute | solution.py:529
  22.3 4.4 %copy-start.4 = (bf16[1024,256]{1,0:T(8,128)(2,1)S(1)}, bf16[1024,256]{1,0:T(8,128)(2,1)}, u32[]{:S(2)}) copy-start(bf16[1024,256]{1,0:T(8,128)(2,1)} %refs_11_.1) | copy-start | bytes 1572868
  30.3 2.0 %collective-permute-start.4 = (f32[336,256]{1,0:T(8,128)S(1)}, f32[336,256]{1,0:T(8,128)S(1)}, u32[]{:S(2)}, u32[]{:S(2)}) collective-permute-start(f32[336,256]{1,0:T(8,128)S(1)} %get-tuple-element.27), channel_id=1, source_target_pairs={{0,1},{1,0},{2,3},{3,2},{4,5},{5,4},{6,7},{7,6},{8,9},{9,8},{10,11... | collective-permute-start | bytes 1032200 | tf_op jit(solution)/shard_map/ppermute | solution.py:529
  31.8 1.7 %collective-permute-start.11 = (bf16[2,256,256]{2,1,0:T(8,128)(2,1)S(1)}, bf16[2,256,256]{2,1,0:T(8,128)(2,1)S(1)}, u32[]{:S(2)}, u32[]{:S(2)}) collective-permute-start(bf16[2,256,256]{2,1,0:T(8,128)(2,1)S(1)} %pair_coef.1.pair_ref), channel_id=1, source_target_pairs={{0,1},{1,0},{2,3},{3,2},{4,5},{5,4},{6,7},{7,6},{8,9},{9,8},{10,11... | collective-permute-start | bytes 786440 | tf_op jit(solution)/shard_map/ppermute | solution.py:529
  32.5 6.6 %collective-permute-start.5 = (f32[168,256]{1,0:T(8,128)S(1)}, f32[168,256]{1,0:T(8,128)S(1)}, u32[]{:S(2)}, u32[]{:S(2)}) collective-permute-start(f32[168,256]{1,0:T(8,128)S(1)} %slice.17), channel_id=1, source_target_pairs={{0,2},{1,5},{2,0},{3,7},{4,6},{5,1},{6,4},{7,3},{8,10},{9,13},{10,... | collective-permute-start | bytes 516104 | tf_op jit(solution)/shard_map/ppermute | solution.py:529
  33.8 7.9 %collective-permute-start.12 = (bf16[256,256]{1,0:T(8,128)(2,1)S(1)}, bf16[256,256]{1,0:T(8,128)(2,1)S(1)}, u32[]{:S(2)}, u32[]{:S(2)}) collective-permute-start(bf16[256,256]{1,0:T(8,128)(2,1)S(1)} %pair_up.1.current_ref), channel_id=1, source_target_pairs={{0,2},{1,3},{2,0},{3,1},{4,6},{5,7},{6,4},{7,5},{8,10},{9,11},{10,... | collective-permute-start | bytes 393224 | tf_op jit(solution)/shard_map/ppermute | solution.py:529
  39.1 6.8 %collective-permute-start.6 = (f32[168,256]{1,0:T(8,128)S(1)}, f32[168,256]{1,0:T(8,128)S(1)}, u32[]{:S(2)}, u32[]{:S(2)}) collective-permute-start(f32[168,256]{1,0:T(8,128)S(1)} %slice_add_fusion), channel_id=1, source_target_pairs={{0,4},{1,3},{2,6},{3,1},{4,0},{5,7},{6,2},{7,5},{8,12},{9,11},{10,... | collective-permute-start | bytes 516104 | tf_op jit(solution)/shard_map/ppermute | solution.py:529
  42.0 6.5 %collective-permute-start.13 = (bf16[256,256]{1,0:T(8,128)(2,1)S(1)}, bf16[256,256]{1,0:T(8,128)(2,1)S(1)}, u32[]{:S(2)}, u32[]{:S(2)}) collective-permute-start(bf16[256,256]{1,0:T(8,128)(2,1)S(1)} %up.8.current_ref), channel_id=1, source_target_pairs={{0,4},{1,5},{2,6},{3,7},{4,0},{5,1},{6,2},{7,3},{8,12},{9,13},{10,... | collective-permute-start | bytes 393224 | tf_op jit(solution)/shard_map/ppermute | solution.py:529
  45.9 12.1 %collective-permute-start.7 = (f32[168,256]{1,0:T(8,128)S(1)}, f32[168,256]{1,0:T(8,128)S(1)}, u32[]{:S(2)}, u32[]{:S(2)}) collective-permute-start(f32[168,256]{1,0:T(8,128)S(1)} %add.22), channel_id=1, source_target_pairs={{0,8},{1,9},{2,10},{3,11},{4,12},{5,13},{6,14},{7,15},{8,0},{9,1},... | collective-permute-start | bytes 516104 | tf_op jit(solution)/shard_map/ppermute | solution.py:529
  48.7 10.6 %collective-permute-start.14 = (bf16[256,256]{1,0:T(8,128)(2,1)S(1)}, bf16[256,256]{1,0:T(8,128)(2,1)S(1)}, u32[]{:S(2)}, u32[]{:S(2)}) collective-permute-start(bf16[256,256]{1,0:T(8,128)(2,1)S(1)} %up.9), channel_id=1, source_target_pairs={{0,8},{1,9},{2,10},{3,11},{4,12},{5,13},{6,14},{7,15},{8,0},{9,1},... | collective-permute-start | bytes 393224 | tf_op jit(solution)/shard_map/ppermute | solution.py:529
  58.0 5.5 %collective-permute-start.8 = (f32[168,256]{1,0:T(8,128)S(1)}, f32[168,256]{1,0:T(8,128)S(1)}, u32[]{:S(2)}, u32[]{:S(2)}) collective-permute-start(f32[168,256]{1,0:T(8,128)S(1)} %add.23.own_ref), channel_id=1, source_target_pairs={{0,2},{1,5},{2,0},{3,7},{4,6},{5,1},{6,4},{7,3},{8,10},{9,13},{10,... | collective-permute-start | bytes 516104 | tf_op jit(solution)/shard_map/ppermute | solution.py:529
  58.8 4.6 %collective-permute-start.15 = (bf16[256,256]{1,0:T(8,128)(2,1)S(1)}, bf16[256,256]{1,0:T(8,128)(2,1)S(1)}, u32[]{:S(2)}, u32[]{:S(2)}) collective-permute-start(bf16[256,256]{1,0:T(8,128)(2,1)S(1)} %collective-permute-done.12.sibling_ref.refs_3_), channel_id=1, source_target_pairs={{0,1},{1,0},{2,3},{3,2},{4,5},{5,4},{6,7},{7,6},{8,9},{9,8},{10,11... | collective-permute-start | bytes 393224 | tf_op jit(solution)/shard_map/ppermute | solution.py:529
  58.8 4.6 %collective-permute-start.16 = (bf16[256,256]{1,0:T(8,128)(2,1)S(1)}, bf16[256,256]{1,0:T(8,128)(2,1)S(1)}, u32[]{:S(2)}, u32[]{:S(2)}) collective-permute-start(bf16[256,256]{1,0:T(8,128)(2,1)S(1)} %collective-permute-done.13.sibling_ref.refs_4_), channel_id=1, source_target_pairs={{0,1},{1,0},{2,3},{3,2},{4,5},{5,4},{6,7},{7,6},{8,9},{9,8},{10,11... | collective-permute-start | bytes 393224 | tf_op jit(solution)/shard_map/ppermute | solution.py:529
  59.4 4.1 %collective-permute-start.17 = (bf16[256,256]{1,0:T(8,128)(2,1)S(1)}, bf16[256,256]{1,0:T(8,128)(2,1)S(1)}, u32[]{:S(2)}, u32[]{:S(2)}) collective-permute-start(bf16[256,256]{1,0:T(8,128)(2,1)S(1)} %collective-permute-done.14.refs_5_), channel_id=1, source_target_pairs={{0,1},{1,0},{2,3},{3,2},{4,5},{5,4},{6,7},{7,6},{8,9},{9,8},{10,11... | collective-permute-start | bytes 393224 | tf_op jit(solution)/shard_map/ppermute | solution.py:529
  59.4 6.6 %collective-permute-start.9 = (f32[168,256]{1,0:T(8,128)S(1)}, f32[168,256]{1,0:T(8,128)S(1)}, u32[]{:S(2)}, u32[]{:S(2)}) collective-permute-start(f32[168,256]{1,0:T(8,128)S(1)} %add.23.own_ref), channel_id=1, source_target_pairs={{0,1},{1,0},{2,3},{3,2},{4,5},{5,4},{6,7},{7,6},{8,9},{9,8},{10,11... | collective-permute-start | bytes 516104 | tf_op jit(solution)/shard_map/ppermute | solution.py:529
  63.5 2.5 %collective-permute-start.10 = (f32[168,256]{1,0:T(8,128)S(1)}, f32[168,256]{1,0:T(8,128)S(1)}, u32[]{:S(2)}, u32[]{:S(2)}) collective-permute-start(f32[168,256]{1,0:T(8,128)S(1)} %collective-permute-done.8.side_ref), channel_id=1, source_target_pairs={{0,1},{1,0},{2,3},{3,2},{4,5},{5,4},{6,7},{7,6},{8,9},{9,8},{10,11... | collective-permute-start | bytes 516104 | tf_op jit(solution)/shard_map/ppermute | solution.py:529
  81.7 1.7 %collective-permute-start.18 = (f32[208,256]{1,0:T(8,128)S(1)}, f32[208,256]{1,0:T(8,128)S(1)}, u32[]{:S(2)}, u32[]{:S(2)}) collective-permute-start(f32[208,256]{1,0:T(8,128)S(1)} %get-tuple-element.30), channel_id=1, source_target_pairs={{0,1},{1,0},{2,3},{3,2},{4,5},{5,4},{6,7},{7,6},{8,9},{9,8},{10,11... | collective-permute-start | bytes 638984 | tf_op jit(solution)/shard_map/ppermute | solution.py:529
  83.4 4.8 %collective-permute-start.19 = (f32[104,256]{1,0:T(8,128)S(1)}, f32[104,256]{1,0:T(8,128)S(1)}, u32[]{:S(2)}, u32[]{:S(2)}) collective-permute-start(f32[104,256]{1,0:T(8,128)S(1)} %slice.19), channel_id=1, source_target_pairs={{0,2},{1,5},{2,0},{3,7},{4,6},{5,1},{6,4},{7,3},{8,10},{9,13},{10,... | collective-permute-start | bytes 319496 | tf_op jit(solution)/shard_map/ppermute | solution.py:529
  88.2 14.9 %collective-permute-start.20 = (f32[104,256]{1,0:T(8,128)S(1)}, f32[104,256]{1,0:T(8,128)S(1)}, u32[]{:S(2)}, u32[]{:S(2)}) collective-permute-start(f32[104,256]{1,0:T(8,128)S(1)} %slice_add_fusion.1.left_ref), channel_id=1, source_target_pairs={{0,4},{1,3},{2,6},{3,1},{4,0},{5,7},{6,2},{7,5},{8,12},{9,11},{10,... | collective-permute-start | bytes 319496 | tf_op jit(solution)/shard_map/ppermute | solution.py:529
  88.3 18.1 %copy-start.3 = (f32[1024,256]{1,0:T(8,128)S(1)}, f32[1024,256]{1,0:T(8,128)}, u32[]{:S(2)}) copy-start(f32[1024,256]{1,0:T(8,128)} %solution_ref.1) | copy-start | bytes 3145732
  103.1 8.1 %collective-permute-start.21 = (f32[104,256]{1,0:T(8,128)S(1)}, f32[104,256]{1,0:T(8,128)S(1)}, u32[]{:S(2)}, u32[]{:S(2)}) collective-permute-start(f32[104,256]{1,0:T(8,128)S(1)} %add.28.left_ref), channel_id=1, source_target_pairs={{0,8},{1,9},{2,10},{3,11},{4,12},{5,13},{6,14},{7,15},{8,0},{9,1},... | collective-permute-start | bytes 319496 | tf_op jit(solution)/shard_map/ppermute | solution.py:529
  111.2 4.8 %collective-permute-start.22 = (f32[104,256]{1,0:T(8,128)S(1)}, f32[104,256]{1,0:T(8,128)S(1)}, u32[]{:S(2)}, u32[]{:S(2)}) collective-permute-start(f32[104,256]{1,0:T(8,128)S(1)} %add.29.own_ref), channel_id=1, source_target_pairs={{0,2},{1,5},{2,0},{3,7},{4,6},{5,1},{6,4},{7,3},{8,10},{9,13},{10,... | collective-permute-start | bytes 319496 | tf_op jit(solution)/shard_map/ppermute | solution.py:529
  112.5 3.5 %collective-permute-start.23 = (f32[104,256]{1,0:T(8,128)S(1)}, f32[104,256]{1,0:T(8,128)S(1)}, u32[]{:S(2)}, u32[]{:S(2)}) collective-permute-start(f32[104,256]{1,0:T(8,128)S(1)} %add.29.own_ref), channel_id=1, source_target_pairs={{0,1},{1,0},{2,3},{3,2},{4,5},{5,4},{6,7},{7,6},{8,9},{9,8},{10,11... | collective-permute-start | bytes 319496 | tf_op jit(solution)/shard_map/ppermute | solution.py:529
  116.0 1.3 collective-permute-start.24
  (3 other events, 9.7 us)

commit v4 on v3

--- a/solution.py
+++ b/solution.py
@@ -67,15 +67,15 @@
     return jnp.concatenate(tiles, 1)
 
 
-def leaf_coefficients(vector, basis_ref, skel_ref):
-    high, low = split(vector)
-    picks = skeleton_rows(skel_ref, vector.shape[0])
+def coef_kernel(direction_ref, basis_ref, skel_ref, coef_ref):
+    high, low = split(direction_ref[...])
+    picks = skeleton_rows(skel_ref, direction_ref.shape[0])
     coef = dot_t(basis_ref[...], high) + (dot(picks, high) + dot(picks, low))
-    return coef.astype(BF16)
-
-
-def coef_kernel(direction_ref, basis_ref, skel_ref, coef_ref):
-    coef_ref[...] = leaf_coefficients(direction_ref[...], basis_ref, skel_ref)
+    coef_ref[...] = coef.astype(BF16)
+
+
+def hold_kernel(value_ref, held_ref):
+    held_ref[...] = value_ref[...]
 
 
 def block_kernel(points_ref, order_ref, after_ref, block_ref, padded, column_ref):
@@ -215,45 +215,125 @@
     return split(down)
 
 
+def factor_kernel(
+    near_ref,
+    high_ref,
+    low_ref,
+    basis_ref,
+    skel_ref,
+    near_gram_out,
+    near_square_out,
+    both_high_out,
+    both_low_out,
+    picked_out,
+    near_both_out,
+    near_picked_out,
+    ties_high_out,
+    ties_low_out,
+    basis_picked_out,
+    coef_out,
+):
+    count, size = near_ref.shape
+    near_high, near_low = split(near_ref[...])
+    near_parts = jnp.concatenate([near_high, near_low], 1)
+    high, low = high_ref[...], low_ref[...]
+    basis = basis_ref[...]
+    places, picks = skeleton_columns(skel_ref, count), skeleton_rows(skel_ref, count)
+    wide = dot(high, near_parts)
+    near_gram_out[...] = wide[:, :size] + (wide[:, size:] + dot(low, near_high))
+    wide = dot_t(near_high, near_parts)
+    cross = wide[:, size:]
+    near_square_out[...] = wide[:, :size] + (cross + cross.T)
+    picked = dot(high, places) + dot(low, places)
+    picked_out[...] = picked.astype(BF16)
+    both = picked + (dot(high, basis) + dot(low, basis))
+    both_high_out[...], both_low_out[...] = split(both)
+    coef_out[...] = both[size:].T.astype(BF16)
+    rank = basis.shape[1]
+    wide = dot(picks, jnp.concatenate([near_parts, basis], 1))
+    near_picked = wide[:, :size] + wide[:, size : 2 * size]
+    basis_picked = wide[:, 2 * size :]
+    near_picked_out[...] = near_picked
+    basis_picked_out[...] = basis_picked.astype(BF16)
+    wide = dot_t(basis, jnp.concatenate([near_parts, basis], 1))
+    near_both_out[...] = near_picked + (wide[:, :size] + wide[:, size : 2 * size])
+    ties = wide[:, 2 * size :] + (basis_picked + basis_picked.T)
+    ties_high_out[...], ties_low_out[...] = split(ties)
+
+
 def down_kernel(levels, *refs):
-    position_ref, near_ref = refs[0], refs[1]
-    siblings = [ref[...] for ref in refs[2 : 2 + levels]]
-    coupling_ref, transfer_ref, basis_ref, skel_ref, high_ref, low_ref, gram_ref = refs[
-        2 + levels : 9 + levels
-    ]
-    image_ref, keep_ref, send_ref, payload = refs[9 + levels :]
-    count, size = near_ref.shape
+    position_ref = refs[0]
+    siblings = [ref[...] for ref in refs[1 : 1 + levels]]
+    (
+        coupling_ref,
+        transfer_ref,
+        near_gram_ref,
+        near_square_ref,
+        both_high_ref,
+        both_low_ref,
+        picked_ref,
+        near_both_ref,
+        near_picked_ref,
+        ties_high_ref,
+        ties_low_ref,
+        basis_picked_ref,
+        gram_ref,
+        down_out,
+        coef_out,
+        keep_ref,
+        send_ref,
+        mixed_out,
+        images_out,
+        payload,
+    ) = refs[1 + levels :]
+    size = gram_ref.shape[1]
     position = position_ref[0]
     high, low = down_chain(position, levels, coupling_ref, transfer_ref, siblings)
-    places = skeleton_columns(skel_ref, count)
-    image = near_ref[...] + dot(basis_ref[...], high) + (dot(places, high) + dot(places, low))
-    image_ref[...] = image
-    image_high, image_low = split(image)
-    both = jnp.concatenate([image_high, image_low], 1)
-    wide = dot(high_ref[...], both)
-    grams = wide[:, :size] + (wide[:, size:] + dot(low_ref[...], image_high))
-    wide = dot_t(image_high, both)
-    cross = wide[:, size:]
-    packed, tail = pack_half(wide[:, :size] + (cross + cross.T))
+    down_out[0], down_out[1] = high, low
+    down = high.astype(F32) + low.astype(F32)
+    picked = dot(basis_picked_ref[...], high) + down
+    change = dot(ties_high_ref[...], high) + dot(ties_low_ref[...], high)
+    change = change + (dot_t(basis_picked_ref[...], low) + down)
+    near_both = near_both_ref[...]
+    coef_out[...] = (near_both + change).astype(BF16)
+    half_high, half_low = split(near_both + 0.5 * change)
+    other = (near_picked_ref[...] + 0.5 * picked).astype(BF16)
+    half = dot_t(high, half_high) + (dot_t(high, half_low) + dot_t(low, other))
+    images = near_square_ref[...] + (half + half.T)
+    grams = dot(both_high_ref[...], high) + (
+        dot(both_low_ref[...], high) + dot(picked_ref[...], low)
+    )
+    grams = near_gram_ref[...] + grams
+    packed, tail = pack_half(images)
     curvature = grams[:size]
     pair, diagonal = pack_pair(0.5 * (curvature + curvature.T), gram_ref[...])
     write_parts(
         position, [pair, grams[size:], packed], [tail, diagonal], payload, keep_ref, send_ref
     )
-
-
-def pair_coef_kernel(image_ref, residual_ref, basis_ref, skel_ref, pair_ref):
-    count, size = image_ref.shape
-    picks = skeleton_rows(skel_ref, count)
-    parts = jnp.concatenate([*split(image_ref[...]), *split(residual_ref[...])], 1)
-    coef = dot_t(basis_ref[...], parts) + dot(picks, parts)
-    pair_ref[0] = (coef[:, :size] + coef[:, size : 2 * size]).astype(BF16)
-    pair_ref[1] = (coef[:, 2 * size : 3 * size] + coef[:, 3 * size :]).astype(BF16)
-
-
-def pair_up_kernel(position_ref, pair_ref, sibling_ref, transfer_ref, coef_ref):
+    mixed_out[...] = grams[size:]
+    images_out[...] = images
+
+
+def image_kernel(near_ref, down_ref, basis_ref, skel_ref, image_ref):
+    places = skeleton_columns(skel_ref, near_ref.shape[0])
+    high, low = down_ref[0], down_ref[1]
+    image_ref[...] = (near_ref[...] + dot(basis_ref[...], high)) + (
+        dot(places, high) + dot(places, low)
+    )
+
+
+def pair_up_kernel(
+    position_ref, image_ref, residual_ref, image_other, residual_other, transfer_ref, coef_ref
+):
     core = position_ref[0] & 1
-    up_kernel(0, position_ref, pair_ref.at[core], sibling_ref.at[core], transfer_ref, coef_ref)
+
+    @pl.when(core == 0)
+    def _():
+        up_kernel(0, position_ref, image_ref, image_other, transfer_ref, coef_ref)
+
+    @pl.when(core == 1)
+    def _():
+        up_kernel(0, position_ref, residual_ref, residual_other, transfer_ref, coef_ref)
 
 
 def pair_near_kernel(block_ref, image_ref, residual_ref, near_ref):
@@ -265,13 +345,17 @@
 
 
 def pair_down_kernel(levels, *refs):
-    position_ref, near_ref, pair_ref = refs[:3]
-    own_refs, other_refs = refs[3 : 2 + levels], refs[2 + levels : 1 + 2 * levels]
-    coupling_ref, transfer_ref, basis_ref, skel_ref, applied_ref = refs[1 + 2 * levels :]
+    position_ref, near_ref, image_ref, residual_ref = refs[:4]
+    own_refs, other_refs = refs[4 : 3 + levels], refs[3 + levels : 2 + 2 * levels]
+    coupling_ref, transfer_ref, basis_ref, skel_ref, applied_ref = refs[2 + 2 * levels :]
     _, count, size = near_ref.shape
     position = position_ref[0]
     core = position & 1
-    siblings = [jnp.concatenate([pair_ref[core], pair_ref[1 - core]], 1)]
+    swap = core == 1
+    left, right = image_ref[...], residual_ref[...]
+    siblings = [
+        jnp.concatenate([jnp.where(swap, right, left), jnp.where(swap, left, right)], 1)
+    ]
     for own_ref, other_ref in zip(own_refs, other_refs):
         siblings.append(jnp.concatenate([own_ref[...], other_ref[...]], 1))
     high, low = down_chain(position, levels, coupling_ref, transfer_ref, siblings)
@@ -294,16 +378,14 @@
     return scaled, column_scale, 1.8 / widest
 
 
-def inverses(matrices, store, errors):
+def inverses(matrices, coarse, store):
     count = len(matrices)
     size = matrices[0].shape[0]
     eye = jnp.where(eye_mask(size), 1.0, 0.0)
     problems = [scaled_problem(matrix) for matrix in matrices]
-    starts = [eye * gain for _, _, gain in problems]
-    slopes = [eye - scaled * gain for scaled, _, gain in problems]
-    guesses = [start + slope * gain for start, slope, (_, _, gain) in zip(starts, slopes, problems)]
-    gaps = list(slopes)
-    for _ in range(4):
+    gaps = [eye - scaled * gain for scaled, _, gain in problems]
+    guesses = [(eye + gap) * gain for gap, (_, _, gain) in zip(gaps, problems)]
+    for _ in range(coarse):
         for at in range(count):
             rough = gaps[at].astype(BF16)
             gaps[at] = dot(rough, rough)
@@ -311,15 +393,18 @@
             guesses[at] = guesses[at] + dot(guesses[at].astype(BF16), gaps[at].astype(BF16))
     total = 0.0
     for at in range(count):
-        scaled = problems[at][0]
-        gap = eye - dot3(scaled, guesses[at])
-        near = jnp.sum(jnp.sum(gap * gap, axis=0, keepdims=True), axis=1, keepdims=True) < 0.5
-        guess = jnp.where(near, guesses[at], starts[at])
-        gap = jnp.where(near, gap, slopes[at])
-        guess = guess + dot3(guess, gap)
-        gap = eye - dot_full(scaled, guess)
-        store[at], errors[at] = guess, gap
+        gap = eye - dot3(problems[at][0], guesses[at])
+        guess = guesses[at] + dot3(guesses[at], gap)
+        rough = gap.astype(BF16)
+        gap = dot(rough, rough)
+        store[at] = guess + dot(guess.astype(BF16), gap.astype(BF16))
         total = total + jnp.sum(gap * gap)
+    good = total < 0.5
+
+    @pl.when(jnp.logical_not(good))
+    def _():
+        for at in range(count):
+            store[at] = eye * problems[at][2]
 
     def unfinished(carry):
         step, total = carry
@@ -329,18 +414,13 @@
         step, _ = carry
         total = 0.0
         for at in range(count):
-            guess = store[at] + dot3(store[at], errors[at])
-            gap = eye - dot_full(problems[at][0], guess)
-            store[at], errors[at] = guess, gap
+            gap = eye - dot_full(problems[at][0], store[at])
+            store[at] = store[at] + dot3(store[at], gap)
             total = total + jnp.sum(gap * gap)
         return step + 1, total
 
-    lax.while_loop(unfinished, refine, (0, total))
-    results = []
-    for at in range(count):
-        guess = store[at]
-        results.append(guess + dot(guess.astype(BF16), errors[at].astype(BF16)))
-    return [(result, problem[1]) for result, problem in zip(results, problems)]
+    lax.while_loop(unfinished, refine, (0, jnp.where(good, total, 1.0)))
+    return [(store[at], problems[at][1]) for at in range(count)]
 
 
 def collect(position, own_ref, side_ref, core_ref, far_ref, payload):
@@ -372,7 +452,9 @@
     image_ref,
     residual_ref,
     applied_ref,
-    image_out,
+    local_mixed_ref,
+    local_images_ref,
+    partial_out,
     residual_out,
     keep_out,
     send_out,
@@ -385,7 +467,6 @@
     payload,
     later,
     store,
-    errors,
 ):
     size = image_ref.shape[1]
     position = position_ref[0]
@@ -394,23 +475,31 @@
     base = 2 * size + size // 2
     images = unpack_half(payload[2 * size : base, :], payload[base : base + 1, :])
     curvature, res_gram = unpack_pair(payload[0:size, :], payload[base + 1 : base + 2, :])
-    (first, first_scale), (second, second_scale) = inverses([curvature, res_gram], store, errors)
+    (first, first_scale), (second, second_scale) = inverses([curvature, res_gram], 3, store)
     alpha = dot3(first, res_gram * first_scale) * first_scale
     fresh = fresh_gram(res_gram, mixed, images, alpha)
     beta = dot3(second, fresh * second_scale) * second_scale
     old_image = image_ref[...]
     residual = residual_ref[...] - dot3(old_image, alpha)
-    image = (applied_ref[1] - dot3(applied_ref[0], alpha)) + dot3(old_image, beta)
+    partial = applied_ref[1] - dot3(applied_ref[0], alpha)
     residual_out[...] = residual
-    image_out[...] = image
-    high, low = split(image)
-    both = jnp.concatenate([high, low], 1)
+    partial_out[...] = partial
+    partial_high, partial_low = split(partial)
+    old_high, old_low = split(old_image)
     residual_high, residual_low = split(residual)
+    both = jnp.concatenate([partial_high, partial_low], 1)
     wide = dot_t(residual_high, both)
-    cross_gram = wide[:, :size] + (wide[:, size:] + dot_t(residual_low, high))
-    wide = dot_t(high, both)
-    cross = wide[:, size:]
-    packed, tail = pack_half(wide[:, :size] + (cross + cross.T))
+    cross_gram = wide[:, :size] + (wide[:, size:] + dot_t(residual_low, partial_high))
+    wide = dot_t(partial_high, jnp.concatenate([both, old_high, old_low], 1))
+    cross = wide[:, size : 2 * size]
+    square = wide[:, :size] + (cross + cross.T)
+    old_gram = wide[:, 2 * size : 3 * size] + wide[:, 3 * size :]
+    old_gram = old_gram + dot_t(partial_low, old_high)
+    local_images = local_images_ref[...]
+    old_cross = local_mixed_ref[...] - dot3(alpha.T, local_images)
+    cross_gram = cross_gram + dot3(old_cross, beta)
+    half = dot3(old_gram, beta) + 0.5 * dot3(beta.T, dot3(local_images, beta))
+    packed, tail = pack_half(square + (half + half.T))
     write_parts(position, [cross_gram, packed], [tail], later, keep_out, send_out)
     alpha_out[...] = alpha
     beta_out[...] = beta
@@ -430,10 +519,9 @@
     inverse_out,
     turn_out,
     store,
-    errors,
 ):
     beta = beta_ref[...]
-    ((inverse, scale),) = inverses([fresh_ref[...]], store, errors)
+    ((inverse, scale),) = inverses([fresh_ref[...]], 4, store)
     inverse_out[...] = inverse * scale
     across = mixed_ref[...].T - dot3(images_ref[...], alpha_ref[...])
     across = across + dot3(curvature_ref[...], beta)
@@ -442,11 +530,21 @@
 
 
 def update_kernel(
-    residual_ref, direction_ref, solution_ref, alpha_ref, beta_ref, direction_out, solution_out
+    residual_ref,
+    direction_ref,
+    solution_ref,
+    partial_ref,
+    image_ref,
+    alpha_ref,
+    beta_ref,
+    direction_out,
+    solution_out,
+    image_out,
 ):
-    direction = direction_ref[...]
-    direction_out[...] = residual_ref[...] + dot3(direction, beta_ref[...])
+    direction, beta = direction_ref[...], beta_ref[...]
+    direction_out[...] = residual_ref[...] + dot3(direction, beta)
     solution_out[...] = solution_ref[...] + dot3(direction, alpha_ref[...])
+    image_out[...] = partial_ref[...] + dot3(image_ref[...], beta)
 
 
 def last_kernel(
@@ -467,7 +565,6 @@
     direction_out,
     payload,
     store,
-    errors,
     solution_held,
     residual_held,
     direction_held,
@@ -480,10 +577,9 @@
     images = unpack_half(payload[size:base, :], payload[base : base + 1, :])
     res_gram = fresh_ref[...]
     curvature = 0.5 * (mixed + mixed.T) + turn_ref[...]
-    ((first, scale),) = inverses([curvature], store, errors)
+    ((first, scale),) = inverses([curvature], 4, store)
     alpha = dot3(first, res_gram * scale) * scale
-    residual = residual_ref[...] - dot3(image_ref[...], alpha)
-    residual_held[...] = residual
+    residual_held[...] = residual_ref[...] - dot3(image_ref[...], alpha)
     copies = [pltpu.make_async_copy(residual_held, residual_out, sems.at[0])]
     copies[0].start()
     solution_held[...] = solution_ref[...] + dot3(direction_ref[...], alpha)
@@ -544,9 +640,9 @@
     quarter = keep.shape[0] // 2
     half = keep + swapped(send, 0)
     own = half[:quarter] + swapped(half[quarter:], 1, 2)
-    own = plus(own, swapped(own, 2, 1), afters[0])
     for level in range(3, levels):
-        own = plus(own, swapped(own, level), afters[1])
+        own = plus(own, swapped(own, level), afters[0] if level == 3 else ())
+    own = plus(own, swapped(own, 2, 1), afters[1])
     side = swapped(own, 1, 2)
     return [own, side, swapped(own, 0), swapped(side, 0)]
 
@@ -575,10 +671,12 @@
         )
         return result
 
+    held = pltpu.VMEM((count, size), F32)
     (current,) = call(
         coef_kernel, "coef", [direction, basis, skeleton], [coef], micros=2.7, limit=60
     )
     siblings = [swapped(current, 0)]
+    (current,) = call(hold_kernel, "hold", [current], [coef], micros=0.5)
     current = up(0, current, siblings[0])
     siblings.append(swapped(current, 1))
     (block,) = call(
@@ -590,9 +688,6 @@
         micros=3.6,
         unused=1,
     )
-    for level in range(1, levels - 1):
-        current = up(level, current, siblings[level], [block] if level == 1 else ())
-        siblings.append(swapped(current, level + 1))
     (near,) = call(near_kernel, "near", [block, direction], [tall], micros=0.7)
     high, low, gram = call(
         prepare_kernel,
@@ -601,28 +696,39 @@
         [((2 * size, count), BF16), ((2 * size, count), BF16), square],
         micros=0.8,
     )
-    image, keep, send = call(
+    afters = {1: [block], 2: [near, high]}
+    for level in range(1, levels - 1):
+        current = up(level, current, siblings[level], afters.get(level, ()))
+        siblings.append(swapped(current, level + 1))
+    double, double_low = ((2 * size, rank), F32), ((2 * size, rank), BF16)
+    factors = call(
+        factor_kernel,
+        "factor",
+        [near, high, low, basis, skeleton],
+        [((2 * size, size), F32), square, double_low, double_low, double_low]
+        + [((rank, size), F32), ((rank, size), F32)]
+        + [((rank, rank), BF16)] * 3
+        + [coef],
+        micros=3.0,
+    )
+    residual_coef = factors[-1]
+    down, image_coef, keep, send, local_mixed, local_images = call(
         functools.partial(down_kernel, levels),
         "down",
-        [position, near, *siblings, coupling, transfer, basis, skeleton, high, low, gram],
-        [tall, ((rows // 2, size), F32), ((rows // 2, size), F32)],
+        [position, *siblings, coupling, transfer, *factors[:-1], gram],
+        [((2, rank, size), BF16), coef, ((rows // 2, size), F32), ((rows // 2, size), F32)]
+        + [square, square],
         [pltpu.VMEM((rows, size), F32)],
-        micros=3.5,
+        micros=2.0,
     )
 
     pieces = [position] + summed(keep, send, levels)
-    (pair,) = call(
-        pair_coef_kernel,
-        "pair_coef",
-        [image, residual, basis, skeleton],
-        [((2, rank, size), BF16)],
-        micros=1.0,
-    )
-    pair_sibling = swapped(pair, 0)
+    (image,) = call(image_kernel, "image", [near, down, basis, skeleton], [tall], micros=0.7)
+    others = [swapped(image_coef, 0), swapped(residual_coef, 0)]
     (current,) = call(
         pair_up_kernel,
         "pair_up",
-        [position, pair, pair_sibling, transfer],
+        [position, image_coef, residual_coef, *others, transfer],
         [coef],
         micros=0.3,
     )
@@ -638,43 +744,42 @@
     (applied,) = call(
         functools.partial(pair_down_kernel, levels),
         "pair_down",
-        [position, near, pair_sibling, *own, *other, coupling, transfer, basis, skeleton],
+        [position, near, *others, *own, *other, coupling, transfer, basis, skeleton],
         [tall_pair],
         micros=2.5,
     )
 
-    image, residual, keep, send, alpha, beta, fresh, mixed, images, curvature = call(
+    partial, residual, keep, send, alpha, beta, fresh, mixed, images, curvature = call(
         first_kernel,
         "first",
-        pieces + [image, residual, applied],
+        pieces + [image, residual, applied, local_mixed, local_images],
         [tall, tall, ((later_rows // 2, size), F32), ((later_rows // 2, size), F32)] + [square] * 6,
-        [pltpu.VMEM((rows, size), F32), pltpu.VMEM((later_rows, size), F32), work, work],
-        micros=9.0,
+        [pltpu.VMEM((rows, size), F32), pltpu.VMEM((later_rows, size), F32), work],
+        micros=7.0,
     )
     inverse, turn = call(
         carry_kernel,
         "carry",
         [alpha, beta, fresh, mixed, images, curvature],
         [square, square],
-        [work, work],
-        micros=3.7,
-    )
-    direction, solution = call(
+        [work],
+        micros=3.0,
+    )
+    direction, solution, image = call(
         update_kernel,
         "update",
-        [residual, direction, solution, alpha, beta],
-        [tall, tall],
-        micros=1.0,
+        [residual, direction, solution, partial, image, alpha, beta],
+        [tall, tall, tall],
+        micros=1.5,
     )
     pieces = [position] + summed(keep, send, levels, ((inverse,), (direction,)))
-    held = pltpu.VMEM((count, size), F32)
     return tuple(
         call(
             last_kernel,
             "last",
             pieces + [image, residual, direction, solution, fresh, inverse, turn],
             [tall, tall, tall],
-            [pltpu.VMEM((later_rows, size), F32), work, work]
+            [pltpu.VMEM((later_rows, size), F32), work]
             + [held] * 3
             + [pltpu.SemaphoreType.DMA((6,))],
             micros=7.0,

time: 136 us -> 133 us (0.978)
  waiting for transfers between devices: 40 us -> 30.5 us
  Pallas kernels: 68.6 us -> 74.4 us
    ppermute x25 -> x26, waiting for transfers between devices: 40 us -> 30.5 us  [swapped(): return lax.ppermute(value, 'leaf', pairs)]
    pallas_call x20 -> x22, Pallas kernels: 68.6 us -> 74.4 us  [call(): pl.pallas_call(kernel, name=name, in_specs=specs, out_specs=[ANY if apart...]
    ppermute x25 -> x26, starting transfers between devices: 24.4 us -> 24.5 us  [swapped(): return lax.ppermute(value, 'leaf', pairs)]
  transfers between devices with their start and end apart: 25 -> 26, of which waited for: 14 -> 18; matrix products, arithmetic and copies ran while one was open for 0% -> 0% of each run, Pallas kernels for 21% -> 23%
where the time goes in v4:
time: 133 us; the launch traced here: 132 us
  Pallas kernels  74.4 us (56%)
  waiting for transfers between devices  30.5 us (23%)
  starting transfers between devices  24.5 us (18%)
    pallas_call x22, Pallas kernels, call(): pl.pallas_call(kernel, name=name, in_specs=specs, out_specs=[ANY if apart...  74.4 us
    ppermute x26, waiting for transfers between devices, swapped(): return lax.ppermute(value, 'leaf', pairs)  30.5 us
    ppermute x26, starting transfers between devices, swapped(): return lax.ppermute(value, 'leaf', pairs)  24.5 us
  transfers between devices with their start and end apart: 26, of which 18 were waited for; matrix products, arithmetic and copies ran while one was open for 0% of the time, Pallas kernels for 23%

profile of v4, /device:TPU:0, one launch (start us, length us, event | category | flops | bytes accessed | tf_op | source)
XLA Modules:
  0.0 131.7 jit_solution(2489463960032527138)
XLA Ops:
  0.6 2.8 %coef.1.value_ref = bf16[256,256]{1,0:T(8,128)(2,1)} custom-call(f32[1024,256]{1,0:T(8,128)} %direction_ref.7, bf16[1024,256]{1,0:T(8,128)(2,1)} %refs_12_.1, s32[1,256]{1,0:T(1,128)} %refs_13_.1), custom_call_target="tpu_custom_call" | custom-call | flops 2969999872 | tf_op jit(solution)/shard_map/coef/pallas_call | solution.py:608
  5.4 2.9 %collective-permute-start.1 = (bf16[256,256]{1,0:T(8,128)(2,1)S(1)}, bf16[256,256]{1,0:T(8,128)(2,1)S(1)}, u32[]{:S(2)}, u32[]{:S(2)}) collective-permute-start(bf16[256,256]{1,0:T(8,128)(2,1)S(1)} %up.5.after_ref.current_ref), channel_id=1, source_target_pairs={{0,2},{1,3},{2,0},{3,1},{4,6},{5,7},{6,4},{7,5},{8,10},{9,11},{10,... | collective-permute-start | bytes 393224 | tf_op jit(solution)/shard_map/ppermute | solution.py:625
  8.3 3.6 %block.1.rest_0_.block_ref = bf16[1024,1024]{1,0:T(8,128)(2,1)S(1)} custom-call(f32[3,1024]{1,0:T(4,128)S(1)} %copy-done.8, s32[1,1024]{1,0:T(1,128)S(1)} %bitcast.2, bf16[256,256]{1,0:T(8,128)(2,1)S(1)} %up.5.after_ref.current_ref), custom_call_target="tpu_custom_call" | custom-call | flops 3960000000 | tf_op jit(solution)/shard_map/block/pallas_call | solution.py:608
  12.4 1.9 %collective-permute-start.2 = (bf16[256,256]{1,0:T(8,128)(2,1)S(1)}, bf16[256,256]{1,0:T(8,128)(2,1)S(1)}, u32[]{:S(2)}, u32[]{:S(2)}) collective-permute-start(bf16[256,256]{1,0:T(8,128)(2,1)S(1)} %up.6.current_ref), channel_id=1, source_target_pairs={{0,4},{1,5},{2,6},{3,7},{4,0},{5,1},{6,2},{7,3},{8,12},{9,13},{10,... | collective-permute-start | bytes 393224 | tf_op jit(solution)/shard_map/ppermute | solution.py:625
  15.8 1.8 %collective-permute-done.2.sibling_ref.refs_3_ = bf16[256,256]{1,0:T(8,128)(2,1)S(1)} collective-permute-done((bf16[256,256]{1,0:T(8,128)(2,1)S(1)}, bf16[256,256]{1,0:T(8,128)(2,1)S(1)}, u32[]{:S(2)}, u32[]{:S(2)}) %collective-permute-start.2) | collective-permute-done | bytes 131104 | tf_op jit(solution)/shard_map/ppermute | solution.py:625
  17.8 2.8 %collective-permute-start.3 = (bf16[256,256]{1,0:T(8,128)(2,1)S(1)}, bf16[256,256]{1,0:T(8,128)(2,1)S(1)}, u32[]{:S(2)}, u32[]{:S(2)}) collective-permute-start(bf16[256,256]{1,0:T(8,128)(2,1)S(1)} %up.7), channel_id=1, source_target_pairs={{0,8},{1,9},{2,10},{3,11},{4,12},{5,13},{6,14},{7,15},{8,0},{9,1},... | collective-permute-start | bytes 393224 | tf_op jit(solution)/shard_map/ppermute | solution.py:625
  20.6 3.2 %factor.1 = (f32[512,256]{1,0:T(8,128)S(1)}, f32[256,256]{1,0:T(8,128)S(1)}, bf16[512,256]{1,0:T(8,128)(2,1)S(1)}, bf16[512,256]{1,0:T(8,128)(2,1)S(1)}, bf16[51...) custom-call(f32[1024,256]{1,0:T(8,128)S(1)} %near.1.rest_0_.near_ref, ...), custom_call_target="tpu_custom_call" | custom-call | flops 3300000000 | tf_op jit(solution)/shard_map/factor/pallas_call | solution.py:608
  23.8 2.0 %collective-permute-done.3.refs_4_ = bf16[256,256]{1,0:T(8,128)(2,1)S(1)} collective-permute-done((bf16[256,256]{1,0:T(8,128)(2,1)S(1)}, bf16[256,256]{1,0:T(8,128)(2,1)S(1)}, u32[]{:S(2)}, u32[]{:S(2)}) %collective-permute-start.3) | collective-permute-done | bytes 131104 | tf_op jit(solution)/shard_map/ppermute | solution.py:625
  25.8 2.1 %down.1 = (bf16[2,256,256]{2,1,0:T(8,128)(2,1)S(1)}, bf16[256,256]{1,0:T(8,128)(2,1)S(1)}, f32[336,256]{1,0:T(8,128)S(1)}, f32[336,256]{1,0:T(8,128)S(1)}, f32[2...) custom-call(s32[1]{0:T(128)} %bitcast.position_ref.refs_0_, bf16[256,256]{1,0:T(8,128)(2,1)S(1)} %collective-permute-done.sibling_ref.refs_1_, ...), custom_call_target="tpu_custom_call" | custom-call | flops 2200000000 | tf_op jit(solution)/shard_map/down/pallas_call | solution.py:608
  28.0 1.6 %collective-permute-done.4 = f32[336,256]{1,0:T(8,128)S(1)} collective-permute-done((f32[336,256]{1,0:T(8,128)S(1)}, f32[336,256]{1,0:T(8,128)S(1)}, u32[]{:S(2)}, u32[]{:S(2)}) %collective-permute-start.4) | collective-permute-done | bytes 344096 | tf_op jit(solution)/shard_map/ppermute | solution.py:625
  29.7 1.1 collective-permute-start.5
  33.8 1.3 collective-permute-done.5
  35.2 1.5 %collective-permute-start.6 = (f32[168,256]{1,0:T(8,128)S(1)}, f32[168,256]{1,0:T(8,128)S(1)}, u32[]{:S(2)}, u32[]{:S(2)}) collective-permute-start(f32[168,256]{1,0:T(8,128)S(1)} %slice_add_fusion), channel_id=1, source_target_pairs={{0,8},{1,9},{2,10},{3,11},{4,12},{5,13},{6,14},{7,15},{8,0},{9,1},... | collective-permute-start | bytes 516104 | tf_op jit(solution)/shard_map/ppermute | solution.py:625
  36.6 2.4 %pair_near.1.rest_0_.refs_1_ = f32[2,1024,256]{2,1,0:T(8,128)S(1)} custom-call(bf16[1024,1024]{1,0:T(8,128)(2,1)S(1)} %block.1.rest_0_.block_ref, f32[1024,256]{1,0:T(8,128)S(1)} %image.1.image_ref, f32[1024,256]{1,0:T(8,128)S(1)} %copy-done.4), custom_call_target="tpu_custom_call" | custom-call | flops 2200000000 | tf_op jit(solution)/shard_map/pair_near/pallas_call | solution.py:608
  39.3 2.3 %collective-permute-start.14 = (bf16[256,256]{1,0:T(8,128)(2,1)S(1)}, bf16[256,256]{1,0:T(8,128)(2,1)S(1)}, u32[]{:S(2)}, u32[]{:S(2)}) collective-permute-start(bf16[256,256]{1,0:T(8,128)(2,1)S(1)} %up.8.current_ref), channel_id=1, source_target_pairs={{0,4},{1,5},{2,6},{3,7},{4,0},{5,1},{6,2},{7,3},{8,12},{9,13},{10,... | collective-permute-start | bytes 393224 | tf_op jit(solution)/shard_map/ppermute | solution.py:625
  41.7 3.8 %collective-permute-done.6 = f32[168,256]{1,0:T(8,128)S(1)} collective-permute-done((f32[168,256]{1,0:T(8,128)S(1)}, f32[168,256]{1,0:T(8,128)S(1)}, u32[]{:S(2)}, u32[]{:S(2)}) %collective-permute-start.6) | collective-permute-done | bytes 172064 | tf_op jit(solution)/shard_map/ppermute | solution.py:625
  45.6 1.9 %collective-permute-done.14.sibling_ref.refs_5_ = bf16[256,256]{1,0:T(8,128)(2,1)S(1)} collective-permute-done((bf16[256,256]{1,0:T(8,128)(2,1)S(1)}, bf16[256,256]{1,0:T(8,128)(2,1)S(1)}, u32[]{:S(2)}, u32[]{:S(2)}) %collective-permute-start.14) | collective-permute-done | bytes 131104 | tf_op jit(solution)/shard_map/ppermute | solution.py:625
  47.8 1.6 %collective-permute-start.15 = (bf16[256,256]{1,0:T(8,128)(2,1)S(1)}, bf16[256,256]{1,0:T(8,128)(2,1)S(1)}, u32[]{:S(2)}, u32[]{:S(2)}) collective-permute-start(bf16[256,256]{1,0:T(8,128)(2,1)S(1)} %up.9), channel_id=1, source_target_pairs={{0,8},{1,9},{2,10},{3,11},{4,12},{5,13},{6,14},{7,15},{8,0},{9,1},... | collective-permute-start | bytes 393224 | tf_op jit(solution)/shard_map/ppermute | solution.py:625
  49.4 2.9 %collective-permute-done.7 = f32[168,256]{1,0:T(8,128)S(1)} collective-permute-done((f32[168,256]{1,0:T(8,128)S(1)}, f32[168,256]{1,0:T(8,128)S(1)}, u32[]{:S(2)}, u32[]{:S(2)}) %collective-permute-start.7) | collective-permute-done | bytes 172064 | tf_op jit(solution)/shard_map/ppermute | solution.py:625
  53.9 2.4 %collective-permute-done.15.refs_6_ = bf16[256,256]{1,0:T(8,128)(2,1)S(1)} collective-permute-done((bf16[256,256]{1,0:T(8,128)(2,1)S(1)}, bf16[256,256]{1,0:T(8,128)(2,1)S(1)}, u32[]{:S(2)}, u32[]{:S(2)}) %collective-permute-start.15) | collective-permute-done | bytes 131104 | tf_op jit(solution)/shard_map/ppermute | solution.py:625
  57.8 2.5 %pair_down.1.applied_ref = f32[2,1024,256]{2,1,0:T(8,128)S(1)} custom-call(s32[1]{0:T(128)} %bitcast.position_ref.refs_0_, f32[2,1024,256]{2,1,0:T(8,128)S(1)} %pair_near.1.rest_0_.refs_1_, bf16[256,256]{1,0:T(8,128)(2,1)S(1)} %collective-permute-done.11.image_other.refs_2_, bf16[256,256]{1,0:T(8,128)(2,1)S(1)} %collective-permute-done.12.residual_other.refs_3_, ...), custom_call_target="tpu_custom_call" | custom-call | flops 2750000128 | tf_op jit(solution)/shard_map/pair_down/pallas_call | solution.py:608
  60.4 22.0 %first.1 = (f32[1024,256]{1,0:T(8,128)S(1)}, f32[1024,256]{1,0:T(8,128)S(1)}, f32[208,256]{1,0:T(8,128)S(1)}, f32[208,256]{1,0:T(8,128)S(1)}, f32[256,256]{1,0:T...) custom-call(s32[1]{0:T(128)} %bitcast.position_ref.refs_0_, ...), custom_call_target="tpu_custom_call" | custom-call | flops 7699999744 | tf_op jit(solution)/shard_map/first/pallas_call | solution.py:608
  82.9 1.1 collective-permute-done.19
  85.1 3.7 %collective-permute-done.20 = f32[104,256]{1,0:T(8,128)S(1)} collective-permute-done((f32[104,256]{1,0:T(8,128)S(1)}, f32[104,256]{1,0:T(8,128)S(1)}, u32[]{:S(2)}, u32[]{:S(2)}) %collective-permute-start.20) | collective-permute-done | bytes 106528 | tf_op jit(solution)/shard_map/ppermute | solution.py:625
  89.4 14.1 %carry.1 = (f32[256,256]{1,0:T(8,128)S(1)}, f32[256,256]{1,0:T(8,128)S(1)}) custom-call(f32[256,256]{1,0:T(8,128)S(1)} %get-tuple-element.60.alpha_ref, f32[256,256]{1,0:T(8,128)S(1)} %get-tuple-element.61.beta_ref, f32[256,256]{1,0:T(8,128)S(1)} %get-tuple-element.62.fresh_ref, f32[256,256]{1,0:T(8,128)S(1)} %get-tuple-element.63.mixed_ref, ...), custom_call_target="tpu_custom_call" | custom-call | flops 3300000000 | tf_op jit(solution)/shard_map/carry/pallas_call | solution.py:608
  103.6 2.7 %collective-permute-start.22 = (f32[104,256]{1,0:T(8,128)S(1)}, f32[104,256]{1,0:T(8,128)S(1)}, u32[]{:S(2)}, u32[]{:S(2)}) collective-permute-start(f32[104,256]{1,0:T(8,128)S(1)} %add.28.left_ref), channel_id=1, source_target_pairs={{0,4},{1,3},{2,6},{3,1},{4,0},{5,7},{6,2},{7,5},{8,12},{9,11},{10,... | collective-permute-start | bytes 319496 | tf_op jit(solution)/shard_map/ppermute | solution.py:625
  106.3 1.4 %update.1 = (f32[1024,256]{1,0:T(8,128)S(1)}, f32[1024,256]{1,0:T(8,128)S(1)}, f32[1024,256]{1,0:T(8,128)S(1)}) custom-call(f32[1024,256]{1,0:T(8,128)S(1)} %get-tuple-element.67.residual_ref, f32[1024,256]{1,0:T(8,128)S(1)} %copy-done.1, f32[1024,256]{1,0:T(8,128)S(1)} %copy-done.5, f32[1024,256]{1,0:T(8,128)S(1)} %get-tuple-element.68.partial_ref, ...), custom_call_target="tpu_custom_call" | custom-call | flops 1650000000 | tf_op jit(solution)/shard_map/update/pallas_call | solution.py:608
  107.7 1.2 collective-permute-done.22.right_ref
  109.0 1.2 collective-permute-start.23
  110.2 3.6 %collective-permute-done.23.side_ref = f32[104,256]{1,0:T(8,128)S(1)} collective-permute-done((f32[104,256]{1,0:T(8,128)S(1)}, f32[104,256]{1,0:T(8,128)S(1)}, u32[]{:S(2)}, u32[]{:S(2)}) %collective-permute-start.23) | collective-permute-done | bytes 106528 | tf_op jit(solution)/shard_map/ppermute | solution.py:625
  113.8 1.3 collective-permute-done.25.far_ref
  115.1 16.4 %last.1 = (f32[1024,256]{1,0:T(8,128)}, f32[1024,256]{1,0:T(8,128)}, f32[1024,256]{1,0:T(8,128)}) custom-call(s32[1]{0:T(128)} %bitcast.position_ref.refs_0_, f32[104,256]{1,0:T(8,128)S(1)} %add.29.own_ref, f32[104,256]{1,0:T(8,128)S(1)} %collective-permute-done.23.side_ref, f32[104,256]{1,0:T(8,128)S(1)} %collective-permute-done.24.core_ref, ...), custom_call_target="tpu_custom_call" | custom-call | flops 7699999744 | tf_op jit(solution)/shard_map/last/pallas_call | solution.py:608
  (70 shorter events, 13.5 us)
Async XLA Ops:
  0.6 7.7 %copy-start.8 = (f32[3,1024]{1,0:T(4,128)S(1)}, f32[3,1024]{1,0:T(4,128)}, u32[]{:S(2)}) copy-start(f32[3,1024]{1,0:T(4,128)} %points_ref.1) | copy-start | bytes 36868
  3.4 4.9 %copy-start.9 = (s32[1024]{0:T(1024)S(1)}, s32[1024]{0:T(1024)}, u32[]{:S(2)}) copy-start(s32[1024]{0:T(1024)} %param.10) | copy-start | bytes 12292
  3.4 1.6 %collective-permute-start = (bf16[256,256]{1,0:T(8,128)(2,1)}, bf16[256,256]{1,0:T(8,128)(2,1)S(1)}, u32[]{:S(2)}, u32[]{:S(2)}) collective-permute-start(bf16[256,256]{1,0:T(8,128)(2,1)} %coef.1.value_ref), channel_id=1, source_target_pairs={{0,1},{1,0},{2,3},{3,2},{4,5},{5,4},{6,7},{7,6},{8,9},{9,8},{10,11... | collective-permute-start | bytes 393224 | tf_op jit(solution)/shard_map/ppermute | solution.py:625
  5.4 6.8 %collective-permute-start.1 = (bf16[256,256]{1,0:T(8,128)(2,1)S(1)}, bf16[256,256]{1,0:T(8,128)(2,1)S(1)}, u32[]{:S(2)}, u32[]{:S(2)}) collective-permute-start(bf16[256,256]{1,0:T(8,128)(2,1)S(1)} %up.5.after_ref.current_ref), channel_id=1, source_target_pairs={{0,2},{1,3},{2,0},{3,1},{4,6},{5,7},{6,4},{7,5},{8,10},{9,11},{10,... | collective-permute-start | bytes 393224 | tf_op jit(solution)/shard_map/ppermute | solution.py:625
  12.4 5.1 %collective-permute-start.2 = (bf16[256,256]{1,0:T(8,128)(2,1)S(1)}, bf16[256,256]{1,0:T(8,128)(2,1)S(1)}, u32[]{:S(2)}, u32[]{:S(2)}) collective-permute-start(bf16[256,256]{1,0:T(8,128)(2,1)S(1)} %up.6.current_ref), channel_id=1, source_target_pairs={{0,4},{1,5},{2,6},{3,7},{4,0},{5,1},{6,2},{7,3},{8,12},{9,13},{10,... | collective-permute-start | bytes 393224 | tf_op jit(solution)/shard_map/ppermute | solution.py:625
  15.8 4.8 %copy-start.2 = (bf16[1024,256]{1,0:T(8,128)(2,1)S(1)}, bf16[1024,256]{1,0:T(8,128)(2,1)}, u32[]{:S(2)}) copy-start(bf16[1024,256]{1,0:T(8,128)(2,1)} %refs_12_.1) | copy-start | bytes 1572868
  15.8 4.8 %copy-start.3 = (s32[1,256]{1,0:T(1,128)S(1)}, s32[1,256]{1,0:T(1,128)}, u32[]{:S(2)}) copy-start(s32[1,256]{1,0:T(1,128)} %refs_13_.1) | copy-start | bytes 3076
  17.8 8.0 %collective-permute-start.3 = (bf16[256,256]{1,0:T(8,128)(2,1)S(1)}, bf16[256,256]{1,0:T(8,128)(2,1)S(1)}, u32[]{:S(2)}, u32[]{:S(2)}) collective-permute-start(bf16[256,256]{1,0:T(8,128)(2,1)S(1)} %up.7), channel_id=1, source_target_pairs={{0,8},{1,9},{2,10},{3,11},{4,12},{5,13},{6,14},{7,15},{8,0},{9,1},... | collective-permute-start | bytes 393224 | tf_op jit(solution)/shard_map/ppermute | solution.py:625
  20.6 5.2 %copy-start.6 = (bf16[1,4,256,256]{3,2,1,0:T(8,128)(2,1)S(1)}, bf16[1,4,256,256]{3,2,1,0:T(8,128)(2,1)}, u32[]{:S(2)}) copy-start(bf16[1,4,256,256]{3,2,1,0:T(8,128)(2,1)} %refs_10_.1) | copy-start | bytes 1572868
  27.9 1.7 %collective-permute-start.4 = (f32[336,256]{1,0:T(8,128)S(1)}, f32[336,256]{1,0:T(8,128)S(1)}, u32[]{:S(2)}, u32[]{:S(2)}) collective-permute-start(f32[336,256]{1,0:T(8,128)S(1)} %get-tuple-element.52), channel_id=1, source_target_pairs={{0,1},{1,0},{2,3},{3,2},{4,5},{5,4},{6,7},{7,6},{8,9},{9,8},{10,11... | collective-permute-start | bytes 1032200 | tf_op jit(solution)/shard_map/ppermute | solution.py:625
  29.7 5.5 %collective-permute-start.5 = (f32[168,256]{1,0:T(8,128)S(1)}, f32[168,256]{1,0:T(8,128)S(1)}, u32[]{:S(2)}, u32[]{:S(2)}) collective-permute-start(f32[168,256]{1,0:T(8,128)S(1)} %slice.17), channel_id=1, source_target_pairs={{0,2},{1,5},{2,0},{3,7},{4,6},{5,1},{6,4},{7,3},{8,10},{9,13},{10,... | collective-permute-start | bytes 516104 | tf_op jit(solution)/shard_map/ppermute | solution.py:625
  30.8 1.3 %collective-permute-start.12 = (bf16[256,256]{1,0:T(8,128)(2,1)S(1)}, bf16[256,256]{1,0:T(8,128)(2,1)S(1)}, u32[]{:S(2)}, u32[]{:S(2)}) collective-permute-start(bf16[256,256]{1,0:T(8,128)(2,1)S(1)} %get-tuple-element.55.residual_ref), channel_id=1, source_target_pairs={{0,1},{1,0},{2,3},{3,2},{4,5},{5,4},{6,7},{7,6},{8,9},{9,8},{10,11... | collective-permute-start | bytes 393224 | tf_op jit(solution)/shard_map/ppermute | solution.py:625
  30.8 1.5 %collective-permute-start.11 = (bf16[256,256]{1,0:T(8,128)(2,1)S(1)}, bf16[256,256]{1,0:T(8,128)(2,1)S(1)}, u32[]{:S(2)}, u32[]{:S(2)}) collective-permute-start(bf16[256,256]{1,0:T(8,128)(2,1)S(1)} %get-tuple-element.54.image_ref), channel_id=1, source_target_pairs={{0,1},{1,0},{2,3},{3,2},{4,5},{5,4},{6,7},{7,6},{8,9},{9,8},{10,11... | collective-permute-start | bytes 393224 | tf_op jit(solution)/shard_map/ppermute | solution.py:625
  32.8 6.3 %collective-permute-start.13 = (bf16[256,256]{1,0:T(8,128)(2,1)S(1)}, bf16[256,256]{1,0:T(8,128)(2,1)S(1)}, u32[]{:S(2)}, u32[]{:S(2)}) collective-permute-start(bf16[256,256]{1,0:T(8,128)(2,1)S(1)} %pair_up.1.current_ref), channel_id=1, source_target_pairs={{0,2},{1,3},{2,0},{3,1},{4,6},{5,7},{6,4},{7,5},{8,10},{9,11},{10,... | collective-permute-start | bytes 393224 | tf_op jit(solution)/shard_map/ppermute | solution.py:625
  35.2 10.3 %collective-permute-start.6 = (f32[168,256]{1,0:T(8,128)S(1)}, f32[168,256]{1,0:T(8,128)S(1)}, u32[]{:S(2)}, u32[]{:S(2)}) collective-permute-start(f32[168,256]{1,0:T(8,128)S(1)} %slice_add_fusion), channel_id=1, source_target_pairs={{0,8},{1,9},{2,10},{3,11},{4,12},{5,13},{6,14},{7,15},{8,0},{9,1},... | collective-permute-start | bytes 516104 | tf_op jit(solution)/shard_map/ppermute | solution.py:625
  39.3 8.2 %collective-permute-start.14 = (bf16[256,256]{1,0:T(8,128)(2,1)S(1)}, bf16[256,256]{1,0:T(8,128)(2,1)S(1)}, u32[]{:S(2)}, u32[]{:S(2)}) collective-permute-start(bf16[256,256]{1,0:T(8,128)(2,1)S(1)} %up.8.current_ref), channel_id=1, source_target_pairs={{0,4},{1,5},{2,6},{3,7},{4,0},{5,1},{6,2},{7,3},{8,12},{9,13},{10,... | collective-permute-start | bytes 393224 | tf_op jit(solution)/shard_map/ppermute | solution.py:625
  45.5 6.8 %collective-permute-start.7 = (f32[168,256]{1,0:T(8,128)S(1)}, f32[168,256]{1,0:T(8,128)S(1)}, u32[]{:S(2)}, u32[]{:S(2)}) collective-permute-start(f32[168,256]{1,0:T(8,128)S(1)} %add.22), channel_id=1, source_target_pairs={{0,4},{1,3},{2,6},{3,1},{4,0},{5,7},{6,2},{7,5},{8,12},{9,11},{10,... | collective-permute-start | bytes 516104 | tf_op jit(solution)/shard_map/ppermute | solution.py:625
  47.8 8.5 %collective-permute-start.15 = (bf16[256,256]{1,0:T(8,128)(2,1)S(1)}, bf16[256,256]{1,0:T(8,128)(2,1)S(1)}, u32[]{:S(2)}, u32[]{:S(2)}) collective-permute-start(bf16[256,256]{1,0:T(8,128)(2,1)S(1)} %up.9), channel_id=1, source_target_pairs={{0,8},{1,9},{2,10},{3,11},{4,12},{5,13},{6,14},{7,15},{8,0},{9,1},... | collective-permute-start | bytes 393224 | tf_op jit(solution)/shard_map/ppermute | solution.py:625
  52.3 5.5 %collective-permute-start.8 = (f32[168,256]{1,0:T(8,128)S(1)}, f32[168,256]{1,0:T(8,128)S(1)}, u32[]{:S(2)}, u32[]{:S(2)}) collective-permute-start(f32[168,256]{1,0:T(8,128)S(1)} %add.23.own_ref), channel_id=1, source_target_pairs={{0,2},{1,5},{2,0},{3,7},{4,6},{5,1},{6,4},{7,3},{8,10},{9,13},{10,... | collective-permute-start | bytes 516104 | tf_op jit(solution)/shard_map/ppermute | solution.py:625
  53.4 4.4 %collective-permute-start.16 = (bf16[256,256]{1,0:T(8,128)(2,1)S(1)}, bf16[256,256]{1,0:T(8,128)(2,1)S(1)}, u32[]{:S(2)}, u32[]{:S(2)}) collective-permute-start(bf16[256,256]{1,0:T(8,128)(2,1)S(1)} %collective-permute-done.13.sibling_ref.refs_4_), channel_id=1, source_target_pairs={{0,1},{1,0},{2,3},{3,2},{4,5},{5,4},{6,7},{7,6},{8,9},{9,8},{10,11... | collective-permute-start | bytes 393224 | tf_op jit(solution)/shard_map/ppermute | solution.py:625
  53.4 4.4 %collective-permute-start.17 = (bf16[256,256]{1,0:T(8,128)(2,1)S(1)}, bf16[256,256]{1,0:T(8,128)(2,1)S(1)}, u32[]{:S(2)}, u32[]{:S(2)}) collective-permute-start(bf16[256,256]{1,0:T(8,128)(2,1)S(1)} %collective-permute-done.14.sibling_ref.refs_5_), channel_id=1, source_target_pairs={{0,1},{1,0},{2,3},{3,2},{4,5},{5,4},{6,7},{7,6},{8,9},{9,8},{10,11... | collective-permute-start | bytes 393224 | tf_op jit(solution)/shard_map/ppermute | solution.py:625
  56.3 1.5 %collective-permute-start.18 = (bf16[256,256]{1,0:T(8,128)(2,1)S(1)}, bf16[256,256]{1,0:T(8,128)(2,1)S(1)}, u32[]{:S(2)}, u32[]{:S(2)}) collective-permute-start(bf16[256,256]{1,0:T(8,128)(2,1)S(1)} %collective-permute-done.15.refs_6_), channel_id=1, source_target_pairs={{0,1},{1,0},{2,3},{3,2},{4,5},{5,4},{6,7},{7,6},{8,9},{9,8},{10,11... | collective-permute-start | bytes 393224 | tf_op jit(solution)/shard_map/ppermute | solution.py:625
  56.3 4.1 %collective-permute-start.9 = (f32[168,256]{1,0:T(8,128)S(1)}, f32[168,256]{1,0:T(8,128)S(1)}, u32[]{:S(2)}, u32[]{:S(2)}) collective-permute-start(f32[168,256]{1,0:T(8,128)S(1)} %add.23.own_ref), channel_id=1, source_target_pairs={{0,1},{1,0},{2,3},{3,2},{4,5},{5,4},{6,7},{7,6},{8,9},{9,8},{10,11... | collective-permute-start | bytes 516104 | tf_op jit(solution)/shard_map/ppermute | solution.py:625
  57.8 2.5 %collective-permute-start.10 = (f32[168,256]{1,0:T(8,128)S(1)}, f32[168,256]{1,0:T(8,128)S(1)}, u32[]{:S(2)}, u32[]{:S(2)}) collective-permute-start(f32[168,256]{1,0:T(8,128)S(1)} %collective-permute-done.8.side_ref), channel_id=1, source_target_pairs={{0,1},{1,0},{2,3},{3,2},{4,5},{5,4},{6,7},{7,6},{8,9},{9,8},{10,11... | collective-permute-start | bytes 516104 | tf_op jit(solution)/shard_map/ppermute | solution.py:625
  82.4 1.7 %collective-permute-start.19 = (f32[208,256]{1,0:T(8,128)S(1)}, f32[208,256]{1,0:T(8,128)S(1)}, u32[]{:S(2)}, u32[]{:S(2)}) collective-permute-start(f32[208,256]{1,0:T(8,128)S(1)} %get-tuple-element.59), channel_id=1, source_target_pairs={{0,1},{1,0},{2,3},{3,2},{4,5},{5,4},{6,7},{7,6},{8,9},{9,8},{10,11... | collective-permute-start | bytes 638984 | tf_op jit(solution)/shard_map/ppermute | solution.py:625
  84.1 4.8 %collective-permute-start.20 = (f32[104,256]{1,0:T(8,128)S(1)}, f32[104,256]{1,0:T(8,128)S(1)}, u32[]{:S(2)}, u32[]{:S(2)}) collective-permute-start(f32[104,256]{1,0:T(8,128)S(1)} %slice.19), channel_id=1, source_target_pairs={{0,2},{1,5},{2,0},{3,7},{4,6},{5,1},{6,4},{7,3},{8,10},{9,13},{10,... | collective-permute-start | bytes 319496 | tf_op jit(solution)/shard_map/ppermute | solution.py:625
  88.9 14.7 %collective-permute-start.21 = (f32[104,256]{1,0:T(8,128)S(1)}, f32[104,256]{1,0:T(8,128)S(1)}, u32[]{:S(2)}, u32[]{:S(2)}) collective-permute-start(f32[104,256]{1,0:T(8,128)S(1)} %slice_add_fusion.1.left_ref), channel_id=1, source_target_pairs={{0,8},{1,9},{2,10},{3,11},{4,12},{5,13},{6,14},{7,15},{8,0},{9,1},... | collective-permute-start | bytes 319496 | tf_op jit(solution)/shard_map/ppermute | solution.py:625
  89.4 16.9 %copy-start.5 = (f32[1024,256]{1,0:T(8,128)S(1)}, f32[1024,256]{1,0:T(8,128)}, u32[]{:S(2)}) copy-start(f32[1024,256]{1,0:T(8,128)} %solution_ref.1) | copy-start | bytes 3145732
  103.6 5.4 %collective-permute-start.22 = (f32[104,256]{1,0:T(8,128)S(1)}, f32[104,256]{1,0:T(8,128)S(1)}, u32[]{:S(2)}, u32[]{:S(2)}) collective-permute-start(f32[104,256]{1,0:T(8,128)S(1)} %add.28.left_ref), channel_id=1, source_target_pairs={{0,4},{1,3},{2,6},{3,1},{4,0},{5,7},{6,2},{7,5},{8,12},{9,11},{10,... | collective-permute-start | bytes 319496 | tf_op jit(solution)/shard_map/ppermute | solution.py:625
  109.0 4.8 %collective-permute-start.23 = (f32[104,256]{1,0:T(8,128)S(1)}, f32[104,256]{1,0:T(8,128)S(1)}, u32[]{:S(2)}, u32[]{:S(2)}) collective-permute-start(f32[104,256]{1,0:T(8,128)S(1)} %add.29.own_ref), channel_id=1, source_target_pairs={{0,2},{1,5},{2,0},{3,7},{4,6},{5,1},{6,4},{7,3},{8,10},{9,13},{10,... | collective-permute-start | bytes 319496 | tf_op jit(solution)/shard_map/ppermute | solution.py:625
  110.2 3.6 %collective-permute-start.24 = (f32[104,256]{1,0:T(8,128)S(1)}, f32[104,256]{1,0:T(8,128)S(1)}, u32[]{:S(2)}, u32[]{:S(2)}) collective-permute-start(f32[104,256]{1,0:T(8,128)S(1)} %add.29.own_ref), channel_id=1, source_target_pairs={{0,1},{1,0},{2,3},{3,2},{4,5},{5,4},{6,7},{7,6},{8,9},{9,8},{10,11... | collective-permute-start | bytes 319496 | tf_op jit(solution)/shard_map/ppermute | solution.py:625
  113.8 1.3 collective-permute-start.25
  (4 other events, 10.1 us)

commit v5 on v4

--- a/solution.py
+++ b/solution.py
@@ -74,8 +74,8 @@
     coef_ref[...] = coef.astype(BF16)
 
 
-def hold_kernel(value_ref, held_ref):
-    held_ref[...] = value_ref[...]
+def hold_kernel(value_ref, *rest):
+    rest[-1][...] = value_ref[...]
 
 
 def block_kernel(points_ref, order_ref, after_ref, block_ref, padded, column_ref):
@@ -121,7 +121,7 @@
     return high, low
 
 
-def prepare_kernel(direction_ref, residual_ref, high_ref, low_ref, gram_ref):
+def prepare_kernel(direction_ref, residual_ref, after_ref, high_ref, low_ref, gram_ref):
     size = direction_ref.shape[1]
     turned_splits(direction_ref[...], high_ref, low_ref, 0)
     high, low = turned_splits(residual_ref[...], high_ref, low_ref, size)
@@ -139,6 +139,19 @@
     coef_ref[...] = (
         dot_t(mine, current_ref[...]) + dot_t(other, sibling_ref[...])
     ).astype(BF16)
+
+
+def half_up_kernel(position_ref, current_ref, sibling_ref, transfer_ref, *rest):
+    whole, coef_ref = rest[-1], rest[-2]
+    up_kernel(0, position_ref, current_ref, sibling_ref, transfer_ref, whole)
+    half = coef_ref.shape[1]
+    value = whole[...]
+    odd = (position_ref[0] & 1) == 1
+    coef_ref[...] = jnp.where(odd, value[:, half:], value[:, :half])
+
+
+def joined(odd, own, other):
+    return jnp.concatenate([jnp.where(odd, other, own), jnp.where(odd, own, other)], 1)
 
 
 def pack_pair(first, second):
@@ -216,6 +229,36 @@
 
 
 def factor_kernel(
+    high_ref,
+    low_ref,
+    basis_ref,
+    skel_ref,
+    after_ref,
+    both_high_out,
+    both_low_out,
+    picked_out,
+    ties_high_out,
+    ties_low_out,
+    basis_picked_out,
+    coef_out,
+):
+    count, rank = basis_ref.shape
+    high, low = high_ref[...], low_ref[...]
+    size = high.shape[0] // 2
+    basis = basis_ref[...]
+    places, picks = skeleton_columns(skel_ref, count), skeleton_rows(skel_ref, count)
+    picked = dot(high, places) + dot(low, places)
+    picked_out[...] = picked.astype(BF16)
+    both = picked + (dot(high, basis) + dot(low, basis))
+    both_high_out[...], both_low_out[...] = split(both)
+    coef_out[...] = both[size:].T.astype(BF16)
+    basis_picked = dot(picks, basis)
+    basis_picked_out[...] = basis_picked.astype(BF16)
+    ties = dot_t(basis, basis) + (basis_picked + basis_picked.T)
+    ties_high_out[...], ties_low_out[...] = split(ties)
+
+
+def near_factor_kernel(
     near_ref,
     high_ref,
     low_ref,
@@ -223,69 +266,53 @@
     skel_ref,
     near_gram_out,
     near_square_out,
-    both_high_out,
-    both_low_out,
-    picked_out,
     near_both_out,
     near_picked_out,
-    ties_high_out,
-    ties_low_out,
-    basis_picked_out,
-    coef_out,
 ):
     count, size = near_ref.shape
     near_high, near_low = split(near_ref[...])
     near_parts = jnp.concatenate([near_high, near_low], 1)
-    high, low = high_ref[...], low_ref[...]
-    basis = basis_ref[...]
-    places, picks = skeleton_columns(skel_ref, count), skeleton_rows(skel_ref, count)
-    wide = dot(high, near_parts)
-    near_gram_out[...] = wide[:, :size] + (wide[:, size:] + dot(low, near_high))
+    wide = dot(high_ref[...], near_parts)
+    near_gram_out[...] = wide[:, :size] + (wide[:, size:] + dot(low_ref[...], near_high))
     wide = dot_t(near_high, near_parts)
     cross = wide[:, size:]
     near_square_out[...] = wide[:, :size] + (cross + cross.T)
-    picked = dot(high, places) + dot(low, places)
-    picked_out[...] = picked.astype(BF16)
-    both = picked + (dot(high, basis) + dot(low, basis))
-    both_high_out[...], both_low_out[...] = split(both)
-    coef_out[...] = both[size:].T.astype(BF16)
-    rank = basis.shape[1]
-    wide = dot(picks, jnp.concatenate([near_parts, basis], 1))
-    near_picked = wide[:, :size] + wide[:, size : 2 * size]
-    basis_picked = wide[:, 2 * size :]
+    wide = dot(skeleton_rows(skel_ref, count), near_parts)
+    near_picked = wide[:, :size] + wide[:, size:]
     near_picked_out[...] = near_picked
-    basis_picked_out[...] = basis_picked.astype(BF16)
-    wide = dot_t(basis, jnp.concatenate([near_parts, basis], 1))
-    near_both_out[...] = near_picked + (wide[:, :size] + wide[:, size : 2 * size])
-    ties = wide[:, 2 * size :] + (basis_picked + basis_picked.T)
-    ties_high_out[...], ties_low_out[...] = split(ties)
+    wide = dot_t(basis_ref[...], near_parts)
+    near_both_out[...] = near_picked + (wide[:, :size] + wide[:, size:])
 
 
 def down_kernel(levels, *refs):
     position_ref = refs[0]
-    siblings = [ref[...] for ref in refs[1 : 1 + levels]]
+    odd = (position_ref[0] & 1) == 1
+    siblings = [refs[1][...]]
+    for at in range(2, 1 + levels):
+        siblings.append(joined(odd, refs[at][...], refs[at + levels - 1][...]))
     (
         coupling_ref,
         transfer_ref,
         near_gram_ref,
         near_square_ref,
+        near_both_ref,
+        near_picked_ref,
         both_high_ref,
         both_low_ref,
         picked_ref,
-        near_both_ref,
-        near_picked_ref,
         ties_high_ref,
         ties_low_ref,
         basis_picked_ref,
         gram_ref,
         down_out,
         coef_out,
+        image_both_out,
         keep_ref,
         send_ref,
         mixed_out,
         images_out,
         payload,
-    ) = refs[1 + levels :]
+    ) = refs[2 * levels :]
     size = gram_ref.shape[1]
     position = position_ref[0]
     high, low = down_chain(position, levels, coupling_ref, transfer_ref, siblings)
@@ -296,6 +323,7 @@
     change = change + (dot_t(basis_picked_ref[...], low) + down)
     near_both = near_both_ref[...]
     coef_out[...] = (near_both + change).astype(BF16)
+    image_both_out[0], image_both_out[1] = split(near_both + change)
     half_high, half_low = split(near_both + 0.5 * change)
     other = (near_picked_ref[...] + 0.5 * picked).astype(BF16)
     half = dot_t(high, half_high) + (dot_t(high, half_low) + dot_t(low, other))
@@ -344,27 +372,80 @@
         near_ref[at] = 2.0 * value + (dot(block, high) + dot(block, low))
 
 
+def pair_cross_kernel(near_ref, image_ref, high_ref, low_ref, after_ref, cross_out):
+    size = image_ref.shape[1]
+    near_high, near_low = split(jnp.concatenate([near_ref[0], near_ref[1]], 1))
+    high, low = high_ref[size:, :], low_ref[size:, :]
+    cross_out[0:size, :] = dot(high, near_high) + (dot(high, near_low) + dot(low, near_high))
+    high, low = split(image_ref[...])
+    cross_out[size:, :] = dot_t(high, near_high) + (dot_t(high, near_low) + dot_t(low, near_high))
+
+
+def pair_square_kernel(near_ref, basis_ref, skel_ref, after_ref, square_out, both_out):
+    width = 2 * near_ref.shape[2]
+    high, low = split(jnp.concatenate([near_ref[0], near_ref[1]], 1))
+    parts = jnp.concatenate([high, low], 1)
+    wide = dot_t(high, parts)
+    cross = wide[:, width:]
+    square_out[...] = wide[:, :width] + (cross + cross.T)
+    wide = dot_t(basis_ref[...], parts) + dot(skeleton_rows(skel_ref, near_ref.shape[1]), parts)
+    both_out[...] = wide[:, :width] + wide[:, width:]
+
+
 def pair_down_kernel(levels, *refs):
-    position_ref, near_ref, image_ref, residual_ref = refs[:4]
-    own_refs, other_refs = refs[4 : 3 + levels], refs[3 + levels : 2 + 2 * levels]
-    coupling_ref, transfer_ref, basis_ref, skel_ref, applied_ref = refs[2 + 2 * levels :]
-    _, count, size = near_ref.shape
+    position_ref, image_other, residual_other = refs[:3]
+    own_refs, other_refs = refs[3 : 2 + levels], refs[2 + levels : 1 + 2 * levels]
+    (
+        coupling_ref,
+        transfer_ref,
+        cross_ref,
+        square_ref,
+        near_both_ref,
+        both_high_ref,
+        both_low_ref,
+        image_both_ref,
+        ties_high_ref,
+        ties_low_ref,
+        mixed_ref,
+        images_ref,
+        down_out,
+        alpha_out,
+        base_out,
+        beta_out,
+    ) = refs[1 + 2 * levels :]
+    size = mixed_ref.shape[0]
     position = position_ref[0]
-    core = position & 1
-    swap = core == 1
-    left, right = image_ref[...], residual_ref[...]
-    siblings = [
-        jnp.concatenate([jnp.where(swap, right, left), jnp.where(swap, left, right)], 1)
-    ]
+    odd = (position & 1) == 1
+    siblings = [jnp.concatenate([image_other[...], residual_other[...]], 1)]
     for own_ref, other_ref in zip(own_refs, other_refs):
-        siblings.append(jnp.concatenate([own_ref[...], other_ref[...]], 1))
+        siblings.append(joined(odd, own_ref[...], other_ref[...]))
     high, low = down_chain(position, levels, coupling_ref, transfer_ref, siblings)
-    places = skeleton_columns(skel_ref, count)
-    spread = (dot(basis_ref[...], high) + dot(basis_ref[...], low)) + (
-        dot(places, high) + dot(places, low)
-    )
-    applied_ref[core] = near_ref[core] + spread[:, :size]
-    applied_ref[1 - core] = near_ref[1 - core] + spread[:, size:]
+    down_out[0], down_out[1] = high, low
+
+    def by(matrix_dot, first_high, first_low):
+        return matrix_dot(first_high, high) + (
+            matrix_dot(first_low, high) + matrix_dot(first_high, low)
+        )
+
+    residual_row = cross_ref[0:size, :] + by(dot, both_high_ref[size:, :], both_low_ref[size:, :])
+    image_row = cross_ref[size:, :] + by(dot_t, image_both_ref[0], image_both_ref[1])
+    tied = by(dot, ties_high_ref[...], ties_low_ref[...])
+    tied = tied + (high.astype(F32) + low.astype(F32))
+    half_high, half_low = split(near_both_ref[...] + 0.5 * tied)
+    half = dot_t(high, half_high) + (dot_t(high, half_low) + dot_t(low, half_high))
+    square = square_ref[...] + (half + half.T)
+    alpha_out[0:size, :] = residual_row[:, :size]
+    alpha_out[size : 2 * size, :] = image_row[:, :size]
+    alpha_out[2 * size : 3 * size, :] = square[size:, :size]
+    alpha_out[3 * size :, :] = square[:size, :size]
+    base_out[0:size, :] = residual_row[:, size:]
+    base_out[size : 2 * size, :] = image_row[:, size:]
+    base_out[2 * size : 3 * size, :] = square[size:, size:]
+    base_out[3 * size :, :] = square[:size, size:]
+    beta_out[0:size, :] = mixed_ref[...]
+    beta_out[size : 2 * size, :] = images_ref[...]
+    beta_out[2 * size : 3 * size, :] = image_row[:, size:].T
+    beta_out[3 * size :, :] = image_row[:, :size].T
 
 
 def scaled_problem(matrix):
@@ -437,10 +518,10 @@
         payload[pl.ds(start, quarter), :] = ref[...]
 
 
-def fresh_gram(res_gram, mixed, images, alpha):
-    bend = dot3(alpha.T, dot3(images, alpha))
-    change = 0.5 * bend - dot3(mixed, alpha)
-    return res_gram + (change + change.T)
+def beta_of(alpha, weighted, mixed_turned, inverse, scale, solved_mixed):
+    eye = jnp.where(eye_mask(alpha.shape[0]), 1.0, 0.0)
+    rest = dot3(inverse, (weighted - mixed_turned) * scale) * scale
+    return (eye - dot3(solved_mixed, alpha)) + rest
 
 
 def first_kernel(
@@ -449,13 +530,9 @@
     side_ref,
     core_ref,
     far_ref,
-    image_ref,
-    residual_ref,
-    applied_ref,
-    local_mixed_ref,
-    local_images_ref,
-    partial_out,
-    residual_out,
+    alpha_part_ref,
+    base_part_ref,
+    beta_part_ref,
     keep_out,
     send_out,
     alpha_out,
@@ -468,7 +545,7 @@
     later,
     store,
 ):
-    size = image_ref.shape[1]
+    size = own_ref.shape[1]
     position = position_ref[0]
     collect(position, own_ref, side_ref, core_ref, far_ref, payload)
     mixed = payload[size : 2 * size, :]
@@ -477,33 +554,19 @@
     curvature, res_gram = unpack_pair(payload[0:size, :], payload[base + 1 : base + 2, :])
     (first, first_scale), (second, second_scale) = inverses([curvature, res_gram], 3, store)
     alpha = dot3(first, res_gram * first_scale) * first_scale
-    fresh = fresh_gram(res_gram, mixed, images, alpha)
-    beta = dot3(second, fresh * second_scale) * second_scale
-    old_image = image_ref[...]
-    residual = residual_ref[...] - dot3(old_image, alpha)
-    partial = applied_ref[1] - dot3(applied_ref[0], alpha)
-    residual_out[...] = residual
-    partial_out[...] = partial
-    partial_high, partial_low = split(partial)
-    old_high, old_low = split(old_image)
-    residual_high, residual_low = split(residual)
-    both = jnp.concatenate([partial_high, partial_low], 1)
-    wide = dot_t(residual_high, both)
-    cross_gram = wide[:, :size] + (wide[:, size:] + dot_t(residual_low, partial_high))
-    wide = dot_t(partial_high, jnp.concatenate([both, old_high, old_low], 1))
-    cross = wide[:, size : 2 * size]
-    square = wide[:, :size] + (cross + cross.T)
-    old_gram = wide[:, 2 * size : 3 * size] + wide[:, 3 * size :]
-    old_gram = old_gram + dot_t(partial_low, old_high)
-    local_images = local_images_ref[...]
-    old_cross = local_mixed_ref[...] - dot3(alpha.T, local_images)
-    cross_gram = cross_gram + dot3(old_cross, beta)
-    half = dot3(old_gram, beta) + 0.5 * dot3(beta.T, dot3(local_images, beta))
-    packed, tail = pack_half(square + (half + half.T))
-    write_parts(position, [cross_gram, packed], [tail], later, keep_out, send_out)
+    solved_mixed = dot3(second, mixed * second_scale) * second_scale
+    weighted = dot3(images, alpha)
+    beta = beta_of(alpha, weighted, mixed.T, first, first_scale, solved_mixed)
+    rows = (base_part_ref[...] - dot3(alpha_part_ref[...], alpha)) + dot3(beta_part_ref[...], beta)
+    image_row = rows[size : 2 * size]
+    turned = dot3(alpha.T, jnp.concatenate([image_row, rows[3 * size :]], 1))
+    square = rows[2 * size : 3 * size] - turned[:, size:] + dot3(beta.T, image_row)
+    packed, tail = pack_half(square)
+    write_parts(position, [rows[:size] - turned[:, :size], packed], [tail], later, keep_out, send_out)
+    change = 0.5 * dot3(alpha.T, weighted) - dot3(mixed, alpha)
+    fresh_out[...] = res_gram + (change + change.T)
     alpha_out[...] = alpha
     beta_out[...] = beta
-    fresh_out[...] = fresh
     mixed_out[...] = mixed
     images_out[...] = images
     curvature_out[...] = curvature
@@ -533,18 +596,31 @@
     residual_ref,
     direction_ref,
     solution_ref,
-    partial_ref,
     image_ref,
+    near_ref,
+    down_ref,
+    basis_ref,
+    skel_ref,
     alpha_ref,
     beta_ref,
+    residual_out,
     direction_out,
     solution_out,
     image_out,
 ):
-    direction, beta = direction_ref[...], beta_ref[...]
-    direction_out[...] = residual_ref[...] + dot3(direction, beta)
-    solution_out[...] = solution_ref[...] + dot3(direction, alpha_ref[...])
-    image_out[...] = partial_ref[...] + dot3(image_ref[...], beta)
+    count, size = image_ref.shape
+    direction, image = direction_ref[...], image_ref[...]
+    alpha, beta = alpha_ref[...], beta_ref[...]
+    residual = residual_ref[...] - dot3(image, alpha)
+    residual_out[...] = residual
+    direction_out[...] = residual + dot3(direction, beta)
+    solution_out[...] = solution_ref[...] + dot3(direction, alpha)
+    down = down_ref[0].astype(F32) + down_ref[1].astype(F32)
+    high, low = split(down[:, size:] - dot3(down[:, :size], alpha))
+    places, basis = skeleton_columns(skel_ref, count), basis_ref[...]
+    far = (dot(basis, high) + dot(basis, low)) + (dot(places, high) + dot(places, low))
+    near = near_ref[1] - dot3(near_ref[0], alpha)
+    image_out[...] = (near + far) + dot3(image, beta)
 
 
 def last_kernel(
@@ -577,6 +653,9 @@
     images = unpack_half(payload[size:base, :], payload[base : base + 1, :])
     res_gram = fresh_ref[...]
     curvature = 0.5 * (mixed + mixed.T) + turn_ref[...]
+    picked = jnp.where(eye_mask(size), res_gram, 0.0)
+    column_scale = lax.rsqrt(jnp.sum(picked, axis=1, keepdims=True))
+    solved_mixed = dot3(inverse_ref[...], mixed * column_scale)
     ((first, scale),) = inverses([curvature], 4, store)
     alpha = dot3(first, res_gram * scale) * scale
     residual_held[...] = residual_ref[...] - dot3(image_ref[...], alpha)
@@ -585,10 +664,7 @@
     solution_held[...] = solution_ref[...] + dot3(direction_ref[...], alpha)
     copies.append(pltpu.make_async_copy(solution_held, solution_out, sems.at[1]))
     copies[1].start()
-    fresh = fresh_gram(res_gram, mixed, images, alpha)
-    picked = jnp.where(eye_mask(size), res_gram, 0.0)
-    column_scale = lax.rsqrt(jnp.sum(picked, axis=1, keepdims=True))
-    beta = dot3(inverse_ref[...], fresh * column_scale)
+    beta = beta_of(alpha, dot3(images, alpha), mixed.T, first, scale, solved_mixed)
     strip = count // 4
     for at in range(4):
         rows = pl.ds(at * strip, strip)
@@ -636,13 +712,13 @@
     return call(add_kernel, "add", [left, right, *after], [result], micros=0.2, unused=len(after))[0]
 
 
-def summed(keep, send, levels, afters=((), ())):
+def summed(keep, send, levels, afters=((), (), ())):
     quarter = keep.shape[0] // 2
     half = keep + swapped(send, 0)
-    own = half[:quarter] + swapped(half[quarter:], 1, 2)
+    own = plus(half[:quarter], swapped(half[quarter:], 1, 2), afters[0])
     for level in range(3, levels):
-        own = plus(own, swapped(own, level), afters[0] if level == 3 else ())
-    own = plus(own, swapped(own, 2, 1), afters[1])
+        own = plus(own, swapped(own, level), afters[1] if level == 3 else ())
+    own = plus(own, swapped(own, 2, 1), afters[2])
     side = swapped(own, 1, 2)
     return [own, side, swapped(own, 0), swapped(side, 0)]
 
@@ -665,7 +741,7 @@
             functools.partial(up_kernel, level),
             "up",
             [position, current, sibling, transfer, *extra],
-            [coef],
+            [(current.shape, BF16)],
             micros=0.3,
             unused=len(extra),
         )
@@ -677,7 +753,14 @@
     )
     siblings = [swapped(current, 0)]
     (current,) = call(hold_kernel, "hold", [current], [coef], micros=0.5)
-    current = up(0, current, siblings[0])
+    (current,) = call(
+        half_up_kernel,
+        "up",
+        [position, current, siblings[0], transfer],
+        [((rank, size // 2), BF16)],
+        [pltpu.VMEM((rank, size), BF16)],
+        micros=0.3,
+    )
     siblings.append(swapped(current, 1))
     (block,) = call(
         block_kernel,
@@ -688,41 +771,58 @@
         micros=3.6,
         unused=1,
     )
-    (near,) = call(near_kernel, "near", [block, direction], [tall], micros=0.7)
     high, low, gram = call(
         prepare_kernel,
         "prepare",
-        [direction, residual],
+        [direction, residual, current],
         [((2 * size, count), BF16), ((2 * size, count), BF16), square],
         micros=0.8,
-    )
-    afters = {1: [block], 2: [near, high]}
-    for level in range(1, levels - 1):
-        current = up(level, current, siblings[level], afters.get(level, ()))
-        siblings.append(swapped(current, level + 1))
-    double, double_low = ((2 * size, rank), F32), ((2 * size, rank), BF16)
+        unused=1,
+    )
+    current = up(1, current, siblings[1], [block, high])
+    siblings.append(swapped(current, 2))
+    (near,) = call(near_kernel, "near", [block, direction], [tall], micros=0.7)
+    double_low = ((2 * size, rank), BF16)
     factors = call(
         factor_kernel,
         "factor",
+        [high, low, basis, skeleton, current],
+        [double_low] * 3 + [((rank, rank), BF16)] * 3 + [coef],
+        micros=1.8,
+        unused=1,
+    )
+    residual_coef = factors[-1]
+    for level in range(2, levels - 1):
+        extra = [near, residual_coef] if level == 2 else ()
+        current = up(level, current, siblings[level], extra)
+        siblings.append(swapped(current, level + 1))
+    near_factors = call(
+        near_factor_kernel,
+        "near_factor",
         [near, high, low, basis, skeleton],
-        [((2 * size, size), F32), square, double_low, double_low, double_low]
-        + [((rank, size), F32), ((rank, size), F32)]
-        + [((rank, rank), BF16)] * 3
-        + [coef],
-        micros=3.0,
-    )
-    residual_coef = factors[-1]
-    down, image_coef, keep, send, local_mixed, local_images = call(
+        [((2 * size, size), F32), square, ((rank, size), F32), ((rank, size), F32)],
+        micros=1.8,
+    )
+    (ready,) = call(
+        hold_kernel,
+        "ready",
+        [siblings[-1], near_factors[0]],
+        [(siblings[-1].shape, BF16)],
+        micros=0.2,
+        unused=1,
+    )
+    siblings += [swapped(value, 0) for value in siblings[1:-1] + [ready]]
+    down, image_coef, image_both, keep, send, local_mixed, local_images = call(
         functools.partial(down_kernel, levels),
         "down",
-        [position, *siblings, coupling, transfer, *factors[:-1], gram],
-        [((2, rank, size), BF16), coef, ((rows // 2, size), F32), ((rows // 2, size), F32)]
+        [position, *siblings, coupling, transfer, *near_factors, *factors[:-1], gram],
+        [((2, rank, size), BF16), coef, ((2, rank, size), BF16)]
+        + [((rows // 2, size), F32)] * 2
         + [square, square],
         [pltpu.VMEM((rows, size), F32)],
         micros=2.0,
     )
 
-    pieces = [position] + summed(keep, send, levels)
     (image,) = call(image_kernel, "image", [near, down, basis, skeleton], [tall], micros=0.7)
     others = [swapped(image_coef, 0), swapped(residual_coef, 0)]
     (current,) = call(
@@ -732,30 +832,57 @@
         [coef],
         micros=0.3,
     )
+    pieces = [position] + summed(keep, send, levels, ((current,), (), ()))
     (near,) = call(
-        pair_near_kernel, "pair_near", [block, image, residual], [tall_pair], micros=2.0
-    )
-    own = []
-    for level in range(1, levels):
-        own.append(swapped(current, level))
-        if level < levels - 1:
-            current = up(level, current, own[-1], [near] if level == 1 else ())
-    other = [swapped(value, 0) for value in own]
-    (applied,) = call(
+        pair_near_kernel,
+        "pair_near",
+        [block, image, residual],
+        [tall_pair],
+        micros=2.4,
+    )
+    own = [swapped(current, 1)]
+    current = up(1, current, own[0], [near])
+    own.append(swapped(current, 2))
+    (cross,) = call(
+        pair_cross_kernel,
+        "pair_cross",
+        [near, image, high, low, current],
+        [((2 * size, 2 * size), F32)],
+        micros=2.3,
+        unused=1,
+    )
+    for level in range(2, levels - 1):
+        current = up(level, current, own[level - 1], [cross] if level == 2 else ())
+        own.append(swapped(current, level + 1))
+    square_part, near_both = call(
+        pair_square_kernel,
+        "pair_square",
+        [near, basis, skeleton, pieces[1]],
+        [((2 * size, 2 * size), F32), ((rank, 2 * size), F32)],
+        micros=2.8,
+        unused=1,
+    )
+    (ready,) = call(
+        hold_kernel, "ready", [own[-1], near_both], [coef], micros=0.2, unused=1
+    )
+    other = [swapped(value, 0) for value in own[:-1] + [ready]]
+    both_high, both_low, _, ties_high, ties_low, _, _ = factors
+    down, alpha_part, base_part, beta_part = call(
         functools.partial(pair_down_kernel, levels),
         "pair_down",
-        [position, near, *others, *own, *other, coupling, transfer, basis, skeleton],
-        [tall_pair],
+        [position, *others, *own, *other, coupling, transfer, cross, square_part, near_both]
+        + [both_high, both_low, image_both, ties_high, ties_low, local_mixed, local_images],
+        [((2, rank, 2 * size), BF16)] + [((4 * size, size), F32)] * 3,
         micros=2.5,
     )
 
-    partial, residual, keep, send, alpha, beta, fresh, mixed, images, curvature = call(
+    keep, send, alpha, beta, fresh, mixed, images, curvature = call(
         first_kernel,
         "first",
-        pieces + [image, residual, applied, local_mixed, local_images],
-        [tall, tall, ((later_rows // 2, size), F32), ((later_rows // 2, size), F32)] + [square] * 6,
+        pieces + [alpha_part, base_part, beta_part],
+        [((later_rows // 2, size), F32), ((later_rows // 2, size), F32)] + [square] * 6,
         [pltpu.VMEM((rows, size), F32), pltpu.VMEM((later_rows, size), F32), work],
-        micros=7.0,
+        micros=5.0,
     )
     inverse, turn = call(
         carry_kernel,
@@ -765,14 +892,14 @@
         [work],
         micros=3.0,
     )
-    direction, solution, image = call(
+    residual, direction, solution, image = call(
         update_kernel,
         "update",
-        [residual, direction, solution, partial, image, alpha, beta],
-        [tall, tall, tall],
-        micros=1.5,
-    )
-    pieces = [position] + summed(keep, send, levels, ((inverse,), (direction,)))
+        [residual, direction, solution, image, near, down, basis, skeleton, alpha, beta],
+        [tall] * 4,
+        micros=3.2,
+    )
+    pieces = [position] + summed(keep, send, levels, ((), (inverse,), (direction,)))
     return tuple(
         call(
             last_kernel,

time: 133 us -> 133 us (level); the launches traced: 132 us -> 134 us
  Pallas kernels: 74.4 us -> 82 us
  waiting for transfers between devices: 30.5 us -> 23.8 us
    pallas_call x22 -> x28, Pallas kernels: 74.4 us -> 82 us  [call(): pl.pallas_call(kernel, name=name, in_specs=specs, out_specs=[ANY if apart...]
    ppermute x26 -> x29, waiting for transfers between devices: 30.5 us -> 23.8 us  [swapped(): return lax.ppermute(value, 'leaf', pairs)]
    ppermute x26 -> x29, starting transfers between devices: 24.5 us -> 25.8 us  [swapped(): return lax.ppermute(value, 'leaf', pairs)]
  transfers between devices with their start and end apart: 26 -> 29, of which waited for: 18 -> 20; matrix products, arithmetic and copies ran while one was open for 0% -> 0% of each run, Pallas kernels for 23% -> 27%
where the time goes in v5:
time: 133 us; the launch traced here: 134 us
  Pallas kernels  82 us (62%)
  starting transfers between devices  25.8 us (19%)
  waiting for transfers between devices  23.8 us (18%)
    pallas_call x28, Pallas kernels, call(): pl.pallas_call(kernel, name=name, in_specs=specs, out_specs=[ANY if apart...  82 us
    ppermute x29, starting transfers between devices, swapped(): return lax.ppermute(value, 'leaf', pairs)  25.8 us
    ppermute x29, waiting for transfers between devices, swapped(): return lax.ppermute(value, 'leaf', pairs)  23.8 us
  transfers between devices with their start and end apart: 29, of which 20 were waited for; matrix products, arithmetic and copies ran while one was open for 0% of the time, Pallas kernels for 27%

profile of v5, /device:TPU:0, one launch (start us, length us, event | category | flops | bytes accessed | tf_op | source)
XLA Modules:
  0.0 134.1 jit_solution(605582850834535292)
XLA Ops:
  0.6 2.8 %coef.1.value_ref = bf16[256,256]{1,0:T(8,128)(2,1)} custom-call(f32[1024,256]{1,0:T(8,128)} %direction_ref.7, bf16[1024,256]{1,0:T(8,128)(2,1)} %basis_ref.11, s32[1,256]{1,0:T(1,128)} %skel_ref.11), custom_call_target="tpu_custom_call" | custom-call | flops 2969999872 | tf_op jit(solution)/shard_map/coef/pallas_call | solution.py:684
  3.9 1.1 copy-done.7
  5.4 2.9 %collective-permute-start.1 = (bf16[256,128]{1,0:T(8,128)(2,1)S(1)}, bf16[256,128]{1,0:T(8,128)(2,1)S(1)}, u32[]{:S(2)}, u32[]{:S(2)}) collective-permute-start(bf16[256,128]{1,0:T(8,128)(2,1)S(1)} %up.5.after_ref.current_ref), channel_id=1, source_target_pairs={{0,2},{1,3},{2,0},{3,1},{4,6},{5,7},{6,4},{7,5},{8,10},{9,11},{10,... | collective-permute-start | bytes 196616 | tf_op jit(solution)/shard_map/ppermute | solution.py:701
  9.1 3.6 %block.1.rest_0_.block_ref = bf16[1024,1024]{1,0:T(8,128)(2,1)S(1)} custom-call(f32[3,1024]{1,0:T(4,128)S(1)} %copy-done.8, s32[1,1024]{1,0:T(1,128)S(1)} %bitcast.2, bf16[256,128]{1,0:T(8,128)(2,1)S(1)} %up.5.after_ref.current_ref), custom_call_target="tpu_custom_call" | custom-call | flops 3960000000 | tf_op jit(solution)/shard_map/block/pallas_call | solution.py:684
  13.7 1.6 %collective-permute-start.2 = (bf16[256,128]{1,0:T(8,128)(2,1)S(1)}, bf16[256,128]{1,0:T(8,128)(2,1)S(1)}, u32[]{:S(2)}, u32[]{:S(2)}) collective-permute-start(bf16[256,128]{1,0:T(8,128)(2,1)S(1)} %up.6.after_ref.current_ref), channel_id=1, source_target_pairs={{0,4},{1,5},{2,6},{3,7},{4,0},{5,1},{6,2},{7,3},{8,12},{9,13},{10,... | collective-permute-start | bytes 196616 | tf_op jit(solution)/shard_map/ppermute | solution.py:701
  15.4 1.6 %factor.1 = (bf16[512,256]{1,0:T(8,128)(2,1)S(1)}, bf16[512,256]{1,0:T(8,128)(2,1)S(1)}, bf16[512,256]{1,0:T(8,128)(2,1)S(1)}, bf16[256,256]{1,0:T(8,128)(2,1)S(...) custom-call(bf16[512,1024]{1,0:T(8,128)(2,1)S(1)} %get-tuple-element.44.rest_1_.high_re, ...), custom_call_target="tpu_custom_call" | custom-call | flops 1980000000 | tf_op jit(solution)/shard_map/factor/pallas_call | solution.py:684
  17.0 1.1 collective-permute-done.2.sibling_ref.refs_3_
  18.3 2.7 %collective-permute-start.3 = (bf16[256,128]{1,0:T(8,128)(2,1)S(1)}, bf16[256,128]{1,0:T(8,128)(2,1)S(1)}, u32[]{:S(2)}, u32[]{:S(2)}) collective-permute-start(bf16[256,128]{1,0:T(8,128)(2,1)S(1)} %up.7), channel_id=1, source_target_pairs={{0,8},{1,9},{2,10},{3,11},{4,12},{5,13},{6,14},{7,15},{8,0},{9,1},... | collective-permute-start | bytes 196616 | tf_op jit(solution)/shard_map/ppermute | solution.py:701
  21.0 1.8 %near_factor.1 = (f32[512,256]{1,0:T(8,128)S(1)}, f32[256,256]{1,0:T(8,128)S(1)}, f32[256,256]{1,0:T(8,128)S(1)}, f32[256,256]{1,0:T(8,128)S(1)}) custom-call(f32[1024,256]{1,0:T(8,128)S(1)} %near.1.rest_0_.near_ref, bf16[512,1024]{1,0:T(8,128)(2,1)S(1)} %get-tuple-element.44.rest_1_.high_ref, bf16[512,1024]{1,0:T(8,128)(2,1)S(1)} %get-tuple-element.45.low_ref, ...), custom_call_target="tpu_custom_call" | custom-call | flops 1980000000 | tf_op jit(solution)/shard_map/near_factor/pallas_call | solution.py:684
  24.8 2.1 %down.1 = (bf16[2,256,256]{2,1,0:T(8,128)(2,1)S(1)}, bf16[256,256]{1,0:T(8,128)(2,1)S(1)}, bf16[2,256,256]{2,1,0:T(8,128)(2,1)S(1)}, f32[336,256]{1,0:T(8,128)S(...) custom-call(s32[1]{0:T(128)} %bitcast.position_ref.refs_0_, ...), custom_call_target="tpu_custom_call" | custom-call | flops 2200000000 | tf_op jit(solution)/shard_map/down/pallas_call | solution.py:684
  27.2 1.5 %collective-permute-done.7 = f32[336,256]{1,0:T(8,128)S(1)} collective-permute-done((f32[336,256]{1,0:T(8,128)S(1)}, f32[336,256]{1,0:T(8,128)S(1)}, u32[]{:S(2)}, u32[]{:S(2)}) %collective-permute-start.7) | collective-permute-done | bytes 344096 | tf_op jit(solution)/shard_map/ppermute | solution.py:701
  32.9 1.3 collective-permute-done.8.right_ref
  34.3 2.7 %collective-permute-start.11 = (f32[168,256]{1,0:T(8,128)S(1)}, f32[168,256]{1,0:T(8,128)S(1)}, u32[]{:S(2)}, u32[]{:S(2)}) collective-permute-start(f32[168,256]{1,0:T(8,128)S(1)} %add.24), channel_id=1, source_target_pairs={{0,8},{1,9},{2,10},{3,11},{4,12},{5,13},{6,14},{7,15},{8,0},{9,1},... | collective-permute-start | bytes 516104 | tf_op jit(solution)/shard_map/ppermute | solution.py:701
  37.0 2.4 %pair_near.1.rest_0_.near_ref = f32[2,1024,256]{2,1,0:T(8,128)S(1)} custom-call(bf16[1024,1024]{1,0:T(8,128)(2,1)S(1)} %block.1.rest_0_.block_ref, f32[1024,256]{1,0:T(8,128)S(1)} %image.1.image_ref, f32[1024,256]{1,0:T(8,128)S(1)} %copy-done.4), custom_call_target="tpu_custom_call" | custom-call | flops 2640000000 | tf_op jit(solution)/shard_map/pair_near/pallas_call | solution.py:684
  39.7 2.2 %collective-permute-start.17 = (bf16[256,256]{1,0:T(8,128)(2,1)S(1)}, bf16[256,256]{1,0:T(8,128)(2,1)S(1)}, u32[]{:S(2)}, u32[]{:S(2)}) collective-permute-start(bf16[256,256]{1,0:T(8,128)(2,1)S(1)} %up.8.after_ref.current_ref), channel_id=1, source_target_pairs={{0,4},{1,5},{2,6},{3,7},{4,0},{5,1},{6,2},{7,3},{8,12},{9,13},{10,... | collective-permute-start | bytes 393224 | tf_op jit(solution)/shard_map/ppermute | solution.py:701
  41.9 3.1 %collective-permute-done.11 = f32[168,256]{1,0:T(8,128)S(1)} collective-permute-done((f32[168,256]{1,0:T(8,128)S(1)}, f32[168,256]{1,0:T(8,128)S(1)}, u32[]{:S(2)}, u32[]{:S(2)}) %collective-permute-start.11) | collective-permute-done | bytes 172064 | tf_op jit(solution)/shard_map/ppermute | solution.py:701
  45.7 1.8 %pair_cross.1.rest_0_.refs_11_ = f32[512,512]{1,0:T(8,128)S(1)} custom-call(f32[2,1024,256]{2,1,0:T(8,128)S(1)} %pair_near.1.rest_0_.near_ref, f32[1024,256]{1,0:T(8,128)S(1)} %image.1.image_ref, bf16[512,1024]{1,0:T(8,128)(2,1)S(1)} %get-tuple-element.44.rest_1_.high_ref, bf16[512,1024]{1,0:T(8,128)(2,1)S(1)} %get-tuple-element.45.low_ref, ...), custom_call_target="tpu_custom_call" | custom-call | flops 2529999872 | tf_op jit(solution)/shard_map/pair_cross/pallas_call | solution.py:684
  47.9 3.5 %collective-permute-start.18 = (bf16[256,256]{1,0:T(8,128)(2,1)S(1)}, bf16[256,256]{1,0:T(8,128)(2,1)S(1)}, u32[]{:S(2)}, u32[]{:S(2)}) collective-permute-start(bf16[256,256]{1,0:T(8,128)(2,1)S(1)} %up.9), channel_id=1, source_target_pairs={{0,8},{1,9},{2,10},{3,11},{4,12},{5,13},{6,14},{7,15},{8,0},{9,1},... | collective-permute-start | bytes 393224 | tf_op jit(solution)/shard_map/ppermute | solution.py:701
  52.2 2.4 %pair_square.1 = (f32[512,512]{1,0:T(8,128)S(1)}, f32[256,512]{1,0:T(8,128)S(1)}) custom-call(f32[2,1024,256]{2,1,0:T(8,128)S(1)} %pair_near.1.rest_0_.near_ref, bf16[1024,256]{1,0:T(8,128)(2,1)S(1)} %copy-done.2, s32[1,256]{1,0:T(1,128)S(1)} %copy-done.3, f32[168,256]{1,0:T(8,128)S(1)} %add.20.after_ref.own_ref), custom_call_target="tpu_custom_call" | custom-call | flops 3080000000 | tf_op jit(solution)/shard_map/pair_square/pallas_call | solution.py:684
  54.6 1.8 %collective-permute-done.18.value_ref.refs_5_ = bf16[256,256]{1,0:T(8,128)(2,1)S(1)} collective-permute-done((bf16[256,256]{1,0:T(8,128)(2,1)S(1)}, bf16[256,256]{1,0:T(8,128)(2,1)S(1)}, u32[]{:S(2)}, u32[]{:S(2)}) %collective-permute-start.18) | collective-permute-done | bytes 131104 | tf_op jit(solution)/shard_map/ppermute | solution.py:701
  57.8 2.9 %pair_down.1 = (bf16[2,256,512]{2,1,0:T(8,128)(2,1)S(1)}, f32[1024,256]{1,0:T(8,128)S(1)}, f32[1024,256]{1,0:T(8,128)S(1)}, f32[1024,256]{1,0:T(8,128)S(1)}) custom-call(s32[1]{0:T(128)} %bitcast.position_ref.refs_0_, bf16[256,256]{1,0:T(8,128)(2,1)S(1)} %collective-permute-done.9.image_other.refs_1_, ...), custom_call_target="tpu_custom_call" | custom-call | flops 2750000128 | tf_op jit(solution)/shard_map/pair_down/pallas_call | solution.py:684
  60.7 21.9 %first.1 = (f32[208,256]{1,0:T(8,128)S(1)}, f32[208,256]{1,0:T(8,128)S(1)}, f32[256,256]{1,0:T(8,128)S(1)}, f32[256,256]{1,0:T(8,128)S(1)}, f32[256,256]{1,0:T(8...) custom-call(s32[1]{0:T(128)} %bitcast.position_ref.refs_0_, ...), custom_call_target="tpu_custom_call" | custom-call | flops 5500000256 | tf_op jit(solution)/shard_map/first/pallas_call | solution.py:684
  82.8 1.3 collective-permute-done.22
  84.2 1.4 %collective-permute-start.23 = (f32[104,256]{1,0:T(8,128)S(1)}, f32[104,256]{1,0:T(8,128)S(1)}, u32[]{:S(2)}, u32[]{:S(2)}) collective-permute-start(f32[104,256]{1,0:T(8,128)S(1)} %slice.19), channel_id=1, source_target_pairs={{0,2},{1,5},{2,0},{3,7},{4,6},{5,1},{6,4},{7,3},{8,10},{9,13},{10,... | collective-permute-start | bytes 319496 | tf_op jit(solution)/shard_map/ppermute | solution.py:701
  85.6 3.4 %collective-permute-done.23 = f32[104,256]{1,0:T(8,128)S(1)} collective-permute-done((f32[104,256]{1,0:T(8,128)S(1)}, f32[104,256]{1,0:T(8,128)S(1)}, u32[]{:S(2)}, u32[]{:S(2)}) %collective-permute-start.23) | collective-permute-done | bytes 106528 | tf_op jit(solution)/shard_map/ppermute | solution.py:701
  89.0 2.3 %collective-permute-start.24 = (f32[104,256]{1,0:T(8,128)S(1)}, f32[104,256]{1,0:T(8,128)S(1)}, u32[]{:S(2)}, u32[]{:S(2)}) collective-permute-start(f32[104,256]{1,0:T(8,128)S(1)} %slice_add_fusion.left_ref), channel_id=1, source_target_pairs={{0,8},{1,9},{2,10},{3,11},{4,12},{5,13},{6,14},{7,15},{8,0},{9,1},... | collective-permute-start | bytes 319496 | tf_op jit(solution)/shard_map/ppermute | solution.py:701
  91.3 14.1 %carry.1 = (f32[256,256]{1,0:T(8,128)S(1)}, f32[256,256]{1,0:T(8,128)S(1)}) custom-call(f32[256,256]{1,0:T(8,128)S(1)} %get-tuple-element.72.alpha_ref, f32[256,256]{1,0:T(8,128)S(1)} %get-tuple-element.73.beta_ref, f32[256,256]{1,0:T(8,128)S(1)} %get-tuple-element.74.fresh_ref, f32[256,256]{1,0:T(8,128)S(1)} %get-tuple-element.75.mixed_ref, ...), custom_call_target="tpu_custom_call" | custom-call | flops 3300000000 | tf_op jit(solution)/shard_map/carry/pallas_call | solution.py:684
  105.7 3.0 %update.1 = (f32[1024,256]{1,0:T(8,128)S(1)}, f32[1024,256]{1,0:T(8,128)S(1)}, f32[1024,256]{1,0:T(8,128)S(1)}, f32[1024,256]{1,0:T(8,128)S(1)}) custom-call(f32[1024,256]{1,0:T(8,128)S(1)} %copy-done.4, f32[1024,256]{1,0:T(8,128)S(1)} %copy-done.1, f32[1024,256]{1,0:T(8,128)S(1)} %copy-done.5, f32[1024,256]{1,0:T(8,128)S(1)} %image.1.image_ref, ...), custom_call_target="tpu_custom_call" | custom-call | flops 3520000000 | tf_op jit(solution)/shard_map/update/pallas_call | solution.py:684
  108.8 1.5 %collective-permute-done.25.right_ref = f32[104,256]{1,0:T(8,128)S(1)} collective-permute-done((f32[104,256]{1,0:T(8,128)S(1)}, f32[104,256]{1,0:T(8,128)S(1)}, u32[]{:S(2)}, u32[]{:S(2)}) %collective-permute-start.25) | collective-permute-done | bytes 106528 | tf_op jit(solution)/shard_map/ppermute | solution.py:701
  110.9 4.1 %collective-permute-done.26.side_ref = f32[104,256]{1,0:T(8,128)S(1)} collective-permute-done((f32[104,256]{1,0:T(8,128)S(1)}, f32[104,256]{1,0:T(8,128)S(1)}, u32[]{:S(2)}, u32[]{:S(2)}) %collective-permute-start.26) | collective-permute-done | bytes 106528 | tf_op jit(solution)/shard_map/ppermute | solution.py:701
  115.0 1.3 collective-permute-done.28.far_ref
  116.3 17.5 %last.1 = (f32[1024,256]{1,0:T(8,128)}, f32[1024,256]{1,0:T(8,128)}, f32[1024,256]{1,0:T(8,128)}) custom-call(s32[1]{0:T(128)} %bitcast.position_ref.refs_0_, f32[104,256]{1,0:T(8,128)S(1)} %add.26.own_ref, f32[104,256]{1,0:T(8,128)S(1)} %collective-permute-done.26.side_ref, f32[104,256]{1,0:T(8,128)S(1)} %collective-permute-done.27.core_ref, ...), custom_call_target="tpu_custom_call" | custom-call | flops 7699999744 | tf_op jit(solution)/shard_map/last/pallas_call | solution.py:684
  (81 shorter events, 14.1 us)
Async XLA Ops:
  3.4 4.9 %copy-start.4 = (f32[1024,256]{1,0:T(8,128)S(1)}, f32[1024,256]{1,0:T(8,128)}, u32[]{:S(2)}) copy-start(f32[1024,256]{1,0:T(8,128)} %residual_ref.5) | copy-start | bytes 3145732
  3.4 1.7 %collective-permute-start = (bf16[256,256]{1,0:T(8,128)(2,1)}, bf16[256,256]{1,0:T(8,128)(2,1)S(1)}, u32[]{:S(2)}, u32[]{:S(2)}) collective-permute-start(bf16[256,256]{1,0:T(8,128)(2,1)} %coef.1.value_ref), channel_id=1, source_target_pairs={{0,1},{1,0},{2,3},{3,2},{4,5},{5,4},{6,7},{7,6},{8,9},{9,8},{10,11... | collective-permute-start | bytes 393224 | tf_op jit(solution)/shard_map/ppermute | solution.py:701
  5.4 8.0 %collective-permute-start.1 = (bf16[256,128]{1,0:T(8,128)(2,1)S(1)}, bf16[256,128]{1,0:T(8,128)(2,1)S(1)}, u32[]{:S(2)}, u32[]{:S(2)}) collective-permute-start(bf16[256,128]{1,0:T(8,128)(2,1)S(1)} %up.5.after_ref.current_ref), channel_id=1, source_target_pairs={{0,2},{1,3},{2,0},{3,1},{4,6},{5,7},{6,4},{7,5},{8,10},{9,11},{10,... | collective-permute-start | bytes 196616 | tf_op jit(solution)/shard_map/ppermute | solution.py:701
  13.7 4.3 %collective-permute-start.2 = (bf16[256,128]{1,0:T(8,128)(2,1)S(1)}, bf16[256,128]{1,0:T(8,128)(2,1)S(1)}, u32[]{:S(2)}, u32[]{:S(2)}) collective-permute-start(bf16[256,128]{1,0:T(8,128)(2,1)S(1)} %up.6.after_ref.current_ref), channel_id=1, source_target_pairs={{0,4},{1,5},{2,6},{3,7},{4,0},{5,1},{6,2},{7,3},{8,12},{9,13},{10,... | collective-permute-start | bytes 196616 | tf_op jit(solution)/shard_map/ppermute | solution.py:701
  18.3 6.5 %copy-start.6 = (bf16[1,4,256,256]{3,2,1,0:T(8,128)(2,1)S(1)}, bf16[1,4,256,256]{3,2,1,0:T(8,128)(2,1)}, u32[]{:S(2)}) copy-start(bf16[1,4,256,256]{3,2,1,0:T(8,128)(2,1)} %refs_9_.3) | copy-start | bytes 1572868
  18.3 5.2 %collective-permute-start.3 = (bf16[256,128]{1,0:T(8,128)(2,1)S(1)}, bf16[256,128]{1,0:T(8,128)(2,1)S(1)}, u32[]{:S(2)}, u32[]{:S(2)}) collective-permute-start(bf16[256,128]{1,0:T(8,128)(2,1)S(1)} %up.7), channel_id=1, source_target_pairs={{0,8},{1,9},{2,10},{3,11},{4,12},{5,13},{6,14},{7,15},{8,0},{9,1},... | collective-permute-start | bytes 196616 | tf_op jit(solution)/shard_map/ppermute | solution.py:701
  22.9 1.3 collective-permute-start.4
  22.9 1.4 %collective-permute-start.5 = (bf16[256,128]{1,0:T(8,128)(2,1)S(1)}, bf16[256,128]{1,0:T(8,128)(2,1)S(1)}, u32[]{:S(2)}, u32[]{:S(2)}) collective-permute-start(bf16[256,128]{1,0:T(8,128)(2,1)S(1)} %collective-permute-done.2.sibling_ref.refs_3_), channel_id=1, source_target_pairs={{0,1},{1,0},{2,3},{3,2},{4,5},{5,4},{6,7},{7,6},{8,9},{9,8},{10,11... | collective-permute-start | bytes 196616 | tf_op jit(solution)/shard_map/ppermute | solution.py:701
  23.6 1.3 collective-permute-start.6
  27.0 1.7 %collective-permute-start.7 = (f32[336,256]{1,0:T(8,128)S(1)}, f32[336,256]{1,0:T(8,128)S(1)}, u32[]{:S(2)}, u32[]{:S(2)}) collective-permute-start(f32[336,256]{1,0:T(8,128)S(1)} %get-tuple-element.59), channel_id=1, source_target_pairs={{0,1},{1,0},{2,3},{3,2},{4,5},{5,4},{6,7},{7,6},{8,9},{9,8},{10,11... | collective-permute-start | bytes 1032200 | tf_op jit(solution)/shard_map/ppermute | solution.py:701
  28.8 5.5 %collective-permute-start.8 = (f32[168,256]{1,0:T(8,128)S(1)}, f32[168,256]{1,0:T(8,128)S(1)}, u32[]{:S(2)}, u32[]{:S(2)}) collective-permute-start(f32[168,256]{1,0:T(8,128)S(1)} %get-tuple-element.85), channel_id=1, source_target_pairs={{0,2},{1,5},{2,0},{3,7},{4,6},{5,1},{6,4},{7,3},{8,10},{9,13},{10,... | collective-permute-start | bytes 516104 | tf_op jit(solution)/shard_map/ppermute | solution.py:701
  29.3 2.0 %collective-permute-start.10 = (bf16[256,256]{1,0:T(8,128)(2,1)S(1)}, bf16[256,256]{1,0:T(8,128)(2,1)S(1)}, u32[]{:S(2)}, u32[]{:S(2)}) collective-permute-start(bf16[256,256]{1,0:T(8,128)(2,1)S(1)} %get-tuple-element.46.rest_1_.residual_ref), channel_id=1, source_target_pairs={{0,1},{1,0},{2,3},{3,2},{4,5},{5,4},{6,7},{7,6},{8,9},{9,8},{10,11... | collective-permute-start | bytes 393224 | tf_op jit(solution)/shard_map/ppermute | solution.py:701
  30.3 1.3 %collective-permute-start.9 = (bf16[256,256]{1,0:T(8,128)(2,1)S(1)}, bf16[256,256]{1,0:T(8,128)(2,1)S(1)}, u32[]{:S(2)}, u32[]{:S(2)}) collective-permute-start(bf16[256,256]{1,0:T(8,128)(2,1)S(1)} %get-tuple-element.60.image_ref), channel_id=1, source_target_pairs={{0,1},{1,0},{2,3},{3,2},{4,5},{5,4},{6,7},{7,6},{8,9},{9,8},{10,11... | collective-permute-start | bytes 393224 | tf_op jit(solution)/shard_map/ppermute | solution.py:701
  32.1 7.3 %collective-permute-start.16 = (bf16[256,256]{1,0:T(8,128)(2,1)S(1)}, bf16[256,256]{1,0:T(8,128)(2,1)S(1)}, u32[]{:S(2)}, u32[]{:S(2)}) collective-permute-start(bf16[256,256]{1,0:T(8,128)(2,1)S(1)} %pair_up.1.rest_0_.current_ref), channel_id=1, source_target_pairs={{0,2},{1,3},{2,0},{3,1},{4,6},{5,7},{6,4},{7,5},{8,10},{9,11},{10,... | collective-permute-start | bytes 393224 | tf_op jit(solution)/shard_map/ppermute | solution.py:701
  34.3 10.7 %collective-permute-start.11 = (f32[168,256]{1,0:T(8,128)S(1)}, f32[168,256]{1,0:T(8,128)S(1)}, u32[]{:S(2)}, u32[]{:S(2)}) collective-permute-start(f32[168,256]{1,0:T(8,128)S(1)} %add.24), channel_id=1, source_target_pairs={{0,8},{1,9},{2,10},{3,11},{4,12},{5,13},{6,14},{7,15},{8,0},{9,1},... | collective-permute-start | bytes 516104 | tf_op jit(solution)/shard_map/ppermute | solution.py:701
  39.7 7.9 %collective-permute-start.17 = (bf16[256,256]{1,0:T(8,128)(2,1)S(1)}, bf16[256,256]{1,0:T(8,128)(2,1)S(1)}, u32[]{:S(2)}, u32[]{:S(2)}) collective-permute-start(bf16[256,256]{1,0:T(8,128)(2,1)S(1)} %up.8.after_ref.current_ref), channel_id=1, source_target_pairs={{0,4},{1,5},{2,6},{3,7},{4,0},{5,1},{6,2},{7,3},{8,12},{9,13},{10,... | collective-permute-start | bytes 393224 | tf_op jit(solution)/shard_map/ppermute | solution.py:701
  41.8 15.7 %collective-permute-start.19 = (bf16[256,256]{1,0:T(8,128)(2,1)S(1)}, bf16[256,256]{1,0:T(8,128)(2,1)S(1)}, u32[]{:S(2)}, u32[]{:S(2)}) collective-permute-start(bf16[256,256]{1,0:T(8,128)(2,1)S(1)} %collective-permute-done.16.sibling_ref.refs_3_), channel_id=1, source_target_pairs={{0,1},{1,0},{2,3},{3,2},{4,5},{5,4},{6,7},{7,6},{8,9},{9,8},{10,11... | collective-permute-start | bytes 393224 | tf_op jit(solution)/shard_map/ppermute | solution.py:701
  45.0 6.9 %collective-permute-start.12 = (f32[168,256]{1,0:T(8,128)S(1)}, f32[168,256]{1,0:T(8,128)S(1)}, u32[]{:S(2)}, u32[]{:S(2)}) collective-permute-start(f32[168,256]{1,0:T(8,128)S(1)} %add.19), channel_id=1, source_target_pairs={{0,4},{1,3},{2,6},{3,1},{4,0},{5,7},{6,2},{7,5},{8,12},{9,11},{10,... | collective-permute-start | bytes 516104 | tf_op jit(solution)/shard_map/ppermute | solution.py:701
  47.9 8.5 %collective-permute-start.18 = (bf16[256,256]{1,0:T(8,128)(2,1)S(1)}, bf16[256,256]{1,0:T(8,128)(2,1)S(1)}, u32[]{:S(2)}, u32[]{:S(2)}) collective-permute-start(bf16[256,256]{1,0:T(8,128)(2,1)S(1)} %up.9), channel_id=1, source_target_pairs={{0,8},{1,9},{2,10},{3,11},{4,12},{5,13},{6,14},{7,15},{8,0},{9,1},... | collective-permute-start | bytes 393224 | tf_op jit(solution)/shard_map/ppermute | solution.py:701
  51.4 6.1 %collective-permute-start.20 = (bf16[256,256]{1,0:T(8,128)(2,1)S(1)}, bf16[256,256]{1,0:T(8,128)(2,1)S(1)}, u32[]{:S(2)}, u32[]{:S(2)}) collective-permute-start(bf16[256,256]{1,0:T(8,128)(2,1)S(1)} %collective-permute-done.17.sibling_ref.refs_4_), channel_id=1, source_target_pairs={{0,1},{1,0},{2,3},{3,2},{4,5},{5,4},{6,7},{7,6},{8,9},{9,8},{10,11... | collective-permute-start | bytes 393224 | tf_op jit(solution)/shard_map/ppermute | solution.py:701
  51.9 5.5 %collective-permute-start.13 = (f32[168,256]{1,0:T(8,128)S(1)}, f32[168,256]{1,0:T(8,128)S(1)}, u32[]{:S(2)}, u32[]{:S(2)}) collective-permute-start(f32[168,256]{1,0:T(8,128)S(1)} %add.20.after_ref.own_ref), channel_id=1, source_target_pairs={{0,2},{1,5},{2,0},{3,7},{4,6},{5,1},{6,4},{7,3},{8,10},{9,13},{10,... | collective-permute-start | bytes 516104 | tf_op jit(solution)/shard_map/ppermute | solution.py:701
  56.4 1.4 %collective-permute-start.21 = (bf16[256,256]{1,0:T(8,128)(2,1)S(1)}, bf16[256,256]{1,0:T(8,128)(2,1)S(1)}, u32[]{:S(2)}, u32[]{:S(2)}) collective-permute-start(bf16[256,256]{1,0:T(8,128)(2,1)S(1)} %ready.3), channel_id=1, source_target_pairs={{0,1},{1,0},{2,3},{3,2},{4,5},{5,4},{6,7},{7,6},{8,9},{9,8},{10,11... | collective-permute-start | bytes 393224 | tf_op jit(solution)/shard_map/ppermute | solution.py:701
  56.5 4.2 %collective-permute-start.14 = (f32[168,256]{1,0:T(8,128)S(1)}, f32[168,256]{1,0:T(8,128)S(1)}, u32[]{:S(2)}, u32[]{:S(2)}) collective-permute-start(f32[168,256]{1,0:T(8,128)S(1)} %add.20.after_ref.own_ref), channel_id=1, source_target_pairs={{0,1},{1,0},{2,3},{3,2},{4,5},{5,4},{6,7},{7,6},{8,9},{9,8},{10,11... | collective-permute-start | bytes 516104 | tf_op jit(solution)/shard_map/ppermute | solution.py:701
  57.4 3.3 %collective-permute-start.15 = (f32[168,256]{1,0:T(8,128)S(1)}, f32[168,256]{1,0:T(8,128)S(1)}, u32[]{:S(2)}, u32[]{:S(2)}) collective-permute-start(f32[168,256]{1,0:T(8,128)S(1)} %collective-permute-done.13.side_ref), channel_id=1, source_target_pairs={{0,1},{1,0},{2,3},{3,2},{4,5},{5,4},{6,7},{7,6},{8,9},{9,8},{10,11... | collective-permute-start | bytes 516104 | tf_op jit(solution)/shard_map/ppermute | solution.py:701
  82.6 1.5 %collective-permute-start.22 = (f32[208,256]{1,0:T(8,128)S(1)}, f32[208,256]{1,0:T(8,128)S(1)}, u32[]{:S(2)}, u32[]{:S(2)}) collective-permute-start(f32[208,256]{1,0:T(8,128)S(1)} %get-tuple-element.71), channel_id=1, source_target_pairs={{0,1},{1,0},{2,3},{3,2},{4,5},{5,4},{6,7},{7,6},{8,9},{9,8},{10,11... | collective-permute-start | bytes 638984 | tf_op jit(solution)/shard_map/ppermute | solution.py:701
  84.2 4.8 %collective-permute-start.23 = (f32[104,256]{1,0:T(8,128)S(1)}, f32[104,256]{1,0:T(8,128)S(1)}, u32[]{:S(2)}, u32[]{:S(2)}) collective-permute-start(f32[104,256]{1,0:T(8,128)S(1)} %slice.19), channel_id=1, source_target_pairs={{0,2},{1,5},{2,0},{3,7},{4,6},{5,1},{6,4},{7,3},{8,10},{9,13},{10,... | collective-permute-start | bytes 319496 | tf_op jit(solution)/shard_map/ppermute | solution.py:701
  89.0 16.5 %collective-permute-start.24 = (f32[104,256]{1,0:T(8,128)S(1)}, f32[104,256]{1,0:T(8,128)S(1)}, u32[]{:S(2)}, u32[]{:S(2)}) collective-permute-start(f32[104,256]{1,0:T(8,128)S(1)} %slice_add_fusion.left_ref), channel_id=1, source_target_pairs={{0,8},{1,9},{2,10},{3,11},{4,12},{5,13},{6,14},{7,15},{8,0},{9,1},... | collective-permute-start | bytes 319496 | tf_op jit(solution)/shard_map/ppermute | solution.py:701
  91.3 14.4 %copy-start.5 = (f32[1024,256]{1,0:T(8,128)S(1)}, f32[1024,256]{1,0:T(8,128)}, u32[]{:S(2)}) copy-start(f32[1024,256]{1,0:T(8,128)} %solution_ref.1) | copy-start | bytes 3145732
  105.5 4.8 %collective-permute-start.25 = (f32[104,256]{1,0:T(8,128)S(1)}, f32[104,256]{1,0:T(8,128)S(1)}, u32[]{:S(2)}, u32[]{:S(2)}) collective-permute-start(f32[104,256]{1,0:T(8,128)S(1)} %add.25.left_ref), channel_id=1, source_target_pairs={{0,4},{1,3},{2,6},{3,1},{4,0},{5,7},{6,2},{7,5},{8,12},{9,11},{10,... | collective-permute-start | bytes 319496 | tf_op jit(solution)/shard_map/ppermute | solution.py:701
  110.3 4.8 %collective-permute-start.26 = (f32[104,256]{1,0:T(8,128)S(1)}, f32[104,256]{1,0:T(8,128)S(1)}, u32[]{:S(2)}, u32[]{:S(2)}) collective-permute-start(f32[104,256]{1,0:T(8,128)S(1)} %add.26.own_ref), channel_id=1, source_target_pairs={{0,2},{1,5},{2,0},{3,7},{4,6},{5,1},{6,4},{7,3},{8,10},{9,13},{10,... | collective-permute-start | bytes 319496 | tf_op jit(solution)/shard_map/ppermute | solution.py:701
  110.9 4.1 %collective-permute-start.27 = (f32[104,256]{1,0:T(8,128)S(1)}, f32[104,256]{1,0:T(8,128)S(1)}, u32[]{:S(2)}, u32[]{:S(2)}) collective-permute-start(f32[104,256]{1,0:T(8,128)S(1)} %add.26.own_ref), channel_id=1, source_target_pairs={{0,1},{1,0},{2,3},{3,2},{4,5},{5,4},{6,7},{7,6},{8,9},{9,8},{10,11... | collective-permute-start | bytes 319496 | tf_op jit(solution)/shard_map/ppermute | solution.py:701
  115.0 1.3 collective-permute-start.28
  (7 other events, 22.4 us)

commit v6 on v5

--- a/solution.py
+++ b/solution.py
@@ -186,7 +186,7 @@
 
 
 def payload_rows(size, with_start):
-    rows = size + size // 2 + 8 + (size if with_start else 0)
+    rows = size + 8 + (size + size // 2 if with_start else 0)
     return -(-rows // 32) * 32
 
 
@@ -557,12 +557,16 @@
     solved_mixed = dot3(second, mixed * second_scale) * second_scale
     weighted = dot3(images, alpha)
     beta = beta_of(alpha, weighted, mixed.T, first, first_scale, solved_mixed)
-    rows = (base_part_ref[...] - dot3(alpha_part_ref[...], alpha)) + dot3(beta_part_ref[...], beta)
+    still = base_part_ref[...] - dot3(alpha_part_ref[...], alpha)
+    rows = still + dot3(beta_part_ref[...], beta)
     image_row = rows[size : 2 * size]
-    turned = dot3(alpha.T, jnp.concatenate([image_row, rows[3 * size :]], 1))
+    turned = dot3(
+        alpha.T, jnp.concatenate([still[size : 2 * size], rows[3 * size :]], 1)
+    )
     square = rows[2 * size : 3 * size] - turned[:, size:] + dot3(beta.T, image_row)
-    packed, tail = pack_half(square)
-    write_parts(position, [rows[:size] - turned[:, :size], packed], [tail], later, keep_out, send_out)
+    plain = still[:size] - turned[:, :size]
+    packed, diagonal = pack_pair(0.5 * (plain + plain.T), square)
+    write_parts(position, [packed], [diagonal], later, keep_out, send_out)
     change = 0.5 * dot3(alpha.T, weighted) - dot3(mixed, alpha)
     fresh_out[...] = res_gram + (change + change.T)
     alpha_out[...] = alpha
@@ -581,14 +585,17 @@
     curvature_ref,
     inverse_out,
     turn_out,
+    rest_out,
     store,
 ):
-    beta = beta_ref[...]
+    beta, alpha = beta_ref[...], alpha_ref[...]
     ((inverse, scale),) = inverses([fresh_ref[...]], 4, store)
     inverse_out[...] = inverse * scale
-    across = mixed_ref[...].T - dot3(images_ref[...], alpha_ref[...])
+    rest = dot3(mixed_ref[...] - dot3(alpha.T, images_ref[...]), beta)
+    rest_out[...] = rest
+    across = mixed_ref[...].T - dot3(images_ref[...], alpha)
     across = across + dot3(curvature_ref[...], beta)
-    turn = dot3(beta.T, across)
+    turn = dot3(beta.T, across) + rest
     turn_out[...] = 0.5 * (turn + turn.T)
 
 
@@ -636,6 +643,7 @@
     fresh_ref,
     inverse_ref,
     turn_ref,
+    rest_ref,
     solution_out,
     residual_out,
     direction_out,
@@ -648,11 +656,10 @@
 ):
     count, size = direction_ref.shape
     collect(position_ref[0], own_ref, side_ref, core_ref, far_ref, payload)
-    mixed = payload[0:size, :]
-    base = size + size // 2
-    images = unpack_half(payload[size:base, :], payload[base : base + 1, :])
+    plain, images = unpack_pair(payload[0:size, :], payload[size : size + 1, :])
+    mixed = plain + rest_ref[...]
+    curvature = plain + turn_ref[...]
     res_gram = fresh_ref[...]
-    curvature = 0.5 * (mixed + mixed.T) + turn_ref[...]
     picked = jnp.where(eye_mask(size), res_gram, 0.0)
     column_scale = lax.rsqrt(jnp.sum(picked, axis=1, keepdims=True))
     solved_mixed = dot3(inverse_ref[...], mixed * column_scale)
@@ -884,11 +891,11 @@
         [pltpu.VMEM((rows, size), F32), pltpu.VMEM((later_rows, size), F32), work],
         micros=5.0,
     )
-    inverse, turn = call(
+    inverse, turn, rest = call(
         carry_kernel,
         "carry",
         [alpha, beta, fresh, mixed, images, curvature],
-        [square, square],
+        [square] * 3,
         [work],
         micros=3.0,
     )
@@ -904,7 +911,7 @@
         call(
             last_kernel,
             "last",
-            pieces + [image, residual, direction, solution, fresh, inverse, turn],
+            pieces + [image, residual, direction, solution, fresh, inverse, turn, rest],
             [tall, tall, tall],
             [pltpu.VMEM((later_rows, size), F32), work]
             + [held] * 3

time: 133 us -> 132 us (level); the launches traced: 134 us -> 131 us
  Pallas kernels: 82 us -> 79.9 us
  waiting for transfers between devices: 23.8 us -> 22.4 us
    pallas_call x28, Pallas kernels: 82 us -> 79.9 us  [call(): pl.pallas_call(kernel, name=name, in_specs=specs, out_specs=[ANY if apart...]
    ppermute x29, waiting for transfers between devices: 23.8 us -> 22.4 us  [swapped(): return lax.ppermute(value, 'leaf', pairs)]
  transfers between devices with their start and end apart: 29 -> 29, of which waited for: 20 -> 20; matrix products, arithmetic and copies ran while one was open for 0% -> 0% of each run, Pallas kernels for 27% -> 28%
where the time goes in v6:
time: 132 us; the launch traced here: 131 us
  Pallas kernels  79.9 us (61%)
  starting transfers between devices  26.1 us (20%)
  waiting for transfers between devices  22.4 us (17%)
    pallas_call x28, Pallas kernels, call(): pl.pallas_call(kernel, name=name, in_specs=specs, out_specs=[ANY if apart...  79.9 us
    ppermute x29, starting transfers between devices, swapped(): return lax.ppermute(value, 'leaf', pairs)  26.1 us
    ppermute x29, waiting for transfers between devices, swapped(): return lax.ppermute(value, 'leaf', pairs)  22.4 us
  transfers between devices with their start and end apart: 29, of which 20 were waited for; matrix products, arithmetic and copies ran while one was open for 0% of the time, Pallas kernels for 28%

profile of v6, /device:TPU:0, one launch (start us, length us, event | category | flops | bytes accessed | tf_op | source)
XLA Modules:
  0.0 130.7 jit_solution(13794980611563646257)
XLA Ops:
  0.6 2.8 %coef.1.value_ref = bf16[256,256]{1,0:T(8,128)(2,1)} custom-call(f32[1024,256]{1,0:T(8,128)} %direction_ref.7, bf16[1024,256]{1,0:T(8,128)(2,1)} %basis_ref.11, s32[1,256]{1,0:T(1,128)} %skel_ref.11), custom_call_target="tpu_custom_call" | custom-call | flops 2969999872 | tf_op jit(solution)/shard_map/coef/pallas_call | solution.py:691
  3.9 1.1 copy-done.7
  5.4 2.9 %collective-permute-start.1 = (bf16[256,128]{1,0:T(8,128)(2,1)S(1)}, bf16[256,128]{1,0:T(8,128)(2,1)S(1)}, u32[]{:S(2)}, u32[]{:S(2)}) collective-permute-start(bf16[256,128]{1,0:T(8,128)(2,1)S(1)} %up.5.after_ref.current_ref), channel_id=1, source_target_pairs={{0,2},{1,3},{2,0},{3,1},{4,6},{5,7},{6,4},{7,5},{8,10},{9,11},{10,... | collective-permute-start | bytes 196616 | tf_op jit(solution)/shard_map/ppermute | solution.py:708
  9.1 3.6 %block.1.rest_0_.block_ref = bf16[1024,1024]{1,0:T(8,128)(2,1)S(1)} custom-call(f32[3,1024]{1,0:T(4,128)S(1)} %copy-done.8, s32[1,1024]{1,0:T(1,128)S(1)} %bitcast.2, bf16[256,128]{1,0:T(8,128)(2,1)S(1)} %up.5.after_ref.current_ref), custom_call_target="tpu_custom_call" | custom-call | flops 3960000000 | tf_op jit(solution)/shard_map/block/pallas_call | solution.py:691
  13.7 1.6 %collective-permute-start.2 = (bf16[256,128]{1,0:T(8,128)(2,1)S(1)}, bf16[256,128]{1,0:T(8,128)(2,1)S(1)}, u32[]{:S(2)}, u32[]{:S(2)}) collective-permute-start(bf16[256,128]{1,0:T(8,128)(2,1)S(1)} %up.6.after_ref.current_ref), channel_id=1, source_target_pairs={{0,4},{1,5},{2,6},{3,7},{4,0},{5,1},{6,2},{7,3},{8,12},{9,13},{10,... | collective-permute-start | bytes 196616 | tf_op jit(solution)/shard_map/ppermute | solution.py:708
  15.4 1.6 %factor.1 = (bf16[512,256]{1,0:T(8,128)(2,1)S(1)}, bf16[512,256]{1,0:T(8,128)(2,1)S(1)}, bf16[512,256]{1,0:T(8,128)(2,1)S(1)}, bf16[256,256]{1,0:T(8,128)(2,1)S(...) custom-call(bf16[512,1024]{1,0:T(8,128)(2,1)S(1)} %get-tuple-element.45.rest_1_.high_re, ...), custom_call_target="tpu_custom_call" | custom-call | flops 1980000000 | tf_op jit(solution)/shard_map/factor/pallas_call | solution.py:691
  17.0 1.1 collective-permute-done.2.sibling_ref.refs_3_
  18.3 2.7 %collective-permute-start.3 = (bf16[256,128]{1,0:T(8,128)(2,1)S(1)}, bf16[256,128]{1,0:T(8,128)(2,1)S(1)}, u32[]{:S(2)}, u32[]{:S(2)}) collective-permute-start(bf16[256,128]{1,0:T(8,128)(2,1)S(1)} %up.7), channel_id=1, source_target_pairs={{0,8},{1,9},{2,10},{3,11},{4,12},{5,13},{6,14},{7,15},{8,0},{9,1},... | collective-permute-start | bytes 196616 | tf_op jit(solution)/shard_map/ppermute | solution.py:708
  21.0 1.8 %near_factor.1 = (f32[512,256]{1,0:T(8,128)S(1)}, f32[256,256]{1,0:T(8,128)S(1)}, f32[256,256]{1,0:T(8,128)S(1)}, f32[256,256]{1,0:T(8,128)S(1)}) custom-call(f32[1024,256]{1,0:T(8,128)S(1)} %near.1.rest_0_.near_ref, bf16[512,1024]{1,0:T(8,128)(2,1)S(1)} %get-tuple-element.45.rest_1_.high_ref, bf16[512,1024]{1,0:T(8,128)(2,1)S(1)} %get-tuple-element.46.low_ref, ...), custom_call_target="tpu_custom_call" | custom-call | flops 1980000000 | tf_op jit(solution)/shard_map/near_factor/pallas_call | solution.py:691
  24.8 2.1 %down.1 = (bf16[2,256,256]{2,1,0:T(8,128)(2,1)S(1)}, bf16[256,256]{1,0:T(8,128)(2,1)S(1)}, bf16[2,256,256]{2,1,0:T(8,128)(2,1)S(1)}, f32[336,256]{1,0:T(8,128)S(...) custom-call(s32[1]{0:T(128)} %bitcast.position_ref.refs_0_, ...), custom_call_target="tpu_custom_call" | custom-call | flops 2200000000 | tf_op jit(solution)/shard_map/down/pallas_call | solution.py:691
  27.2 1.5 %collective-permute-done.7 = f32[336,256]{1,0:T(8,128)S(1)} collective-permute-done((f32[336,256]{1,0:T(8,128)S(1)}, f32[336,256]{1,0:T(8,128)S(1)}, u32[]{:S(2)}, u32[]{:S(2)}) %collective-permute-start.7) | collective-permute-done | bytes 344096 | tf_op jit(solution)/shard_map/ppermute | solution.py:708
  32.9 1.3 %collective-permute-done.8.right_ref = f32[168,256]{1,0:T(8,128)S(1)} collective-permute-done((f32[168,256]{1,0:T(8,128)S(1)}, f32[168,256]{1,0:T(8,128)S(1)}, u32[]{:S(2)}, u32[]{:S(2)}) %collective-permute-start.8) | collective-permute-done | bytes 172064 | tf_op jit(solution)/shard_map/ppermute | solution.py:708
  34.3 2.7 %collective-permute-start.11 = (f32[168,256]{1,0:T(8,128)S(1)}, f32[168,256]{1,0:T(8,128)S(1)}, u32[]{:S(2)}, u32[]{:S(2)}) collective-permute-start(f32[168,256]{1,0:T(8,128)S(1)} %add.24), channel_id=1, source_target_pairs={{0,8},{1,9},{2,10},{3,11},{4,12},{5,13},{6,14},{7,15},{8,0},{9,1},... | collective-permute-start | bytes 516104 | tf_op jit(solution)/shard_map/ppermute | solution.py:708
  37.0 2.4 %pair_near.1.rest_0_.near_ref = f32[2,1024,256]{2,1,0:T(8,128)S(1)} custom-call(bf16[1024,1024]{1,0:T(8,128)(2,1)S(1)} %block.1.rest_0_.block_ref, f32[1024,256]{1,0:T(8,128)S(1)} %image.1.image_ref, f32[1024,256]{1,0:T(8,128)S(1)} %copy-done.4), custom_call_target="tpu_custom_call" | custom-call | flops 2640000000 | tf_op jit(solution)/shard_map/pair_near/pallas_call | solution.py:691
  39.7 2.2 %collective-permute-start.17 = (bf16[256,256]{1,0:T(8,128)(2,1)S(1)}, bf16[256,256]{1,0:T(8,128)(2,1)S(1)}, u32[]{:S(2)}, u32[]{:S(2)}) collective-permute-start(bf16[256,256]{1,0:T(8,128)(2,1)S(1)} %up.8.after_ref.current_ref), channel_id=1, source_target_pairs={{0,4},{1,5},{2,6},{3,7},{4,0},{5,1},{6,2},{7,3},{8,12},{9,13},{10,... | collective-permute-start | bytes 393224 | tf_op jit(solution)/shard_map/ppermute | solution.py:708
  41.9 3.1 %collective-permute-done.11 = f32[168,256]{1,0:T(8,128)S(1)} collective-permute-done((f32[168,256]{1,0:T(8,128)S(1)}, f32[168,256]{1,0:T(8,128)S(1)}, u32[]{:S(2)}, u32[]{:S(2)}) %collective-permute-start.11) | collective-permute-done | bytes 172064 | tf_op jit(solution)/shard_map/ppermute | solution.py:708
  45.7 1.8 %pair_cross.1.rest_0_.refs_11_ = f32[512,512]{1,0:T(8,128)S(1)} custom-call(f32[2,1024,256]{2,1,0:T(8,128)S(1)} %pair_near.1.rest_0_.near_ref, f32[1024,256]{1,0:T(8,128)S(1)} %image.1.image_ref, bf16[512,1024]{1,0:T(8,128)(2,1)S(1)} %get-tuple-element.45.rest_1_.high_ref, bf16[512,1024]{1,0:T(8,128)(2,1)S(1)} %get-tuple-element.46.low_ref, ...), custom_call_target="tpu_custom_call" | custom-call | flops 2529999872 | tf_op jit(solution)/shard_map/pair_cross/pallas_call | solution.py:691
  47.9 3.5 %collective-permute-start.18 = (bf16[256,256]{1,0:T(8,128)(2,1)S(1)}, bf16[256,256]{1,0:T(8,128)(2,1)S(1)}, u32[]{:S(2)}, u32[]{:S(2)}) collective-permute-start(bf16[256,256]{1,0:T(8,128)(2,1)S(1)} %up.9), channel_id=1, source_target_pairs={{0,8},{1,9},{2,10},{3,11},{4,12},{5,13},{6,14},{7,15},{8,0},{9,1},... | collective-permute-start | bytes 393224 | tf_op jit(solution)/shard_map/ppermute | solution.py:708
  52.2 2.4 %pair_square.1 = (f32[512,512]{1,0:T(8,128)S(1)}, f32[256,512]{1,0:T(8,128)S(1)}) custom-call(f32[2,1024,256]{2,1,0:T(8,128)S(1)} %pair_near.1.rest_0_.near_ref, bf16[1024,256]{1,0:T(8,128)(2,1)S(1)} %copy-done.2, s32[1,256]{1,0:T(1,128)S(1)} %copy-done.3, f32[168,256]{1,0:T(8,128)S(1)} %add.20.after_ref.own_ref), custom_call_target="tpu_custom_call" | custom-call | flops 3080000000 | tf_op jit(solution)/shard_map/pair_square/pallas_call | solution.py:691
  54.6 1.8 %collective-permute-done.18.value_ref.refs_5_ = bf16[256,256]{1,0:T(8,128)(2,1)S(1)} collective-permute-done((bf16[256,256]{1,0:T(8,128)(2,1)S(1)}, bf16[256,256]{1,0:T(8,128)(2,1)S(1)}, u32[]{:S(2)}, u32[]{:S(2)}) %collective-permute-start.18) | collective-permute-done | bytes 131104 | tf_op jit(solution)/shard_map/ppermute | solution.py:708
  57.8 2.9 %pair_down.1 = (bf16[2,256,512]{2,1,0:T(8,128)(2,1)S(1)}, f32[1024,256]{1,0:T(8,128)S(1)}, f32[1024,256]{1,0:T(8,128)S(1)}, f32[1024,256]{1,0:T(8,128)S(1)}) custom-call(s32[1]{0:T(128)} %bitcast.position_ref.refs_0_, bf16[256,256]{1,0:T(8,128)(2,1)S(1)} %collective-permute-done.9.image_other.refs_1_, ...), custom_call_target="tpu_custom_call" | custom-call | flops 2750000128 | tf_op jit(solution)/shard_map/pair_down/pallas_call | solution.py:691
  60.7 20.2 %first.1 = (f32[144,256]{1,0:T(8,128)S(1)}, f32[144,256]{1,0:T(8,128)S(1)}, f32[256,256]{1,0:T(8,128)S(1)}, f32[256,256]{1,0:T(8,128)S(1)}, f32[256,256]{1,0:T(8...) custom-call(s32[1]{0:T(128)} %bitcast.position_ref.refs_0_, ...), custom_call_target="tpu_custom_call" | custom-call | flops 5500000256 | tf_op jit(solution)/shard_map/first/pallas_call | solution.py:691
  81.2 1.2 collective-permute-done.22
  82.5 1.4 %collective-permute-start.23 = (f32[72,256]{1,0:T(8,128)S(1)}, f32[72,256]{1,0:T(8,128)S(1)}, u32[]{:S(2)}, u32[]{:S(2)}) collective-permute-start(f32[72,256]{1,0:T(8,128)S(1)} %slice.19), channel_id=1, source_target_pairs={{0,2},{1,5},{2,0},{3,7},{4,6},{5,1},{6,4},{7,3},{8,10},{9,13},{10,... | collective-permute-start | bytes 221192 | tf_op jit(solution)/shard_map/ppermute | solution.py:708
  83.8 3.0 %collective-permute-done.23 = f32[72,256]{1,0:T(8,128)S(1)} collective-permute-done((f32[72,256]{1,0:T(8,128)S(1)}, f32[72,256]{1,0:T(8,128)S(1)}, u32[]{:S(2)}, u32[]{:S(2)}) %collective-permute-start.23) | collective-permute-done | bytes 73760 | tf_op jit(solution)/shard_map/ppermute | solution.py:708
  86.9 2.3 %collective-permute-start.24 = (f32[72,256]{1,0:T(8,128)S(1)}, f32[72,256]{1,0:T(8,128)S(1)}, u32[]{:S(2)}, u32[]{:S(2)}) collective-permute-start(f32[72,256]{1,0:T(8,128)S(1)} %slice_add_fusion.left_ref), channel_id=1, source_target_pairs={{0,8},{1,9},{2,10},{3,11},{4,12},{5,13},{6,14},{7,15},{8,0},{9,1},... | collective-permute-start | bytes 221192 | tf_op jit(solution)/shard_map/ppermute | solution.py:708
  89.2 14.4 %carry.1 = (f32[256,256]{1,0:T(8,128)S(1)}, f32[256,256]{1,0:T(8,128)S(1)}, f32[256,256]{1,0:T(8,128)S(1)}) custom-call(f32[256,256]{1,0:T(8,128)S(1)} %get-tuple-element.73.alpha_ref, f32[256,256]{1,0:T(8,128)S(1)} %get-tuple-element.74.beta_ref, f32[256,256]{1,0:T(8,128)S(1)} %get-tuple-element.75.fresh_ref, f32[256,256]{1,0:T(8,128)S(1)} %get-tuple-element.76.mixed_ref, ...), custom_call_target="tpu_custom_call" | custom-call | flops 3300000000 | tf_op jit(solution)/shard_map/carry/pallas_call | solution.py:691
  103.9 3.0 %update.1 = (f32[1024,256]{1,0:T(8,128)S(1)}, f32[1024,256]{1,0:T(8,128)S(1)}, f32[1024,256]{1,0:T(8,128)S(1)}, f32[1024,256]{1,0:T(8,128)S(1)}) custom-call(f32[1024,256]{1,0:T(8,128)S(1)} %copy-done.4, f32[1024,256]{1,0:T(8,128)S(1)} %copy-done.1, f32[1024,256]{1,0:T(8,128)S(1)} %copy-done.5, f32[1024,256]{1,0:T(8,128)S(1)} %image.1.image_ref, ...), custom_call_target="tpu_custom_call" | custom-call | flops 3520000000 | tf_op jit(solution)/shard_map/update/pallas_call | solution.py:691
  107.0 1.1 collective-permute-done.25.right_ref
  109.0 3.5 %collective-permute-done.26.side_ref = f32[72,256]{1,0:T(8,128)S(1)} collective-permute-done((f32[72,256]{1,0:T(8,128)S(1)}, f32[72,256]{1,0:T(8,128)S(1)}, u32[]{:S(2)}, u32[]{:S(2)}) %collective-permute-start.26) | collective-permute-done | bytes 73760 | tf_op jit(solution)/shard_map/ppermute | solution.py:708
  112.5 1.3 collective-permute-done.28.far_ref
  113.8 16.7 %last.1 = (f32[1024,256]{1,0:T(8,128)}, f32[1024,256]{1,0:T(8,128)}, f32[1024,256]{1,0:T(8,128)}) custom-call(s32[1]{0:T(128)} %bitcast.position_ref.refs_0_, f32[72,256]{1,0:T(8,128)S(1)} %add.26.own_ref, f32[72,256]{1,0:T(8,128)S(1)} %collective-permute-done.26.side_ref, f32[72,256]{1,0:T(8,128)S(1)} %collective-permute-done.27.core_ref, ...), custom_call_target="tpu_custom_call" | custom-call | flops 7699999744 | tf_op jit(solution)/shard_map/last/pallas_call | solution.py:691
  (81 shorter events, 14.4 us)
Async XLA Ops:
  3.4 4.9 %copy-start.4 = (f32[1024,256]{1,0:T(8,128)S(1)}, f32[1024,256]{1,0:T(8,128)}, u32[]{:S(2)}) copy-start(f32[1024,256]{1,0:T(8,128)} %residual_ref.5) | copy-start | bytes 3145732
  3.4 1.7 %collective-permute-start = (bf16[256,256]{1,0:T(8,128)(2,1)}, bf16[256,256]{1,0:T(8,128)(2,1)S(1)}, u32[]{:S(2)}, u32[]{:S(2)}) collective-permute-start(bf16[256,256]{1,0:T(8,128)(2,1)} %coef.1.value_ref), channel_id=1, source_target_pairs={{0,1},{1,0},{2,3},{3,2},{4,5},{5,4},{6,7},{7,6},{8,9},{9,8},{10,11... | collective-permute-start | bytes 393224 | tf_op jit(solution)/shard_map/ppermute | solution.py:708
  5.4 8.0 %collective-permute-start.1 = (bf16[256,128]{1,0:T(8,128)(2,1)S(1)}, bf16[256,128]{1,0:T(8,128)(2,1)S(1)}, u32[]{:S(2)}, u32[]{:S(2)}) collective-permute-start(bf16[256,128]{1,0:T(8,128)(2,1)S(1)} %up.5.after_ref.current_ref), channel_id=1, source_target_pairs={{0,2},{1,3},{2,0},{3,1},{4,6},{5,7},{6,4},{7,5},{8,10},{9,11},{10,... | collective-permute-start | bytes 196616 | tf_op jit(solution)/shard_map/ppermute | solution.py:708
  13.7 4.3 %collective-permute-start.2 = (bf16[256,128]{1,0:T(8,128)(2,1)S(1)}, bf16[256,128]{1,0:T(8,128)(2,1)S(1)}, u32[]{:S(2)}, u32[]{:S(2)}) collective-permute-start(bf16[256,128]{1,0:T(8,128)(2,1)S(1)} %up.6.after_ref.current_ref), channel_id=1, source_target_pairs={{0,4},{1,5},{2,6},{3,7},{4,0},{5,1},{6,2},{7,3},{8,12},{9,13},{10,... | collective-permute-start | bytes 196616 | tf_op jit(solution)/shard_map/ppermute | solution.py:708
  18.3 6.5 %copy-start.6 = (bf16[1,4,256,256]{3,2,1,0:T(8,128)(2,1)S(1)}, bf16[1,4,256,256]{3,2,1,0:T(8,128)(2,1)}, u32[]{:S(2)}) copy-start(bf16[1,4,256,256]{3,2,1,0:T(8,128)(2,1)} %refs_9_.3) | copy-start | bytes 1572868
  18.3 5.2 %collective-permute-start.3 = (bf16[256,128]{1,0:T(8,128)(2,1)S(1)}, bf16[256,128]{1,0:T(8,128)(2,1)S(1)}, u32[]{:S(2)}, u32[]{:S(2)}) collective-permute-start(bf16[256,128]{1,0:T(8,128)(2,1)S(1)} %up.7), channel_id=1, source_target_pairs={{0,8},{1,9},{2,10},{3,11},{4,12},{5,13},{6,14},{7,15},{8,0},{9,1},... | collective-permute-start | bytes 196616 | tf_op jit(solution)/shard_map/ppermute | solution.py:708
  22.9 1.3 %collective-permute-start.4 = (bf16[256,128]{1,0:T(8,128)(2,1)S(1)}, bf16[256,128]{1,0:T(8,128)(2,1)S(1)}, u32[]{:S(2)}, u32[]{:S(2)}) collective-permute-start(bf16[256,128]{1,0:T(8,128)(2,1)S(1)} %collective-permute-done.1.sibling_ref.refs_2_), channel_id=1, source_target_pairs={{0,1},{1,0},{2,3},{3,2},{4,5},{5,4},{6,7},{7,6},{8,9},{9,8},{10,11... | collective-permute-start | bytes 196616 | tf_op jit(solution)/shard_map/ppermute | solution.py:708
  22.9 1.4 %collective-permute-start.5 = (bf16[256,128]{1,0:T(8,128)(2,1)S(1)}, bf16[256,128]{1,0:T(8,128)(2,1)S(1)}, u32[]{:S(2)}, u32[]{:S(2)}) collective-permute-start(bf16[256,128]{1,0:T(8,128)(2,1)S(1)} %collective-permute-done.2.sibling_ref.refs_3_), channel_id=1, source_target_pairs={{0,1},{1,0},{2,3},{3,2},{4,5},{5,4},{6,7},{7,6},{8,9},{9,8},{10,11... | collective-permute-start | bytes 196616 | tf_op jit(solution)/shard_map/ppermute | solution.py:708
  23.6 1.3 collective-permute-start.6
  27.0 1.7 %collective-permute-start.7 = (f32[336,256]{1,0:T(8,128)S(1)}, f32[336,256]{1,0:T(8,128)S(1)}, u32[]{:S(2)}, u32[]{:S(2)}) collective-permute-start(f32[336,256]{1,0:T(8,128)S(1)} %get-tuple-element.60), channel_id=1, source_target_pairs={{0,1},{1,0},{2,3},{3,2},{4,5},{5,4},{6,7},{7,6},{8,9},{9,8},{10,11... | collective-permute-start | bytes 1032200 | tf_op jit(solution)/shard_map/ppermute | solution.py:708
  28.8 5.5 %collective-permute-start.8 = (f32[168,256]{1,0:T(8,128)S(1)}, f32[168,256]{1,0:T(8,128)S(1)}, u32[]{:S(2)}, u32[]{:S(2)}) collective-permute-start(f32[168,256]{1,0:T(8,128)S(1)} %get-tuple-element.87), channel_id=1, source_target_pairs={{0,2},{1,5},{2,0},{3,7},{4,6},{5,1},{6,4},{7,3},{8,10},{9,13},{10,... | collective-permute-start | bytes 516104 | tf_op jit(solution)/shard_map/ppermute | solution.py:708
  29.3 2.0 %collective-permute-start.10 = (bf16[256,256]{1,0:T(8,128)(2,1)S(1)}, bf16[256,256]{1,0:T(8,128)(2,1)S(1)}, u32[]{:S(2)}, u32[]{:S(2)}) collective-permute-start(bf16[256,256]{1,0:T(8,128)(2,1)S(1)} %get-tuple-element.47.rest_1_.residual_ref), channel_id=1, source_target_pairs={{0,1},{1,0},{2,3},{3,2},{4,5},{5,4},{6,7},{7,6},{8,9},{9,8},{10,11... | collective-permute-start | bytes 393224 | tf_op jit(solution)/shard_map/ppermute | solution.py:708
  30.3 1.3 %collective-permute-start.9 = (bf16[256,256]{1,0:T(8,128)(2,1)S(1)}, bf16[256,256]{1,0:T(8,128)(2,1)S(1)}, u32[]{:S(2)}, u32[]{:S(2)}) collective-permute-start(bf16[256,256]{1,0:T(8,128)(2,1)S(1)} %get-tuple-element.61.image_ref), channel_id=1, source_target_pairs={{0,1},{1,0},{2,3},{3,2},{4,5},{5,4},{6,7},{7,6},{8,9},{9,8},{10,11... | collective-permute-start | bytes 393224 | tf_op jit(solution)/shard_map/ppermute | solution.py:708
  32.1 7.3 %collective-permute-start.16 = (bf16[256,256]{1,0:T(8,128)(2,1)S(1)}, bf16[256,256]{1,0:T(8,128)(2,1)S(1)}, u32[]{:S(2)}, u32[]{:S(2)}) collective-permute-start(bf16[256,256]{1,0:T(8,128)(2,1)S(1)} %pair_up.1.rest_0_.current_ref), channel_id=1, source_target_pairs={{0,2},{1,3},{2,0},{3,1},{4,6},{5,7},{6,4},{7,5},{8,10},{9,11},{10,... | collective-permute-start | bytes 393224 | tf_op jit(solution)/shard_map/ppermute | solution.py:708
  34.3 10.7 %collective-permute-start.11 = (f32[168,256]{1,0:T(8,128)S(1)}, f32[168,256]{1,0:T(8,128)S(1)}, u32[]{:S(2)}, u32[]{:S(2)}) collective-permute-start(f32[168,256]{1,0:T(8,128)S(1)} %add.24), channel_id=1, source_target_pairs={{0,8},{1,9},{2,10},{3,11},{4,12},{5,13},{6,14},{7,15},{8,0},{9,1},... | collective-permute-start | bytes 516104 | tf_op jit(solution)/shard_map/ppermute | solution.py:708
  39.7 7.9 %collective-permute-start.17 = (bf16[256,256]{1,0:T(8,128)(2,1)S(1)}, bf16[256,256]{1,0:T(8,128)(2,1)S(1)}, u32[]{:S(2)}, u32[]{:S(2)}) collective-permute-start(bf16[256,256]{1,0:T(8,128)(2,1)S(1)} %up.8.after_ref.current_ref), channel_id=1, source_target_pairs={{0,4},{1,5},{2,6},{3,7},{4,0},{5,1},{6,2},{7,3},{8,12},{9,13},{10,... | collective-permute-start | bytes 393224 | tf_op jit(solution)/shard_map/ppermute | solution.py:708
  41.8 15.7 %collective-permute-start.19 = (bf16[256,256]{1,0:T(8,128)(2,1)S(1)}, bf16[256,256]{1,0:T(8,128)(2,1)S(1)}, u32[]{:S(2)}, u32[]{:S(2)}) collective-permute-start(bf16[256,256]{1,0:T(8,128)(2,1)S(1)} %collective-permute-done.16.sibling_ref.refs_3_), channel_id=1, source_target_pairs={{0,1},{1,0},{2,3},{3,2},{4,5},{5,4},{6,7},{7,6},{8,9},{9,8},{10,11... | collective-permute-start | bytes 393224 | tf_op jit(solution)/shard_map/ppermute | solution.py:708
  45.0 6.9 %collective-permute-start.12 = (f32[168,256]{1,0:T(8,128)S(1)}, f32[168,256]{1,0:T(8,128)S(1)}, u32[]{:S(2)}, u32[]{:S(2)}) collective-permute-start(f32[168,256]{1,0:T(8,128)S(1)} %add.19), channel_id=1, source_target_pairs={{0,4},{1,3},{2,6},{3,1},{4,0},{5,7},{6,2},{7,5},{8,12},{9,11},{10,... | collective-permute-start | bytes 516104 | tf_op jit(solution)/shard_map/ppermute | solution.py:708
  47.9 8.5 %collective-permute-start.18 = (bf16[256,256]{1,0:T(8,128)(2,1)S(1)}, bf16[256,256]{1,0:T(8,128)(2,1)S(1)}, u32[]{:S(2)}, u32[]{:S(2)}) collective-permute-start(bf16[256,256]{1,0:T(8,128)(2,1)S(1)} %up.9), channel_id=1, source_target_pairs={{0,8},{1,9},{2,10},{3,11},{4,12},{5,13},{6,14},{7,15},{8,0},{9,1},... | collective-permute-start | bytes 393224 | tf_op jit(solution)/shard_map/ppermute | solution.py:708
  51.4 6.1 %collective-permute-start.20 = (bf16[256,256]{1,0:T(8,128)(2,1)S(1)}, bf16[256,256]{1,0:T(8,128)(2,1)S(1)}, u32[]{:S(2)}, u32[]{:S(2)}) collective-permute-start(bf16[256,256]{1,0:T(8,128)(2,1)S(1)} %collective-permute-done.17.sibling_ref.refs_4_), channel_id=1, source_target_pairs={{0,1},{1,0},{2,3},{3,2},{4,5},{5,4},{6,7},{7,6},{8,9},{9,8},{10,11... | collective-permute-start | bytes 393224 | tf_op jit(solution)/shard_map/ppermute | solution.py:708
  51.9 5.5 %collective-permute-start.13 = (f32[168,256]{1,0:T(8,128)S(1)}, f32[168,256]{1,0:T(8,128)S(1)}, u32[]{:S(2)}, u32[]{:S(2)}) collective-permute-start(f32[168,256]{1,0:T(8,128)S(1)} %add.20.after_ref.own_ref), channel_id=1, source_target_pairs={{0,2},{1,5},{2,0},{3,7},{4,6},{5,1},{6,4},{7,3},{8,10},{9,13},{10,... | collective-permute-start | bytes 516104 | tf_op jit(solution)/shard_map/ppermute | solution.py:708
  56.4 1.4 %collective-permute-start.21 = (bf16[256,256]{1,0:T(8,128)(2,1)S(1)}, bf16[256,256]{1,0:T(8,128)(2,1)S(1)}, u32[]{:S(2)}, u32[]{:S(2)}) collective-permute-start(bf16[256,256]{1,0:T(8,128)(2,1)S(1)} %ready.3), channel_id=1, source_target_pairs={{0,1},{1,0},{2,3},{3,2},{4,5},{5,4},{6,7},{7,6},{8,9},{9,8},{10,11... | collective-permute-start | bytes 393224 | tf_op jit(solution)/shard_map/ppermute | solution.py:708
  56.5 4.2 %collective-permute-start.14 = (f32[168,256]{1,0:T(8,128)S(1)}, f32[168,256]{1,0:T(8,128)S(1)}, u32[]{:S(2)}, u32[]{:S(2)}) collective-permute-start(f32[168,256]{1,0:T(8,128)S(1)} %add.20.after_ref.own_ref), channel_id=1, source_target_pairs={{0,1},{1,0},{2,3},{3,2},{4,5},{5,4},{6,7},{7,6},{8,9},{9,8},{10,11... | collective-permute-start | bytes 516104 | tf_op jit(solution)/shard_map/ppermute | solution.py:708
  57.4 3.3 %collective-permute-start.15 = (f32[168,256]{1,0:T(8,128)S(1)}, f32[168,256]{1,0:T(8,128)S(1)}, u32[]{:S(2)}, u32[]{:S(2)}) collective-permute-start(f32[168,256]{1,0:T(8,128)S(1)} %collective-permute-done.13.side_ref), channel_id=1, source_target_pairs={{0,1},{1,0},{2,3},{3,2},{4,5},{5,4},{6,7},{7,6},{8,9},{9,8},{10,11... | collective-permute-start | bytes 516104 | tf_op jit(solution)/shard_map/ppermute | solution.py:708
  81.0 1.4 %collective-permute-start.22 = (f32[144,256]{1,0:T(8,128)S(1)}, f32[144,256]{1,0:T(8,128)S(1)}, u32[]{:S(2)}, u32[]{:S(2)}) collective-permute-start(f32[144,256]{1,0:T(8,128)S(1)} %get-tuple-element.72), channel_id=1, source_target_pairs={{0,1},{1,0},{2,3},{3,2},{4,5},{5,4},{6,7},{7,6},{8,9},{9,8},{10,11... | collective-permute-start | bytes 442376 | tf_op jit(solution)/shard_map/ppermute | solution.py:708
  82.5 4.4 %collective-permute-start.23 = (f32[72,256]{1,0:T(8,128)S(1)}, f32[72,256]{1,0:T(8,128)S(1)}, u32[]{:S(2)}, u32[]{:S(2)}) collective-permute-start(f32[72,256]{1,0:T(8,128)S(1)} %slice.19), channel_id=1, source_target_pairs={{0,2},{1,5},{2,0},{3,7},{4,6},{5,1},{6,4},{7,3},{8,10},{9,13},{10,... | collective-permute-start | bytes 221192 | tf_op jit(solution)/shard_map/ppermute | solution.py:708
  86.9 16.7 %collective-permute-start.24 = (f32[72,256]{1,0:T(8,128)S(1)}, f32[72,256]{1,0:T(8,128)S(1)}, u32[]{:S(2)}, u32[]{:S(2)}) collective-permute-start(f32[72,256]{1,0:T(8,128)S(1)} %slice_add_fusion.left_ref), channel_id=1, source_target_pairs={{0,8},{1,9},{2,10},{3,11},{4,12},{5,13},{6,14},{7,15},{8,0},{9,1},... | collective-permute-start | bytes 221192 | tf_op jit(solution)/shard_map/ppermute | solution.py:708
  89.2 14.7 %copy-start.5 = (f32[1024,256]{1,0:T(8,128)S(1)}, f32[1024,256]{1,0:T(8,128)}, u32[]{:S(2)}) copy-start(f32[1024,256]{1,0:T(8,128)} %solution_ref.1) | copy-start | bytes 3145732
  103.7 4.4 %collective-permute-start.25 = (f32[72,256]{1,0:T(8,128)S(1)}, f32[72,256]{1,0:T(8,128)S(1)}, u32[]{:S(2)}, u32[]{:S(2)}) collective-permute-start(f32[72,256]{1,0:T(8,128)S(1)} %add.25.left_ref), channel_id=1, source_target_pairs={{0,4},{1,3},{2,6},{3,1},{4,0},{5,7},{6,2},{7,5},{8,12},{9,11},{10,... | collective-permute-start | bytes 221192 | tf_op jit(solution)/shard_map/ppermute | solution.py:708
  108.1 4.4 %collective-permute-start.26 = (f32[72,256]{1,0:T(8,128)S(1)}, f32[72,256]{1,0:T(8,128)S(1)}, u32[]{:S(2)}, u32[]{:S(2)}) collective-permute-start(f32[72,256]{1,0:T(8,128)S(1)} %add.26.own_ref), channel_id=1, source_target_pairs={{0,2},{1,5},{2,0},{3,7},{4,6},{5,1},{6,4},{7,3},{8,10},{9,13},{10,... | collective-permute-start | bytes 221192 | tf_op jit(solution)/shard_map/ppermute | solution.py:708
  109.0 3.5 %collective-permute-start.27 = (f32[72,256]{1,0:T(8,128)S(1)}, f32[72,256]{1,0:T(8,128)S(1)}, u32[]{:S(2)}, u32[]{:S(2)}) collective-permute-start(f32[72,256]{1,0:T(8,128)S(1)} %add.26.own_ref), channel_id=1, source_target_pairs={{0,1},{1,0},{2,3},{3,2},{4,5},{5,4},{6,7},{7,6},{8,9},{9,8},{10,11... | collective-permute-start | bytes 221192 | tf_op jit(solution)/shard_map/ppermute | solution.py:708
  112.5 1.3 collective-permute-start.28
  (7 other events, 22.4 us)

commit v7 on v6

--- a/solution.py
+++ b/solution.py
@@ -108,7 +108,7 @@
 
     lax.fori_loop(0, count // strip, step, 0)
 
-def near_kernel(block_ref, direction_ref, near_ref):
+def near_kernel(block_ref, direction_ref, after_ref, near_ref):
     low_direction = direction_ref[...].astype(BF16)
     near_ref[...] = dot(block_ref[...], low_direction) + 2.0 * low_direction.astype(F32)
 
@@ -788,7 +788,9 @@
     )
     current = up(1, current, siblings[1], [block, high])
     siblings.append(swapped(current, 2))
-    (near,) = call(near_kernel, "near", [block, direction], [tall], micros=0.7)
+    (near,) = call(
+        near_kernel, "near", [block, direction, current], [tall], micros=0.7, unused=1
+    )
     double_low = ((2 * size, rank), BF16)
     factors = call(
         factor_kernel,

time: 132 us -> 131 us (level); the launches traced: 131 us -> 132 us
  Pallas kernels: 79.9 us -> 81.5 us
    pallas_call x28, Pallas kernels: 79.9 us -> 81.5 us  [call(): pl.pallas_call(kernel, name=name, in_specs=specs, out_specs=[ANY if apart...]
where the time goes in v7:
time: 131 us; the launch traced here: 132 us
  Pallas kernels  81.5 us (62%)
  starting transfers between devices  26 us (20%)
  waiting for transfers between devices  21.8 us (17%)
    pallas_call x28, Pallas kernels, call(): pl.pallas_call(kernel, name=name, in_specs=specs, out_specs=[ANY if apart...  81.5 us
    ppermute x29, starting transfers between devices, swapped(): return lax.ppermute(value, 'leaf', pairs)  26 us
    ppermute x29, waiting for transfers between devices, swapped(): return lax.ppermute(value, 'leaf', pairs)  21.8 us
  transfers between devices with their start and end apart: 29, of which 20 were waited for; matrix products, arithmetic and copies ran while one was open for 0% of the time, Pallas kernels for 28%

profile of v7, /device:TPU:0, one launch (start us, length us, event | category | flops | bytes accessed | tf_op | source)
XLA Modules:
  0.0 131.6 jit_solution(3362807260782367347)
XLA Ops:
  0.6 2.8 %coef.1.value_ref = bf16[256,256]{1,0:T(8,128)(2,1)} custom-call(f32[1024,256]{1,0:T(8,128)} %direction_ref.7, bf16[1024,256]{1,0:T(8,128)(2,1)} %basis_ref.11, s32[1,256]{1,0:T(1,128)} %skel_ref.11), custom_call_target="tpu_custom_call" | custom-call | flops 2969999872 | tf_op jit(solution)/shard_map/coef/pallas_call | solution.py:691
  5.4 2.9 %collective-permute-start.1 = (bf16[256,128]{1,0:T(8,128)(2,1)S(1)}, bf16[256,128]{1,0:T(8,128)(2,1)S(1)}, u32[]{:S(2)}, u32[]{:S(2)}) collective-permute-start(bf16[256,128]{1,0:T(8,128)(2,1)S(1)} %up.5.after_ref.current_ref), channel_id=1, source_target_pairs={{0,2},{1,3},{2,0},{3,1},{4,6},{5,7},{6,4},{7,5},{8,10},{9,11},{10,... | collective-permute-start | bytes 196616 | tf_op jit(solution)/shard_map/ppermute | solution.py:708
  8.3 3.6 %block.1.rest_0_.block_ref = bf16[1024,1024]{1,0:T(8,128)(2,1)S(1)} custom-call(f32[3,1024]{1,0:T(4,128)S(1)} %copy-done.8, s32[1,1024]{1,0:T(1,128)S(1)} %bitcast.2, bf16[256,128]{1,0:T(8,128)(2,1)S(1)} %up.5.after_ref.current_ref), custom_call_target="tpu_custom_call" | custom-call | flops 3960000000 | tf_op jit(solution)/shard_map/block/pallas_call | solution.py:691
  13.0 1.6 %collective-permute-start.2 = (bf16[256,128]{1,0:T(8,128)(2,1)S(1)}, bf16[256,128]{1,0:T(8,128)(2,1)S(1)}, u32[]{:S(2)}, u32[]{:S(2)}) collective-permute-start(bf16[256,128]{1,0:T(8,128)(2,1)S(1)} %up.6.after_ref.current_ref), channel_id=1, source_target_pairs={{0,4},{1,5},{2,6},{3,7},{4,0},{5,1},{6,2},{7,3},{8,12},{9,13},{10,... | collective-permute-start | bytes 196616 | tf_op jit(solution)/shard_map/ppermute | solution.py:708
  14.7 1.6 %factor.1 = (bf16[512,256]{1,0:T(8,128)(2,1)S(1)}, bf16[512,256]{1,0:T(8,128)(2,1)S(1)}, bf16[512,256]{1,0:T(8,128)(2,1)S(1)}, bf16[256,256]{1,0:T(8,128)(2,1)S(...) custom-call(bf16[512,1024]{1,0:T(8,128)(2,1)S(1)} %get-tuple-element.45.rest_1_.high_re, ...), custom_call_target="tpu_custom_call" | custom-call | flops 1980000000 | tf_op jit(solution)/shard_map/factor/pallas_call | solution.py:691
  17.6 2.7 %collective-permute-start.3 = (bf16[256,128]{1,0:T(8,128)(2,1)S(1)}, bf16[256,128]{1,0:T(8,128)(2,1)S(1)}, u32[]{:S(2)}, u32[]{:S(2)}) collective-permute-start(bf16[256,128]{1,0:T(8,128)(2,1)S(1)} %up.7), channel_id=1, source_target_pairs={{0,8},{1,9},{2,10},{3,11},{4,12},{5,13},{6,14},{7,15},{8,0},{9,1},... | collective-permute-start | bytes 196616 | tf_op jit(solution)/shard_map/ppermute | solution.py:708
  20.3 1.8 %near_factor.1 = (f32[512,256]{1,0:T(8,128)S(1)}, f32[256,256]{1,0:T(8,128)S(1)}, f32[256,256]{1,0:T(8,128)S(1)}, f32[256,256]{1,0:T(8,128)S(1)}) custom-call(f32[1024,256]{1,0:T(8,128)S(1)} %near.1.rest_0_.near_ref, bf16[512,1024]{1,0:T(8,128)(2,1)S(1)} %get-tuple-element.45.rest_1_.high_ref, bf16[512,1024]{1,0:T(8,128)(2,1)S(1)} %get-tuple-element.46.low_ref, ...), custom_call_target="tpu_custom_call" | custom-call | flops 1980000000 | tf_op jit(solution)/shard_map/near_factor/pallas_call | solution.py:691
  24.1 2.1 %down.1 = (bf16[2,256,256]{2,1,0:T(8,128)(2,1)S(1)}, bf16[256,256]{1,0:T(8,128)(2,1)S(1)}, bf16[2,256,256]{2,1,0:T(8,128)(2,1)S(1)}, f32[336,256]{1,0:T(8,128)S(...) custom-call(s32[1]{0:T(128)} %bitcast.position_ref.refs_0_, ...), custom_call_target="tpu_custom_call" | custom-call | flops 2200000000 | tf_op jit(solution)/shard_map/down/pallas_call | solution.py:691
  26.5 1.5 %collective-permute-done.7 = f32[336,256]{1,0:T(8,128)S(1)} collective-permute-done((f32[336,256]{1,0:T(8,128)S(1)}, f32[336,256]{1,0:T(8,128)S(1)}, u32[]{:S(2)}, u32[]{:S(2)}) %collective-permute-start.7) | collective-permute-done | bytes 344096 | tf_op jit(solution)/shard_map/ppermute | solution.py:708
  28.6 1.0 collective-permute-start.10
  32.2 1.3 collective-permute-done.8.right_ref
  33.6 2.7 %collective-permute-start.11 = (f32[168,256]{1,0:T(8,128)S(1)}, f32[168,256]{1,0:T(8,128)S(1)}, u32[]{:S(2)}, u32[]{:S(2)}) collective-permute-start(f32[168,256]{1,0:T(8,128)S(1)} %add.24), channel_id=1, source_target_pairs={{0,8},{1,9},{2,10},{3,11},{4,12},{5,13},{6,14},{7,15},{8,0},{9,1},... | collective-permute-start | bytes 516104 | tf_op jit(solution)/shard_map/ppermute | solution.py:708
  36.3 2.4 %pair_near.1.rest_0_.near_ref = f32[2,1024,256]{2,1,0:T(8,128)S(1)} custom-call(bf16[1024,1024]{1,0:T(8,128)(2,1)S(1)} %block.1.rest_0_.block_ref, f32[1024,256]{1,0:T(8,128)S(1)} %image.1.image_ref, f32[1024,256]{1,0:T(8,128)S(1)} %copy-done.4), custom_call_target="tpu_custom_call" | custom-call | flops 2640000000 | tf_op jit(solution)/shard_map/pair_near/pallas_call | solution.py:691
  39.0 2.2 %collective-permute-start.17 = (bf16[256,256]{1,0:T(8,128)(2,1)S(1)}, bf16[256,256]{1,0:T(8,128)(2,1)S(1)}, u32[]{:S(2)}, u32[]{:S(2)}) collective-permute-start(bf16[256,256]{1,0:T(8,128)(2,1)S(1)} %up.8.after_ref.current_ref), channel_id=1, source_target_pairs={{0,4},{1,5},{2,6},{3,7},{4,0},{5,1},{6,2},{7,3},{8,12},{9,13},{10,... | collective-permute-start | bytes 393224 | tf_op jit(solution)/shard_map/ppermute | solution.py:708
  41.1 3.1 %collective-permute-done.11 = f32[168,256]{1,0:T(8,128)S(1)} collective-permute-done((f32[168,256]{1,0:T(8,128)S(1)}, f32[168,256]{1,0:T(8,128)S(1)}, u32[]{:S(2)}, u32[]{:S(2)}) %collective-permute-start.11) | collective-permute-done | bytes 172064 | tf_op jit(solution)/shard_map/ppermute | solution.py:708
  45.0 1.8 %pair_cross.1.rest_0_.refs_11_ = f32[512,512]{1,0:T(8,128)S(1)} custom-call(f32[2,1024,256]{2,1,0:T(8,128)S(1)} %pair_near.1.rest_0_.near_ref, f32[1024,256]{1,0:T(8,128)S(1)} %image.1.image_ref, bf16[512,1024]{1,0:T(8,128)(2,1)S(1)} %get-tuple-element.45.rest_1_.high_ref, bf16[512,1024]{1,0:T(8,128)(2,1)S(1)} %get-tuple-element.46.low_ref, ...), custom_call_target="tpu_custom_call" | custom-call | flops 2529999872 | tf_op jit(solution)/shard_map/pair_cross/pallas_call | solution.py:691
  47.2 3.5 %collective-permute-start.18 = (bf16[256,256]{1,0:T(8,128)(2,1)S(1)}, bf16[256,256]{1,0:T(8,128)(2,1)S(1)}, u32[]{:S(2)}, u32[]{:S(2)}) collective-permute-start(bf16[256,256]{1,0:T(8,128)(2,1)S(1)} %up.9), channel_id=1, source_target_pairs={{0,8},{1,9},{2,10},{3,11},{4,12},{5,13},{6,14},{7,15},{8,0},{9,1},... | collective-permute-start | bytes 393224 | tf_op jit(solution)/shard_map/ppermute | solution.py:708
  51.5 2.4 %pair_square.1 = (f32[512,512]{1,0:T(8,128)S(1)}, f32[256,512]{1,0:T(8,128)S(1)}) custom-call(f32[2,1024,256]{2,1,0:T(8,128)S(1)} %pair_near.1.rest_0_.near_ref, bf16[1024,256]{1,0:T(8,128)(2,1)S(1)} %copy-done.2, s32[1,256]{1,0:T(1,128)S(1)} %copy-done.3, f32[168,256]{1,0:T(8,128)S(1)} %add.20.after_ref.own_ref), custom_call_target="tpu_custom_call" | custom-call | flops 3080000000 | tf_op jit(solution)/shard_map/pair_square/pallas_call | solution.py:691
  53.9 1.8 %collective-permute-done.18.value_ref.refs_5_ = bf16[256,256]{1,0:T(8,128)(2,1)S(1)} collective-permute-done((bf16[256,256]{1,0:T(8,128)(2,1)S(1)}, bf16[256,256]{1,0:T(8,128)(2,1)S(1)}, u32[]{:S(2)}, u32[]{:S(2)}) %collective-permute-start.18) | collective-permute-done | bytes 131104 | tf_op jit(solution)/shard_map/ppermute | solution.py:708
  57.1 2.9 %pair_down.1 = (bf16[2,256,512]{2,1,0:T(8,128)(2,1)S(1)}, f32[1024,256]{1,0:T(8,128)S(1)}, f32[1024,256]{1,0:T(8,128)S(1)}, f32[1024,256]{1,0:T(8,128)S(1)}) custom-call(s32[1]{0:T(128)} %bitcast.position_ref.refs_0_, bf16[256,256]{1,0:T(8,128)(2,1)S(1)} %collective-permute-done.9.image_other.refs_1_, ...), custom_call_target="tpu_custom_call" | custom-call | flops 2750000128 | tf_op jit(solution)/shard_map/pair_down/pallas_call | solution.py:691
  60.0 21.9 %first.1 = (f32[144,256]{1,0:T(8,128)S(1)}, f32[144,256]{1,0:T(8,128)S(1)}, f32[256,256]{1,0:T(8,128)S(1)}, f32[256,256]{1,0:T(8,128)S(1)}, f32[256,256]{1,0:T(8...) custom-call(s32[1]{0:T(128)} %bitcast.position_ref.refs_0_, ...), custom_call_target="tpu_custom_call" | custom-call | flops 5500000256 | tf_op jit(solution)/shard_map/first/pallas_call | solution.py:691
  82.1 1.2 collective-permute-done.22
  83.4 1.4 %collective-permute-start.23 = (f32[72,256]{1,0:T(8,128)S(1)}, f32[72,256]{1,0:T(8,128)S(1)}, u32[]{:S(2)}, u32[]{:S(2)}) collective-permute-start(f32[72,256]{1,0:T(8,128)S(1)} %slice.19), channel_id=1, source_target_pairs={{0,2},{1,5},{2,0},{3,7},{4,6},{5,1},{6,4},{7,3},{8,10},{9,13},{10,... | collective-permute-start | bytes 221192 | tf_op jit(solution)/shard_map/ppermute | solution.py:708
  84.7 3.1 %collective-permute-done.23 = f32[72,256]{1,0:T(8,128)S(1)} collective-permute-done((f32[72,256]{1,0:T(8,128)S(1)}, f32[72,256]{1,0:T(8,128)S(1)}, u32[]{:S(2)}, u32[]{:S(2)}) %collective-permute-start.23) | collective-permute-done | bytes 73760 | tf_op jit(solution)/shard_map/ppermute | solution.py:708
  87.8 2.3 %collective-permute-start.24 = (f32[72,256]{1,0:T(8,128)S(1)}, f32[72,256]{1,0:T(8,128)S(1)}, u32[]{:S(2)}, u32[]{:S(2)}) collective-permute-start(f32[72,256]{1,0:T(8,128)S(1)} %slice_add_fusion.left_ref), channel_id=1, source_target_pairs={{0,8},{1,9},{2,10},{3,11},{4,12},{5,13},{6,14},{7,15},{8,0},{9,1},... | collective-permute-start | bytes 221192 | tf_op jit(solution)/shard_map/ppermute | solution.py:708
  90.1 14.4 %carry.1 = (f32[256,256]{1,0:T(8,128)S(1)}, f32[256,256]{1,0:T(8,128)S(1)}, f32[256,256]{1,0:T(8,128)S(1)}) custom-call(f32[256,256]{1,0:T(8,128)S(1)} %get-tuple-element.73.alpha_ref, f32[256,256]{1,0:T(8,128)S(1)} %get-tuple-element.74.beta_ref, f32[256,256]{1,0:T(8,128)S(1)} %get-tuple-element.75.fresh_ref, f32[256,256]{1,0:T(8,128)S(1)} %get-tuple-element.76.mixed_ref, ...), custom_call_target="tpu_custom_call" | custom-call | flops 3300000000 | tf_op jit(solution)/shard_map/carry/pallas_call | solution.py:691
  104.8 3.0 %update.1 = (f32[1024,256]{1,0:T(8,128)S(1)}, f32[1024,256]{1,0:T(8,128)S(1)}, f32[1024,256]{1,0:T(8,128)S(1)}, f32[1024,256]{1,0:T(8,128)S(1)}) custom-call(f32[1024,256]{1,0:T(8,128)S(1)} %copy-done.4, f32[1024,256]{1,0:T(8,128)S(1)} %copy-done.1, f32[1024,256]{1,0:T(8,128)S(1)} %copy-done.5, f32[1024,256]{1,0:T(8,128)S(1)} %image.1.image_ref, ...), custom_call_target="tpu_custom_call" | custom-call | flops 3520000000 | tf_op jit(solution)/shard_map/update/pallas_call | solution.py:691
  107.9 1.1 collective-permute-done.25.right_ref
  109.0 0.9 collective-permute-start.26
  109.9 3.5 %collective-permute-done.26.side_ref = f32[72,256]{1,0:T(8,128)S(1)} collective-permute-done((f32[72,256]{1,0:T(8,128)S(1)}, f32[72,256]{1,0:T(8,128)S(1)}, u32[]{:S(2)}, u32[]{:S(2)}) %collective-permute-start.26) | collective-permute-done | bytes 73760 | tf_op jit(solution)/shard_map/ppermute | solution.py:708
  113.4 1.3 collective-permute-done.28.far_ref
  114.7 16.7 %last.1 = (f32[1024,256]{1,0:T(8,128)}, f32[1024,256]{1,0:T(8,128)}, f32[1024,256]{1,0:T(8,128)}) custom-call(s32[1]{0:T(128)} %bitcast.position_ref.refs_0_, f32[72,256]{1,0:T(8,128)S(1)} %add.26.own_ref, f32[72,256]{1,0:T(8,128)S(1)} %collective-permute-done.26.side_ref, f32[72,256]{1,0:T(8,128)S(1)} %collective-permute-done.27.core_ref, ...), custom_call_target="tpu_custom_call" | custom-call | flops 7699999744 | tf_op jit(solution)/shard_map/last/pallas_call | solution.py:691
  (81 shorter events, 13.8 us)
Async XLA Ops:
  0.6 7.7 %copy-start.8 = (f32[3,1024]{1,0:T(4,128)S(1)}, f32[3,1024]{1,0:T(4,128)}, u32[]{:S(2)}) copy-start(f32[3,1024]{1,0:T(4,128)} %points_ref.1) | copy-start | bytes 36868
  3.4 1.6 %collective-permute-start = (bf16[256,256]{1,0:T(8,128)(2,1)}, bf16[256,256]{1,0:T(8,128)(2,1)S(1)}, u32[]{:S(2)}, u32[]{:S(2)}) collective-permute-start(bf16[256,256]{1,0:T(8,128)(2,1)} %coef.1.value_ref), channel_id=1, source_target_pairs={{0,1},{1,0},{2,3},{3,2},{4,5},{5,4},{6,7},{7,6},{8,9},{9,8},{10,11... | collective-permute-start | bytes 393224 | tf_op jit(solution)/shard_map/ppermute | solution.py:708
  5.4 7.3 %collective-permute-start.1 = (bf16[256,128]{1,0:T(8,128)(2,1)S(1)}, bf16[256,128]{1,0:T(8,128)(2,1)S(1)}, u32[]{:S(2)}, u32[]{:S(2)}) collective-permute-start(bf16[256,128]{1,0:T(8,128)(2,1)S(1)} %up.5.after_ref.current_ref), channel_id=1, source_target_pairs={{0,2},{1,3},{2,0},{3,1},{4,6},{5,7},{6,4},{7,5},{8,10},{9,11},{10,... | collective-permute-start | bytes 196616 | tf_op jit(solution)/shard_map/ppermute | solution.py:708
  13.0 4.3 %collective-permute-start.2 = (bf16[256,128]{1,0:T(8,128)(2,1)S(1)}, bf16[256,128]{1,0:T(8,128)(2,1)S(1)}, u32[]{:S(2)}, u32[]{:S(2)}) collective-permute-start(bf16[256,128]{1,0:T(8,128)(2,1)S(1)} %up.6.after_ref.current_ref), channel_id=1, source_target_pairs={{0,4},{1,5},{2,6},{3,7},{4,0},{5,1},{6,2},{7,3},{8,12},{9,13},{10,... | collective-permute-start | bytes 196616 | tf_op jit(solution)/shard_map/ppermute | solution.py:708
  17.6 6.5 %copy-start.6 = (bf16[1,4,256,256]{3,2,1,0:T(8,128)(2,1)S(1)}, bf16[1,4,256,256]{3,2,1,0:T(8,128)(2,1)}, u32[]{:S(2)}) copy-start(bf16[1,4,256,256]{3,2,1,0:T(8,128)(2,1)} %refs_9_.3) | copy-start | bytes 1572868
  17.6 5.2 %collective-permute-start.3 = (bf16[256,128]{1,0:T(8,128)(2,1)S(1)}, bf16[256,128]{1,0:T(8,128)(2,1)S(1)}, u32[]{:S(2)}, u32[]{:S(2)}) collective-permute-start(bf16[256,128]{1,0:T(8,128)(2,1)S(1)} %up.7), channel_id=1, source_target_pairs={{0,8},{1,9},{2,10},{3,11},{4,12},{5,13},{6,14},{7,15},{8,0},{9,1},... | collective-permute-start | bytes 196616 | tf_op jit(solution)/shard_map/ppermute | solution.py:708
  22.1 1.3 %collective-permute-start.4 = (bf16[256,128]{1,0:T(8,128)(2,1)S(1)}, bf16[256,128]{1,0:T(8,128)(2,1)S(1)}, u32[]{:S(2)}, u32[]{:S(2)}) collective-permute-start(bf16[256,128]{1,0:T(8,128)(2,1)S(1)} %collective-permute-done.1.sibling_ref.refs_2_), channel_id=1, source_target_pairs={{0,1},{1,0},{2,3},{3,2},{4,5},{5,4},{6,7},{7,6},{8,9},{9,8},{10,11... | collective-permute-start | bytes 196616 | tf_op jit(solution)/shard_map/ppermute | solution.py:708
  22.2 1.4 %collective-permute-start.5 = (bf16[256,128]{1,0:T(8,128)(2,1)S(1)}, bf16[256,128]{1,0:T(8,128)(2,1)S(1)}, u32[]{:S(2)}, u32[]{:S(2)}) collective-permute-start(bf16[256,128]{1,0:T(8,128)(2,1)S(1)} %collective-permute-done.2.sibling_ref.refs_3_), channel_id=1, source_target_pairs={{0,1},{1,0},{2,3},{3,2},{4,5},{5,4},{6,7},{7,6},{8,9},{9,8},{10,11... | collective-permute-start | bytes 196616 | tf_op jit(solution)/shard_map/ppermute | solution.py:708
  22.9 1.3 collective-permute-start.6
  26.3 1.7 %collective-permute-start.7 = (f32[336,256]{1,0:T(8,128)S(1)}, f32[336,256]{1,0:T(8,128)S(1)}, u32[]{:S(2)}, u32[]{:S(2)}) collective-permute-start(f32[336,256]{1,0:T(8,128)S(1)} %get-tuple-element.60), channel_id=1, source_target_pairs={{0,1},{1,0},{2,3},{3,2},{4,5},{5,4},{6,7},{7,6},{8,9},{9,8},{10,11... | collective-permute-start | bytes 1032200 | tf_op jit(solution)/shard_map/ppermute | solution.py:708
  28.1 5.5 %collective-permute-start.8 = (f32[168,256]{1,0:T(8,128)S(1)}, f32[168,256]{1,0:T(8,128)S(1)}, u32[]{:S(2)}, u32[]{:S(2)}) collective-permute-start(f32[168,256]{1,0:T(8,128)S(1)} %get-tuple-element.87), channel_id=1, source_target_pairs={{0,2},{1,5},{2,0},{3,7},{4,6},{5,1},{6,4},{7,3},{8,10},{9,13},{10,... | collective-permute-start | bytes 516104 | tf_op jit(solution)/shard_map/ppermute | solution.py:708
  28.6 2.0 %collective-permute-start.10 = (bf16[256,256]{1,0:T(8,128)(2,1)S(1)}, bf16[256,256]{1,0:T(8,128)(2,1)S(1)}, u32[]{:S(2)}, u32[]{:S(2)}) collective-permute-start(bf16[256,256]{1,0:T(8,128)(2,1)S(1)} %get-tuple-element.47.rest_1_.residual_ref), channel_id=1, source_target_pairs={{0,1},{1,0},{2,3},{3,2},{4,5},{5,4},{6,7},{7,6},{8,9},{9,8},{10,11... | collective-permute-start | bytes 393224 | tf_op jit(solution)/shard_map/ppermute | solution.py:708
  29.6 1.3 %collective-permute-start.9 = (bf16[256,256]{1,0:T(8,128)(2,1)S(1)}, bf16[256,256]{1,0:T(8,128)(2,1)S(1)}, u32[]{:S(2)}, u32[]{:S(2)}) collective-permute-start(bf16[256,256]{1,0:T(8,128)(2,1)S(1)} %get-tuple-element.61.image_ref), channel_id=1, source_target_pairs={{0,1},{1,0},{2,3},{3,2},{4,5},{5,4},{6,7},{7,6},{8,9},{9,8},{10,11... | collective-permute-start | bytes 393224 | tf_op jit(solution)/shard_map/ppermute | solution.py:708
  31.4 7.3 %collective-permute-start.16 = (bf16[256,256]{1,0:T(8,128)(2,1)S(1)}, bf16[256,256]{1,0:T(8,128)(2,1)S(1)}, u32[]{:S(2)}, u32[]{:S(2)}) collective-permute-start(bf16[256,256]{1,0:T(8,128)(2,1)S(1)} %pair_up.1.rest_0_.current_ref), channel_id=1, source_target_pairs={{0,2},{1,3},{2,0},{3,1},{4,6},{5,7},{6,4},{7,5},{8,10},{9,11},{10,... | collective-permute-start | bytes 393224 | tf_op jit(solution)/shard_map/ppermute | solution.py:708
  33.6 10.7 %collective-permute-start.11 = (f32[168,256]{1,0:T(8,128)S(1)}, f32[168,256]{1,0:T(8,128)S(1)}, u32[]{:S(2)}, u32[]{:S(2)}) collective-permute-start(f32[168,256]{1,0:T(8,128)S(1)} %add.24), channel_id=1, source_target_pairs={{0,8},{1,9},{2,10},{3,11},{4,12},{5,13},{6,14},{7,15},{8,0},{9,1},... | collective-permute-start | bytes 516104 | tf_op jit(solution)/shard_map/ppermute | solution.py:708
  39.0 7.9 %collective-permute-start.17 = (bf16[256,256]{1,0:T(8,128)(2,1)S(1)}, bf16[256,256]{1,0:T(8,128)(2,1)S(1)}, u32[]{:S(2)}, u32[]{:S(2)}) collective-permute-start(bf16[256,256]{1,0:T(8,128)(2,1)S(1)} %up.8.after_ref.current_ref), channel_id=1, source_target_pairs={{0,4},{1,5},{2,6},{3,7},{4,0},{5,1},{6,2},{7,3},{8,12},{9,13},{10,... | collective-permute-start | bytes 393224 | tf_op jit(solution)/shard_map/ppermute | solution.py:708
  41.1 15.7 %collective-permute-start.19 = (bf16[256,256]{1,0:T(8,128)(2,1)S(1)}, bf16[256,256]{1,0:T(8,128)(2,1)S(1)}, u32[]{:S(2)}, u32[]{:S(2)}) collective-permute-start(bf16[256,256]{1,0:T(8,128)(2,1)S(1)} %collective-permute-done.16.sibling_ref.refs_3_), channel_id=1, source_target_pairs={{0,1},{1,0},{2,3},{3,2},{4,5},{5,4},{6,7},{7,6},{8,9},{9,8},{10,11... | collective-permute-start | bytes 393224 | tf_op jit(solution)/shard_map/ppermute | solution.py:708
  44.3 6.9 %collective-permute-start.12 = (f32[168,256]{1,0:T(8,128)S(1)}, f32[168,256]{1,0:T(8,128)S(1)}, u32[]{:S(2)}, u32[]{:S(2)}) collective-permute-start(f32[168,256]{1,0:T(8,128)S(1)} %add.19), channel_id=1, source_target_pairs={{0,4},{1,3},{2,6},{3,1},{4,0},{5,7},{6,2},{7,5},{8,12},{9,11},{10,... | collective-permute-start | bytes 516104 | tf_op jit(solution)/shard_map/ppermute | solution.py:708
  47.2 8.5 %collective-permute-start.18 = (bf16[256,256]{1,0:T(8,128)(2,1)S(1)}, bf16[256,256]{1,0:T(8,128)(2,1)S(1)}, u32[]{:S(2)}, u32[]{:S(2)}) collective-permute-start(bf16[256,256]{1,0:T(8,128)(2,1)S(1)} %up.9), channel_id=1, source_target_pairs={{0,8},{1,9},{2,10},{3,11},{4,12},{5,13},{6,14},{7,15},{8,0},{9,1},... | collective-permute-start | bytes 393224 | tf_op jit(solution)/shard_map/ppermute | solution.py:708
  50.7 6.1 %collective-permute-start.20 = (bf16[256,256]{1,0:T(8,128)(2,1)S(1)}, bf16[256,256]{1,0:T(8,128)(2,1)S(1)}, u32[]{:S(2)}, u32[]{:S(2)}) collective-permute-start(bf16[256,256]{1,0:T(8,128)(2,1)S(1)} %collective-permute-done.17.sibling_ref.refs_4_), channel_id=1, source_target_pairs={{0,1},{1,0},{2,3},{3,2},{4,5},{5,4},{6,7},{7,6},{8,9},{9,8},{10,11... | collective-permute-start | bytes 393224 | tf_op jit(solution)/shard_map/ppermute | solution.py:708
  51.2 5.5 %collective-permute-start.13 = (f32[168,256]{1,0:T(8,128)S(1)}, f32[168,256]{1,0:T(8,128)S(1)}, u32[]{:S(2)}, u32[]{:S(2)}) collective-permute-start(f32[168,256]{1,0:T(8,128)S(1)} %add.20.after_ref.own_ref), channel_id=1, source_target_pairs={{0,2},{1,5},{2,0},{3,7},{4,6},{5,1},{6,4},{7,3},{8,10},{9,13},{10,... | collective-permute-start | bytes 516104 | tf_op jit(solution)/shard_map/ppermute | solution.py:708
  55.7 1.4 %collective-permute-start.21 = (bf16[256,256]{1,0:T(8,128)(2,1)S(1)}, bf16[256,256]{1,0:T(8,128)(2,1)S(1)}, u32[]{:S(2)}, u32[]{:S(2)}) collective-permute-start(bf16[256,256]{1,0:T(8,128)(2,1)S(1)} %ready.3), channel_id=1, source_target_pairs={{0,1},{1,0},{2,3},{3,2},{4,5},{5,4},{6,7},{7,6},{8,9},{9,8},{10,11... | collective-permute-start | bytes 393224 | tf_op jit(solution)/shard_map/ppermute | solution.py:708
  55.8 4.2 %collective-permute-start.14 = (f32[168,256]{1,0:T(8,128)S(1)}, f32[168,256]{1,0:T(8,128)S(1)}, u32[]{:S(2)}, u32[]{:S(2)}) collective-permute-start(f32[168,256]{1,0:T(8,128)S(1)} %add.20.after_ref.own_ref), channel_id=1, source_target_pairs={{0,1},{1,0},{2,3},{3,2},{4,5},{5,4},{6,7},{7,6},{8,9},{9,8},{10,11... | collective-permute-start | bytes 516104 | tf_op jit(solution)/shard_map/ppermute | solution.py:708
  56.7 3.3 %collective-permute-start.15 = (f32[168,256]{1,0:T(8,128)S(1)}, f32[168,256]{1,0:T(8,128)S(1)}, u32[]{:S(2)}, u32[]{:S(2)}) collective-permute-start(f32[168,256]{1,0:T(8,128)S(1)} %collective-permute-done.13.side_ref), channel_id=1, source_target_pairs={{0,1},{1,0},{2,3},{3,2},{4,5},{5,4},{6,7},{7,6},{8,9},{9,8},{10,11... | collective-permute-start | bytes 516104 | tf_op jit(solution)/shard_map/ppermute | solution.py:708
  81.9 1.4 %collective-permute-start.22 = (f32[144,256]{1,0:T(8,128)S(1)}, f32[144,256]{1,0:T(8,128)S(1)}, u32[]{:S(2)}, u32[]{:S(2)}) collective-permute-start(f32[144,256]{1,0:T(8,128)S(1)} %get-tuple-element.72), channel_id=1, source_target_pairs={{0,1},{1,0},{2,3},{3,2},{4,5},{5,4},{6,7},{7,6},{8,9},{9,8},{10,11... | collective-permute-start | bytes 442376 | tf_op jit(solution)/shard_map/ppermute | solution.py:708
  83.4 4.4 %collective-permute-start.23 = (f32[72,256]{1,0:T(8,128)S(1)}, f32[72,256]{1,0:T(8,128)S(1)}, u32[]{:S(2)}, u32[]{:S(2)}) collective-permute-start(f32[72,256]{1,0:T(8,128)S(1)} %slice.19), channel_id=1, source_target_pairs={{0,2},{1,5},{2,0},{3,7},{4,6},{5,1},{6,4},{7,3},{8,10},{9,13},{10,... | collective-permute-start | bytes 221192 | tf_op jit(solution)/shard_map/ppermute | solution.py:708
  87.8 16.7 %collective-permute-start.24 = (f32[72,256]{1,0:T(8,128)S(1)}, f32[72,256]{1,0:T(8,128)S(1)}, u32[]{:S(2)}, u32[]{:S(2)}) collective-permute-start(f32[72,256]{1,0:T(8,128)S(1)} %slice_add_fusion.left_ref), channel_id=1, source_target_pairs={{0,8},{1,9},{2,10},{3,11},{4,12},{5,13},{6,14},{7,15},{8,0},{9,1},... | collective-permute-start | bytes 221192 | tf_op jit(solution)/shard_map/ppermute | solution.py:708
  90.1 14.7 %copy-start.5 = (f32[1024,256]{1,0:T(8,128)S(1)}, f32[1024,256]{1,0:T(8,128)}, u32[]{:S(2)}) copy-start(f32[1024,256]{1,0:T(8,128)} %solution_ref.1) | copy-start | bytes 3145732
  104.6 4.4 %collective-permute-start.25 = (f32[72,256]{1,0:T(8,128)S(1)}, f32[72,256]{1,0:T(8,128)S(1)}, u32[]{:S(2)}, u32[]{:S(2)}) collective-permute-start(f32[72,256]{1,0:T(8,128)S(1)} %add.25.left_ref), channel_id=1, source_target_pairs={{0,4},{1,3},{2,6},{3,1},{4,0},{5,7},{6,2},{7,5},{8,12},{9,11},{10,... | collective-permute-start | bytes 221192 | tf_op jit(solution)/shard_map/ppermute | solution.py:708
  109.0 4.4 %collective-permute-start.26 = (f32[72,256]{1,0:T(8,128)S(1)}, f32[72,256]{1,0:T(8,128)S(1)}, u32[]{:S(2)}, u32[]{:S(2)}) collective-permute-start(f32[72,256]{1,0:T(8,128)S(1)} %add.26.own_ref), channel_id=1, source_target_pairs={{0,2},{1,5},{2,0},{3,7},{4,6},{5,1},{6,4},{7,3},{8,10},{9,13},{10,... | collective-permute-start | bytes 221192 | tf_op jit(solution)/shard_map/ppermute | solution.py:708
  109.9 3.5 %collective-permute-start.27 = (f32[72,256]{1,0:T(8,128)S(1)}, f32[72,256]{1,0:T(8,128)S(1)}, u32[]{:S(2)}, u32[]{:S(2)}) collective-permute-start(f32[72,256]{1,0:T(8,128)S(1)} %add.26.own_ref), channel_id=1, source_target_pairs={{0,1},{1,0},{2,3},{3,2},{4,5},{5,4},{6,7},{7,6},{8,9},{9,8},{10,11... | collective-permute-start | bytes 221192 | tf_op jit(solution)/shard_map/ppermute | solution.py:708
  113.4 1.3 collective-permute-start.28
  (7 other events, 21.3 us)
